TPU v7x, 1024 devices: a whole 8x8x8 slice. The times are simulated.
1024 devices in a mesh: dp: 64 (over y, z_lo, core), tensor: 16 (over x, z_hi).
Axes of the slice: x: 8, y: 8, z: 8 (z_hi: 2, z_lo: 4; z = z_hi * 4 + z_lo), core: 2. Of those that a mesh axis runs over, the one named last changes fastest.
Arguments:
- inputs: bfloat16 [24576, 6144], P('dp'), may hold values from -6 to 6
- ln_gain: float32 [6144], replicated, may hold values from 0.1 to 1.9
- w_query: bfloat16 [6144, 4096], P(None, 'tensor'), may hold values from -0.078125 to 0.078125
- query_grad: bfloat16 [24576, 4096], P('dp', 'tensor'), may hold values from -6 to 6
- skip_grad: bfloat16 [24576, 6144], P(('dp', 'tensor')), may hold values from -6 to 6
Outputs:
- input_grad: bfloat16 [24576, 6144], P(('dp', 'tensor'))
- weight_grad: float32 [6144, 4096], P('dp', 'tensor')
All inputs are finite; a program needn't handle non-finite values.
Results may differ from a plain program's by a relative error of at most 0.015.
Values may be sent and summed in bfloat16 or wider, within the bound.
No kernel may reach another device: no remote copies, remote signals or barrier semaphores. Data moves between devices by JAX's collectives and lax.ppermute only.
A program may use at most 128 MiB of HBM per device.

v0:
```python
import jax
import jax.numpy as jnp
from jax import lax
from jax.sharding import PartitionSpec as P


def weight_reduce(scaled, query_grad):
    replicas = lax.axis_size("dp")
    summed = lax.psum_scatter(
        lax.dot_general(
            scaled, query_grad, (((0,), (0,)), ((), ())), preferred_element_type=jnp.float32
        ),
        "dp",
        scatter_dimension=0,
        tiled=True,
    )
    return summed / replicas


def feature_reduce(query_grad, w_query):
    return lax.psum_scatter(
        lax.dot_general(
            query_grad, w_query, (((1,), (1,)), ((), ())), preferred_element_type=jnp.float32
        ).astype(jnp.bfloat16),
        "tensor",
        scatter_dimension=0,
        tiled=True,
    ).astype(jnp.float32)


def per_device(inputs, ln_gain, w_query, query_grad, skip_grad):
    values = inputs.astype(jnp.float32)
    center = values - jnp.mean(values, axis=1, keepdims=True)
    inverse = lax.rsqrt(jnp.mean(center * center, axis=1, keepdims=True) + 1e-06)
    normed = center * inverse
    scaled = (normed * ln_gain[None, :]).astype(jnp.bfloat16)
    own_rows = skip_grad.shape[0]
    d_scaled = feature_reduce(query_grad, w_query)
    weight_grad = weight_reduce(scaled, query_grad)
    first = lax.axis_index("tensor") * own_rows
    normed_own = lax.dynamic_slice_in_dim(normed, first, own_rows, 0)
    inverse_own = lax.dynamic_slice_in_dim(inverse, first, own_rows, 0)
    gated = d_scaled * ln_gain[None, :]
    mean_g = jnp.mean(gated, axis=1, keepdims=True)
    mean_gn = jnp.mean(gated * normed_own, axis=1, keepdims=True)
    input_grad = skip_grad.astype(jnp.float32) + inverse_own * (
        gated - mean_g - normed_own * mean_gn
    )
    return (input_grad.astype(jnp.bfloat16), weight_grad)


def solution(mesh):
    placed = (P("dp", None), P(), P(None, "tensor"), P("dp", "tensor"), P(("dp", "tensor"), None))
    return jax.shard_map(
        per_device,
        mesh=mesh,
        in_specs=placed,
        out_specs=(P(("dp", "tensor"), None), P("dp", "tensor")),
        check_vma=False,
    )
```

profile of v0, /device:TPU:8, one launch (start us, length us, event | category | flops | bytes accessed | tf_op | source)
XLA Modules:
  0.0 578.0 jit_solution(8141621006360739380)
XLA Ops:
  7.2 0.0 copy-start
  7.2 0.0 reduce-scatter.3.cloned.1.call-start
  7.2 1.8 copy-done
  9.1 4.5 convolution_convert_fusion
  13.5 0.0 copy-start.1
  13.5 0.0 copy-start.3
  13.5 0.0 reduce-scatter.3.cloned.1.call-update
  13.6 0.0 reduce-scatter.5.cloned.1.call-start
  13.6 3.1 convert_reduce_fusion
  16.7 3.7 fusion.2
  20.4 0.0 copy-done.1
  20.4 0.0 copy-done.3
  20.4 7.4 %fusion.3 = f32[6144,256]{1,0:T(8,128)} fusion(bf16[384,256]{1,0:T(8,128)(2,1)S(1)} %copy-done.1, f32[6144]{0:T(1024)S(1)} %copy-done.3, bf16[384,6144]{1,0:T(8,128)(2,1)} %param.5, f32[384]{0:T(512)S(1)} %add_rsqrt_fusion, f32[384]{0:T(512)S(1)} %broadcast_multiply_fusion.1), kind=kOutput, calls=%fused_computation.7 | convolution fusion | flops 1219756032 | bytes 11234304 | tf_op jit(solution)/shard_map/dot_general | solution.py:10
  27.9 0.0 copy-start.2
  27.9 0.0 reduce-scatter.5.cloned.1.call-update
  27.9 0.1 dynamic-slice.3
  28.0 7.8 %fusion = f32[384,6144]{1,0:T(8,128)} fusion(bf16[384,6144]{1,0:T(8,128)(2,1)} %param.5, f32[384]{0:T(512)S(1)} %add_rsqrt_fusion, f32[384]{0:T(512)S(1)} %broadcast_multiply_fusion.1), kind=kLoop, calls=%fused_computation.2 | loop fusion | flops 7077888 | bytes 14158848 | tf_op jit(solution)/shard_map/mul | solution.py:35
  35.8 239.5 %reduce-scatter.3.cloned.1.call-done = bf16[24,6144]{1,0:T(8,128)(2,1)} async-done(((bf16[384,6144]{1,0:T(8,128)(2,1)}), bf16[24,6144]{1,0:T(8,128)(2,1)}) %reduce-scatter.3.cloned.1.call-update) | async-done | bytes 294928 | tf_op jit(solution)/shard_map/reduce_scatter | solution.py:21
  275.3 1.4 fusion.5
  276.6 0.0 copy-done.2
  276.6 2.1 add_convert_fusion
  278.7 290.9 %reduce-scatter.5.cloned.1.call-done = f32[96,256]{1,0:T(8,128)} async-done(((f32[6144,256]{1,0:T(8,128)}), f32[96,256]{1,0:T(8,128)}) %reduce-scatter.5.cloned.1.call-update) | async-done | bytes 98320 | tf_op jit(solution)/shard_map/reduce_scatter | solution.py:9
  569.6 1.5 broadcast_multiply_fusion
  (3 shorter events, 0.0 us)
Async XLA Ops:
  7.2 1.9 copy-start
  7.2 268.1 %reduce-scatter.3.cloned.1.call-start = ((), (), s32[]{:S(2)}) async-start(), calls=%async_computation.2 | async-start | bytes 5013504 | tf_op jit(solution)/shard_map/reduce_scatter | solution.py:21
  13.5 6.9 %copy-start.1 = (bf16[384,256]{1,0:T(8,128)(2,1)S(1)}, bf16[384,256]{1,0:T(8,128)(2,1)}, u32[]{:S(2)}) copy-start(bf16[384,256]{1,0:T(8,128)(2,1)} %param.8) | copy-start | bytes 589828
  13.5 6.9 %copy-start.3 = (f32[6144]{0:T(1024)S(1)}, f32[6144]{0:T(1024)}, u32[]{:S(2)}) copy-start(f32[6144]{0:T(1024)} %param.6) | copy-start | bytes 73732
  13.6 556.1 %reduce-scatter.5.cloned.1.call-start = ((), (), s32[]{:S(2)}) async-start(), calls=%async_computation.3 | async-start | bytes 6389760 | tf_op jit(solution)/shard_map/reduce_scatter | solution.py:9
  27.9 248.8 %copy-start.2 = (bf16[24,6144]{1,0:T(8,128)(2,1)S(1)}, bf16[24,6144]{1,0:T(8,128)(2,1)}, u32[]{:S(2)}) copy-start(bf16[24,6144]{1,0:T(8,128)(2,1)} %param.9) | copy-start | bytes 884740
Sparse Core Ops, SparseCore 0:
  13.9 261.3 reduce-scatter.2
  278.7 290.9 reduce-scatter.4
where the time goes:
time: 578 us
  waiting for transfers between devices  530 us (92%)
  other arithmetic  19.6 us (3%)
  between operations  14.1 us (2%)
  matrix products  11.9 us (2%)
    reduce_scatter x1, waiting for transfers between devices, weight_reduce(): lax.psum_scatter(lax.dot_general(scaled, query_grad, (((0,), (0,)), ((),...  291 us
    reduce_scatter x1, waiting for transfers between devices, feature_reduce(): lax.psum_scatter(lax.dot_general(query_grad, w_query, (((1,), (1,)), ((),...  239 us
  transfers between devices with their start and end apart: 2, of which 2 were waited for; matrix products, arithmetic and copies ran while one was open for 4% of the time, Pallas kernels for 0%

commit v1 on v0

v1 whole, which is shorter than its diff:
```python
import jax
import jax.numpy as jnp
from jax import lax
from jax.sharding import Mesh, PartitionSpec as P

DP = ("y", "z_lo", "core")
TENSOR = ("x", "z_hi")
SPLIT = (8, 4, 2, 8, 2)


def shifted(part, axis, step):
    size = lax.axis_size(axis)
    return lax.ppermute(part, axis, [(i, (i + step) % size) for i in range(size)])


def direct_reduce(blocks, axis):
    size = lax.axis_size(axis)
    me = lax.axis_index(axis)
    narrow = blocks.astype(jnp.bfloat16)
    arrived = [
        shifted(lax.dynamic_index_in_dim(narrow, (me + step) % size, 0, False), axis, step)
        for step in range(1, size)
    ]
    total = lax.dynamic_index_in_dim(blocks, me, 0, False)
    for part in arrived:
        total = total + part.astype(jnp.float32)
    return total


def weight_reduce(term):
    columns = term.shape[1]
    replicas = lax.axis_size(DP)
    cores, z_lo, y = lax.axis_size("core"), lax.axis_size("z_lo"), lax.axis_size("y")
    rows = term.shape[0] // replicas
    blocks = term.reshape(y * z_lo, cores, rows, columns).transpose(1, 0, 2, 3)
    total = direct_reduce(blocks, "core")
    total = direct_reduce(total.reshape(y, z_lo * rows, columns), "y")
    total = direct_reduce(total.reshape(z_lo, rows, columns), "z_lo")
    return total / replicas


def feature_reduce(query_grad, w_query):
    term = lax.dot_general(
        query_grad, w_query, (((1,), (1,)), ((), ())), preferred_element_type=jnp.float32
    ).astype(jnp.bfloat16)
    across = lax.psum_scatter(term, "x", scatter_dimension=0, tiled=True)
    halves = across.reshape(2, across.shape[0] // 2, across.shape[1])
    me = lax.axis_index("z_hi")
    own = lax.dynamic_index_in_dim(halves, me, 0, False)
    other = lax.dynamic_index_in_dim(halves, 1 - me, 0, False)
    return own.astype(jnp.float32) + shifted(other, "z_hi", 1).astype(jnp.float32)


def per_device(inputs, ln_gain, w_query, query_grad, skip_grad):
    d_scaled = feature_reduce(query_grad, w_query)
    values = inputs.astype(jnp.float32)
    mean = jnp.mean(values, axis=1, keepdims=True)
    center = values - mean
    inverse = lax.rsqrt(jnp.mean(center * center, axis=1, keepdims=True) + 1e-06)
    scaled = (center * inverse * ln_gain[None, :]).astype(jnp.bfloat16)
    term = lax.dot_general(
        scaled, query_grad, (((0,), (0,)), ((), ())), preferred_element_type=jnp.float32
    )
    weight_grad = weight_reduce(term)

    own_rows = skip_grad.shape[0]
    first = lax.axis_index(TENSOR) * own_rows
    own_values = lax.dynamic_slice_in_dim(inputs, first, own_rows, 0).astype(jnp.float32)
    mean_own = lax.dynamic_slice_in_dim(mean, first, own_rows, 0)
    inverse_own = lax.dynamic_slice_in_dim(inverse, first, own_rows, 0)
    normed_own = (own_values - mean_own) * inverse_own
    gated = d_scaled * ln_gain[None, :]
    mean_g = jnp.mean(gated, axis=1, keepdims=True)
    mean_gn = jnp.mean(gated * normed_own, axis=1, keepdims=True)
    input_grad = skip_grad.astype(jnp.float32) + inverse_own * (
        gated - mean_g - normed_own * mean_gn
    )
    return (input_grad.astype(jnp.bfloat16), weight_grad)


def solution(mesh):
    fine = Mesh(mesh.devices.reshape(SPLIT), DP + TENSOR)
    placed = (P(DP, None), P(), P(None, TENSOR), P(DP, TENSOR), P(DP + TENSOR, None))
    return jax.shard_map(
        per_device,
        mesh=fine,
        in_specs=placed,
        out_specs=(P(DP + TENSOR, None), P(DP, TENSOR)),
        check_vma=False,
    )
```

time: 578 us -> 142 us (0.25)
  the two profiles are of different devices: /device:TPU:8 before, /device:TPU:16 now
where the time goes in v1:
time: 142 us; the launch traced here: 141 us
  starting transfers between devices  59.3 us (42%)
  waiting for transfers between devices  31.8 us (22%)
  other arithmetic  15.2 us (11%)
  between operations  14.4 us (10%)
  local copies, waits for them, and re-layouts  12.9 us (9%)
  matrix products  7.27 us (5%)
    ppermute x12, starting transfers between devices, shifted(): lax.ppermute(part, axis, [(i, (i + step) % size) for i in range(size)])  59.3 us
    ppermute x12, waiting for transfers between devices, shifted(): lax.ppermute(part, axis, [(i, (i + step) % size) for i in range(size)])  31.8 us
    unnamed x16, local copies, waits for them, and re-layouts  7.33 us
    dot_general x1, matrix products, feature_reduce(): lax.dot_general(query_grad, w_query, (((1,), (1,)), ((), ())), preferred_...  4.58 us
    add x2, other arithmetic, direct_reduce(): total = total + part.astype(jnp.float32)  4.49 us
    squeeze x3, local copies, waits for them, and re-layouts, direct_reduce(): lax.dynamic_index_in_dim(narrow, (me + step) % size, 0, False)  3.74 us
    reduce_sum x1, other arithmetic, per_device(): mean = jnp.mean(values, axis=1, keepdims=True)  3.19 us
  transfers between devices with their start and end apart: 13, of which 7 were waited for; matrix products, arithmetic and copies ran while one was open for 13% of the time, Pallas kernels for 0%

profile of v1, /device:TPU:16, one launch (start us, length us, event | category | flops | bytes accessed | tf_op | source)
XLA Modules:
  0.0 140.9 jit_solution(11084197975294613883)
XLA Ops:
  7.2 1.8 %copy-done = bf16[6144,256]{1,0:T(8,128)(2,1)S(1)} copy-done((bf16[6144,256]{1,0:T(8,128)(2,1)S(1)}, bf16[6144,256]{1,0:T(8,128)(2,1)}, u32[]{:S(2)}) %copy-start) | copy-done | bytes 3145752
  9.1 4.6 %convolution_convert_fusion = bf16[384,6144]{1,0:T(8,128)(2,1)} fusion(bf16[384,256]{1,0:T(8,128)(2,1)} %param.8, bf16[6144,256]{1,0:T(8,128)(2,1)S(1)} %copy-done), kind=kOutput, calls=%fused_computation.7 | convolution fusion | flops 1210318848 | bytes 8060928 | tf_op jit(solution)/shard_map/dot_general | solution.py:43
  13.7 3.2 %convert_reduce_fusion = f32[384]{0:T(512)S(1)} fusion(bf16[384,6144]{1,0:T(8,128)(2,1)} %param.5), kind=kLoop, calls=%fused_computation.1 | loop fusion | flops 4718208 | bytes 4720128 | tf_op jit(solution)/shard_map/reduce_sum | solution.py:57
  18.8 2.7 %fusion.5 = f32[6144,256]{1,0:T(8,128)S(1)} fusion(bf16[384,256]{1,0:T(8,128)(2,1)S(1)} %copy-done.4, bf16[384,6144]{1,0:T(8,128)(2,1)S(1)} %copy-done.1, f32[6144]{0:T(1024)S(1)} %copy-done.7, f32[384]{0:T(512)S(1)} %add_rsqrt_fusion, f32[384]{0:T(512)S(1)} %broadcast_multiply_fusion), kind=kOutput, calls=%fused_computation.8 | convolution fusion | flops 1219756032 | bytes 11234304 | tf_op jit(solution)/shard_map/dot_general | solution.py:61
  21.5 2.6 %copy-done.3 = f32[6144,256]{1,0:T(8,128)} copy-done((f32[6144,256]{1,0:T(8,128)}, f32[6144,256]{1,0:T(8,128)S(1)}, u32[]{:S(2)}) %copy-start.3) | copy-done | bytes 6291480
  24.2 1.4 fusion.10
  25.6 1.9 %collective-permute-start.1 = (bf16[32,96,256]{2,1,0:T(8,128)(2,1)}, bf16[32,96,256]{2,1,0:T(8,128)(2,1)}, u32[]{:S(2)}, u32[]{:S(2)}) collective-permute-start(bf16[32,96,256]{2,1,0:T(8,128)(2,1)} %fusion.10), channel_id=1, source_target_pairs={{0,16},{16,0},{1,17},{17,1},{2,18},{18,2},{3,19},{19,3},{4,20},{20... | collective-permute-start | bytes 4718600 | tf_op jit(solution)/shard_map/ppermute | solution.py:13
  27.6 3.6 %collective-permute-done.1 = bf16[32,96,256]{2,1,0:T(8,128)(2,1)} collective-permute-done((bf16[32,96,256]{2,1,0:T(8,128)(2,1)}, bf16[32,96,256]{2,1,0:T(8,128)(2,1)}, u32[]{:S(2)}, u32[]{:S(2)}) %collective-permute-start.1) | collective-permute-done | bytes 1572896 | tf_op jit(solution)/shard_map/ppermute | solution.py:13
  31.2 2.8 %bitcast_add_fusion = f32[32,96,256]{2,1,0:T(8,128)S(1)} fusion(bf16[32,96,256]{2,1,0:T(8,128)(2,1)} %collective-permute-done.1, f32[32,2,96,256]{3,2,1,0:T(8,128)} %bitcast.65, s32[]{:T(128)S(6)} %select_n.110), kind=kLoop, calls=%fused_computation.13 | loop fusion | flops 1572864 | bytes 7864324 | tf_op jit(solution)/shard_map/add | solution.py:26
  34.0 1.6 %copy-done.2 = f32[32,96,256]{2,1,0:T(8,128)} copy-done((f32[32,96,256]{2,1,0:T(8,128)}, f32[32,96,256]{2,1,0:T(8,128)S(1)}, u32[]{:S(2)}) %copy-start.2) | copy-done | bytes 3145752
  36.6 3.6 %collective-permute-start.2 = (bf16[384,256]{1,0:T(8,128)(2,1)S(1)}, bf16[384,256]{1,0:T(8,128)(2,1)S(1)}, u32[]{:S(2)}, u32[]{:S(2)}) collective-permute-start(bf16[384,256]{1,0:T(8,128)(2,1)S(1)} %get-tuple-element.4), channel_id=1, source_target_pairs={{0,128},{128,256},{256,384},{384,512},{512,640},{640,768},{768,896... | collective-permute-start | bytes 589832 | tf_op jit(solution)/shard_map/ppermute | solution.py:13
  40.2 5.9 %collective-permute-start.3 = (bf16[384,256]{1,0:T(8,128)(2,1)S(1)}, bf16[384,256]{1,0:T(8,128)(2,1)S(1)}, u32[]{:S(2)}, u32[]{:S(2)}) collective-permute-start(bf16[384,256]{1,0:T(8,128)(2,1)S(1)} %get-tuple-element.10), channel_id=1, source_target_pairs={{0,256},{128,384},{256,512},{384,640},{512,768},{640,896},{768,0},... | collective-permute-start | bytes 589832 | tf_op jit(solution)/shard_map/ppermute | solution.py:13
  46.2 3.2 %collective-permute-start.4 = (bf16[384,256]{1,0:T(8,128)(2,1)}, bf16[384,256]{1,0:T(8,128)(2,1)}, u32[]{:S(2)}, u32[]{:S(2)}) collective-permute-start(bf16[384,256]{1,0:T(8,128)(2,1)} %get-tuple-element.9), channel_id=1, source_target_pairs={{0,384},{128,512},{256,640},{384,768},{512,896},{640,0},{768,128},... | collective-permute-start | bytes 589832 | tf_op jit(solution)/shard_map/ppermute | solution.py:13
  49.3 13.3 %collective-permute-start.5 = (bf16[384,256]{1,0:T(8,128)(2,1)}, bf16[384,256]{1,0:T(8,128)(2,1)}, u32[]{:S(2)}, u32[]{:S(2)}) collective-permute-start(bf16[384,256]{1,0:T(8,128)(2,1)} %get-tuple-element.8), channel_id=1, source_target_pairs={{0,512},{128,640},{256,768},{384,896},{512,0},{640,128},{768,256},... | collective-permute-start | bytes 589832 | tf_op jit(solution)/shard_map/ppermute | solution.py:13
  62.6 6.9 %collective-permute-start.6 = (bf16[384,256]{1,0:T(8,128)(2,1)}, bf16[384,256]{1,0:T(8,128)(2,1)}, u32[]{:S(2)}, u32[]{:S(2)}) collective-permute-start(bf16[384,256]{1,0:T(8,128)(2,1)} %get-tuple-element.7), channel_id=1, source_target_pairs={{0,640},{128,768},{256,896},{384,0},{512,128},{640,256},{768,384},... | collective-permute-start | bytes 589832 | tf_op jit(solution)/shard_map/ppermute | solution.py:13
  69.6 1.9 %collective-permute-start.7 = (bf16[384,256]{1,0:T(8,128)(2,1)S(1)}, bf16[384,256]{1,0:T(8,128)(2,1)}, u32[]{:S(2)}, u32[]{:S(2)}) collective-permute-start(bf16[384,256]{1,0:T(8,128)(2,1)S(1)} %get-tuple-element.6), channel_id=1, source_target_pairs={{0,768},{128,896},{256,0},{384,128},{512,256},{640,384},{768,512},... | collective-permute-start | bytes 589832 | tf_op jit(solution)/shard_map/ppermute | solution.py:13
  71.5 3.6 %collective-permute-done.3 = bf16[384,256]{1,0:T(8,128)(2,1)S(1)} collective-permute-done((bf16[384,256]{1,0:T(8,128)(2,1)S(1)}, bf16[384,256]{1,0:T(8,128)(2,1)S(1)}, u32[]{:S(2)}, u32[]{:S(2)}) %collective-permute-start.3) | collective-permute-done | bytes 196640 | tf_op jit(solution)/shard_map/ppermute | solution.py:13
  75.8 1.9 %collective-permute-start.8 = (bf16[384,256]{1,0:T(8,128)(2,1)S(1)}, bf16[384,256]{1,0:T(8,128)(2,1)}, u32[]{:S(2)}, u32[]{:S(2)}) collective-permute-start(bf16[384,256]{1,0:T(8,128)(2,1)S(1)} %get-tuple-element.5), channel_id=1, source_target_pairs={{0,896},{128,0},{256,128},{384,256},{512,384},{640,512},{768,640},... | collective-permute-start | bytes 589832 | tf_op jit(solution)/shard_map/ppermute | solution.py:13
  77.7 2.1 %collective-permute-done.4 = bf16[384,256]{1,0:T(8,128)(2,1)} collective-permute-done((bf16[384,256]{1,0:T(8,128)(2,1)}, bf16[384,256]{1,0:T(8,128)(2,1)}, u32[]{:S(2)}, u32[]{:S(2)}) %collective-permute-start.4) | collective-permute-done | bytes 196640 | tf_op jit(solution)/shard_map/ppermute | solution.py:13
  79.8 9.6 %collective-permute-done.6 = bf16[384,256]{1,0:T(8,128)(2,1)} collective-permute-done((bf16[384,256]{1,0:T(8,128)(2,1)}, bf16[384,256]{1,0:T(8,128)(2,1)}, u32[]{:S(2)}, u32[]{:S(2)}) %collective-permute-start.6) | collective-permute-done | bytes 196640 | tf_op jit(solution)/shard_map/ppermute | solution.py:13
  89.4 7.4 %collective-permute-done.8 = bf16[384,256]{1,0:T(8,128)(2,1)} collective-permute-done((bf16[384,256]{1,0:T(8,128)(2,1)S(1)}, bf16[384,256]{1,0:T(8,128)(2,1)}, u32[]{:S(2)}, u32[]{:S(2)}) %collective-permute-start.8) | collective-permute-done | bytes 196640 | tf_op jit(solution)/shard_map/ppermute | solution.py:13
  96.9 1.7 %fusion.18 = f32[384,256]{1,0:T(8,128)S(1)} fusion(bf16[384,256]{1,0:T(8,128)(2,1)} %collective-permute-done.8, bf16[384,256]{1,0:T(8,128)(2,1)} %collective-permute-done.7, bf16[384,256]{1,0:T(8,128)(2,1)} %collective-permute-done.6, bf16[384,256]{1,0:T(8,128)(2,1)} %collective-permute-done.5, bf16[384,256]{1,0:T(8,128)(2,1)} %collective-permute-done.4, ...), kind=kLoop, calls=%fused_computation.27 | loop fusion | flops 1376256 | bytes 2162692 | tf_op jit(solution)/shard_map/add | solution.py:26
  99.3 1.7 %dynamic-slice_bitcast_fusion = bf16[24,6144]{1,0:T(8,128)(2,1)} fusion(bf16[2,24,6144]{2,1,0:T(8,128)(2,1)} %bitcast.68, s32[]{:T(128)S(6)} %select_n.109), kind=kLoop, calls=%fused_computation.28 | loop fusion | bytes 589828 | tf_op jit(solution)/shard_map/jit(dynamic_index_in_dim)/squeeze | solution.py:50
  101.0 8.3 %collective-permute-start = (bf16[24,6144]{1,0:T(8,128)(2,1)}, bf16[24,6144]{1,0:T(8,128)(2,1)}, u32[]{:S(2)}, u32[]{:S(2)}) collective-permute-start(bf16[24,6144]{1,0:T(8,128)(2,1)} %dynamic-slice_bitcast_fusion), channel_id=1, source_target_pairs={{0,1},{1,0},{2,3},{3,2},{4,5},{5,4},{6,7},{7,6},{8,9},{9,8},{10,11... | collective-permute-start | bytes 884744 | tf_op jit(solution)/shard_map/ppermute | solution.py:13
  109.3 1.5 %dynamic-slice_bitcast_fusion.10 = (bf16[96,256]{1,0:T(8,128)(2,1)}, bf16[96,256]{1,0:T(8,128)(2,1)}, bf16[96,256]{1,0:T(8,128)(2,1)}) fusion(bf16[4,96,256]{2,1,0:T(8,128)(2,1)} %convert_element_type.89, s32[]{:T(128)S(6)} %select_n.130, s32[]{:T(128)S(6)} %select_n.134, s32[]{:T(128)S(6)} %select_n.132), kind=kLoop, calls=%fused_computation.42 | loop fusion | bytes 294924 | tf_op jit(solution)/shard_map/jit(dynamic_index_in_dim)/squeeze | solution.py:21
  110.8 6.5 %collective-permute-start.10 = (bf16[96,256]{1,0:T(8,128)(2,1)}, bf16[96,256]{1,0:T(8,128)(2,1)}, u32[]{:S(2)}, u32[]{:S(2)}) collective-permute-start(bf16[96,256]{1,0:T(8,128)(2,1)} %get-tuple-element.13), channel_id=1, source_target_pairs={{0,64},{32,96},{64,0},{96,32},{1,65},{33,97},{65,1},{97,33},{2,66}... | collective-permute-start | bytes 147464 | tf_op jit(solution)/shard_map/ppermute | solution.py:13
  117.3 3.3 %collective-permute-start.11 = (bf16[96,256]{1,0:T(8,128)(2,1)}, bf16[96,256]{1,0:T(8,128)(2,1)}, u32[]{:S(2)}, u32[]{:S(2)}) collective-permute-start(bf16[96,256]{1,0:T(8,128)(2,1)} %get-tuple-element.12), channel_id=1, source_target_pairs={{0,96},{32,0},{64,32},{96,64},{1,97},{33,1},{65,33},{97,65},{2,98}... | collective-permute-start | bytes 147464 | tf_op jit(solution)/shard_map/ppermute | solution.py:13
  120.6 2.5 %collective-permute-start.9 = (bf16[96,256]{1,0:T(8,128)(2,1)}, bf16[96,256]{1,0:T(8,128)(2,1)}, u32[]{:S(2)}, u32[]{:S(2)}) collective-permute-start(bf16[96,256]{1,0:T(8,128)(2,1)} %get-tuple-element.11), channel_id=1, source_target_pairs={{0,32},{32,64},{64,96},{96,0},{1,33},{33,65},{65,97},{97,1},{2,34}... | collective-permute-start | bytes 147464 | tf_op jit(solution)/shard_map/ppermute | solution.py:13
  123.3 4.5 %collective-permute-done.10 = bf16[96,256]{1,0:T(8,128)(2,1)} collective-permute-done((bf16[96,256]{1,0:T(8,128)(2,1)}, bf16[96,256]{1,0:T(8,128)(2,1)}, u32[]{:S(2)}, u32[]{:S(2)}) %collective-permute-start.10) | collective-permute-done | bytes 49184 | tf_op jit(solution)/shard_map/ppermute | solution.py:13
  128.8 1.5 %fusion.21 = f32[96,256]{1,0:T(8,128)} fusion(bf16[96,256]{1,0:T(8,128)(2,1)} %collective-permute-done.11, bf16[96,256]{1,0:T(8,128)(2,1)} %collective-permute-done.10, bf16[96,256]{1,0:T(8,128)(2,1)} %collective-permute-done.9, f32[4,96,256]{2,1,0:T(8,128)S(1)} %bitcast.67, s32[]{:T(128)S(6)} %select_n.128), kind=kLoop, calls=%fused_computation.39 | loop fusion | flops 172032 | bytes 344068 | tf_op jit(solution)/shard_map/div | solution.py:39
  130.3 1.5 %fusion.12 = (f32[24]{0:T(128)S(1)}, f32[24]{0:T(128)S(1)}) fusion(bf16[24,6144]{1,0:T(8,128)(2,1)} %collective-permute-done, f32[6144]{0:T(1024)} %param.6, bf16[2,24,6144]{2,1,0:T(8,128)(2,1)} %bitcast.69, s32[]{:T(128)S(6)} %select_n.108, f32[24]{0:T(128)S(1)} %dynamic-slice.12, f32[24]{0:T(128)S(1)} %dynamic-slice.13, bf16[384,6144]{1,0:T(8,128)(2,1)} %param.5, ...), kind=kLoop, calls=%fused_computation.20 | loop fusion | flops 1474512 | bytes 909704 | tf_op jit(solution)/shard_map/reduce_sum | solution.py:73
  131.8 2.3 %add_convert_fusion = bf16[24,6144]{1,0:T(8,128)(2,1)} fusion(bf16[24,6144]{1,0:T(8,128)(2,1)} %param.9, bf16[24,6144]{1,0:T(8,128)(2,1)} %collective-permute-done, f32[24]{0:T(128)S(1)} %get-tuple-element.14, f32[24]{0:T(128)S(1)} %dynamic-slice.13, f32[24]{0:T(128)S(1)} %get-tuple-element.15, f32[6144]{0:T(1024)} %param.6, f32[24]{0:T(128)S(1)} %dynamic-slice.12, ...), kind=kLoop, calls=%fused_computation.17 | loop fusion | flops 2064384 | bytes 1499528 | tf_op jit(solution)/shard_map/convert_element_type | solution.py:78
  (31 shorter events, 5.5 us)
Async XLA Ops:
  7.2 1.9 %copy-start = (bf16[6144,256]{1,0:T(8,128)(2,1)S(1)}, bf16[6144,256]{1,0:T(8,128)(2,1)}, u32[]{:S(2)}) copy-start(bf16[6144,256]{1,0:T(8,128)(2,1)} %param.7) | copy-start | bytes 9437188
  7.2 92.1 %reduce-scatter.2.cloned.1.call-start = ((), (), s32[]{:S(2)}) async-start(), calls=%async_computation.1 | async-start | bytes 5308416 | tf_op jit(solution)/shard_map/reduce_scatter | solution.py:46
  13.7 3.8 %copy-start.1 = (bf16[384,6144]{1,0:T(8,128)(2,1)S(1)}, bf16[384,6144]{1,0:T(8,128)(2,1)}, u32[]{:S(2)}) copy-start(bf16[384,6144]{1,0:T(8,128)(2,1)} %param.5) | copy-start | bytes 14155780
  13.7 5.1 %copy-start.4 = (bf16[384,256]{1,0:T(8,128)(2,1)S(1)}, bf16[384,256]{1,0:T(8,128)(2,1)}, u32[]{:S(2)}) copy-start(bf16[384,256]{1,0:T(8,128)(2,1)} %param.8) | copy-start | bytes 589828
  13.7 5.1 %copy-start.7 = (f32[6144]{0:T(1024)S(1)}, f32[6144]{0:T(1024)}, u32[]{:S(2)}) copy-start(f32[6144]{0:T(1024)} %param.6) | copy-start | bytes 73732
  21.5 2.7 %copy-start.3 = (f32[6144,256]{1,0:T(8,128)}, f32[6144,256]{1,0:T(8,128)S(1)}, u32[]{:S(2)}) copy-start(f32[6144,256]{1,0:T(8,128)S(1)} %fusion.5) | copy-start | bytes 18874372
  25.6 5.6 %collective-permute-start.1 = (bf16[32,96,256]{2,1,0:T(8,128)(2,1)}, bf16[32,96,256]{2,1,0:T(8,128)(2,1)}, u32[]{:S(2)}, u32[]{:S(2)}) collective-permute-start(bf16[32,96,256]{2,1,0:T(8,128)(2,1)} %fusion.10), channel_id=1, source_target_pairs={{0,16},{16,0},{1,17},{17,1},{2,18},{18,2},{3,19},{19,3},{4,20},{20... | collective-permute-start | bytes 4718600 | tf_op jit(solution)/shard_map/ppermute | solution.py:13
  34.0 1.6 %copy-start.2 = (f32[32,96,256]{2,1,0:T(8,128)}, f32[32,96,256]{2,1,0:T(8,128)S(1)}, u32[]{:S(2)}) copy-start(f32[32,96,256]{2,1,0:T(8,128)S(1)} %bitcast_add_fusion) | copy-start | bytes 9437188
  36.6 32.9 %collective-permute-start.2 = (bf16[384,256]{1,0:T(8,128)(2,1)S(1)}, bf16[384,256]{1,0:T(8,128)(2,1)S(1)}, u32[]{:S(2)}, u32[]{:S(2)}) collective-permute-start(bf16[384,256]{1,0:T(8,128)(2,1)S(1)} %get-tuple-element.4), channel_id=1, source_target_pairs={{0,128},{128,256},{256,384},{384,512},{512,640},{640,768},{768,896... | collective-permute-start | bytes 589832 | tf_op jit(solution)/shard_map/ppermute | solution.py:13
  40.2 34.9 %collective-permute-start.3 = (bf16[384,256]{1,0:T(8,128)(2,1)S(1)}, bf16[384,256]{1,0:T(8,128)(2,1)S(1)}, u32[]{:S(2)}, u32[]{:S(2)}) collective-permute-start(bf16[384,256]{1,0:T(8,128)(2,1)S(1)} %get-tuple-element.10), channel_id=1, source_target_pairs={{0,256},{128,384},{256,512},{384,640},{512,768},{640,896},{768,0},... | collective-permute-start | bytes 589832 | tf_op jit(solution)/shard_map/ppermute | solution.py:13
  46.2 33.7 %collective-permute-start.4 = (bf16[384,256]{1,0:T(8,128)(2,1)}, bf16[384,256]{1,0:T(8,128)(2,1)}, u32[]{:S(2)}, u32[]{:S(2)}) collective-permute-start(bf16[384,256]{1,0:T(8,128)(2,1)} %get-tuple-element.9), channel_id=1, source_target_pairs={{0,384},{128,512},{256,640},{384,768},{512,896},{640,0},{768,128},... | collective-permute-start | bytes 589832 | tf_op jit(solution)/shard_map/ppermute | solution.py:13
  49.3 30.5 %collective-permute-start.5 = (bf16[384,256]{1,0:T(8,128)(2,1)}, bf16[384,256]{1,0:T(8,128)(2,1)}, u32[]{:S(2)}, u32[]{:S(2)}) collective-permute-start(bf16[384,256]{1,0:T(8,128)(2,1)} %get-tuple-element.8), channel_id=1, source_target_pairs={{0,512},{128,640},{256,768},{384,896},{512,0},{640,128},{768,256},... | collective-permute-start | bytes 589832 | tf_op jit(solution)/shard_map/ppermute | solution.py:13
  62.6 26.8 %collective-permute-start.6 = (bf16[384,256]{1,0:T(8,128)(2,1)}, bf16[384,256]{1,0:T(8,128)(2,1)}, u32[]{:S(2)}, u32[]{:S(2)}) collective-permute-start(bf16[384,256]{1,0:T(8,128)(2,1)} %get-tuple-element.7), channel_id=1, source_target_pairs={{0,640},{128,768},{256,896},{384,0},{512,128},{640,256},{768,384},... | collective-permute-start | bytes 589832 | tf_op jit(solution)/shard_map/ppermute | solution.py:13
  69.6 5.5 %copy-start.5 = (bf16[384,256]{1,0:T(8,128)(2,1)}, bf16[384,256]{1,0:T(8,128)(2,1)S(1)}, u32[]{:S(2)}) copy-start(bf16[384,256]{1,0:T(8,128)(2,1)S(1)} %collective-permute-done.2) | copy-start | bytes 589828
  69.6 19.9 %collective-permute-start.7 = (bf16[384,256]{1,0:T(8,128)(2,1)S(1)}, bf16[384,256]{1,0:T(8,128)(2,1)}, u32[]{:S(2)}, u32[]{:S(2)}) collective-permute-start(bf16[384,256]{1,0:T(8,128)(2,1)S(1)} %get-tuple-element.6), channel_id=1, source_target_pairs={{0,768},{128,896},{256,0},{384,128},{512,256},{640,384},{768,512},... | collective-permute-start | bytes 589832 | tf_op jit(solution)/shard_map/ppermute | solution.py:13
  75.1 0.7 copy-start.6
  75.8 21.1 %collective-permute-start.8 = (bf16[384,256]{1,0:T(8,128)(2,1)S(1)}, bf16[384,256]{1,0:T(8,128)(2,1)}, u32[]{:S(2)}, u32[]{:S(2)}) collective-permute-start(bf16[384,256]{1,0:T(8,128)(2,1)S(1)} %get-tuple-element.5), channel_id=1, source_target_pairs={{0,896},{128,0},{256,128},{384,256},{512,384},{640,512},{768,640},... | collective-permute-start | bytes 589832 | tf_op jit(solution)/shard_map/ppermute | solution.py:13
  101.0 29.4 %collective-permute-start = (bf16[24,6144]{1,0:T(8,128)(2,1)}, bf16[24,6144]{1,0:T(8,128)(2,1)}, u32[]{:S(2)}, u32[]{:S(2)}) collective-permute-start(bf16[24,6144]{1,0:T(8,128)(2,1)} %dynamic-slice_bitcast_fusion), channel_id=1, source_target_pairs={{0,1},{1,0},{2,3},{3,2},{4,5},{5,4},{6,7},{7,6},{8,9},{9,8},{10,11... | collective-permute-start | bytes 884744 | tf_op jit(solution)/shard_map/ppermute | solution.py:13
  110.8 17.1 %collective-permute-start.10 = (bf16[96,256]{1,0:T(8,128)(2,1)}, bf16[96,256]{1,0:T(8,128)(2,1)}, u32[]{:S(2)}, u32[]{:S(2)}) collective-permute-start(bf16[96,256]{1,0:T(8,128)(2,1)} %get-tuple-element.13), channel_id=1, source_target_pairs={{0,64},{32,96},{64,0},{96,32},{1,65},{33,97},{65,1},{97,33},{2,66}... | collective-permute-start | bytes 147464 | tf_op jit(solution)/shard_map/ppermute | solution.py:13
  117.3 10.6 %collective-permute-start.11 = (bf16[96,256]{1,0:T(8,128)(2,1)}, bf16[96,256]{1,0:T(8,128)(2,1)}, u32[]{:S(2)}, u32[]{:S(2)}) collective-permute-start(bf16[96,256]{1,0:T(8,128)(2,1)} %get-tuple-element.12), channel_id=1, source_target_pairs={{0,96},{32,0},{64,32},{96,64},{1,97},{33,1},{65,33},{97,65},{2,98}... | collective-permute-start | bytes 147464 | tf_op jit(solution)/shard_map/ppermute | solution.py:13
  120.6 8.2 %collective-permute-start.9 = (bf16[96,256]{1,0:T(8,128)(2,1)}, bf16[96,256]{1,0:T(8,128)(2,1)}, u32[]{:S(2)}, u32[]{:S(2)}) collective-permute-start(bf16[96,256]{1,0:T(8,128)(2,1)} %get-tuple-element.11), channel_id=1, source_target_pairs={{0,32},{32,64},{64,96},{96,0},{1,33},{33,65},{65,97},{97,1},{2,34}... | collective-permute-start | bytes 147464 | tf_op jit(solution)/shard_map/ppermute | solution.py:13
Sparse Core Ops, SparseCore 0:
  13.8 76.1 reduce-scatter.1

commit v2 on v1

v2 whole, which is shorter than its diff:
```python
import jax
import jax.numpy as jnp
from jax import lax
from jax.sharding import Mesh, PartitionSpec as P

DP = ("y", "z_lo", "core")
TENSOR = ("x", "z_hi")
SPLIT = (8, 4, 2, 8, 2)


def wide(part):
    return part.astype(jnp.float32)


def narrow(part):
    return part.astype(jnp.bfloat16)


def swap(part, axis, bit):
    return lax.ppermute(part, axis, [(i, i ^ bit) for i in range(lax.axis_size(axis))])


def swap_even(part, axis):
    return swap(part, axis, 1)


def swap_odd(part, axis):
    size = lax.axis_size(axis)
    return lax.ppermute(
        part, axis, [(i, (i + 1 if i % 2 else i - 1) % size) for i in range(size)]
    )


def halve(total, axis, bit, dim):
    mine = (lax.axis_index(axis) // bit) % 2
    send = lax.dynamic_index_in_dim(total, 1 - mine, dim, False)
    keep = lax.dynamic_index_in_dim(total, mine, dim, False)
    return wide(keep) + wide(swap(narrow(send), axis, bit))


def weight_reduce(term):
    replicas = lax.axis_size(DP)
    rows, columns = term.shape[0] // replicas, term.shape[1]
    total = term.reshape((2,) * 6 + (rows, columns))
    total = halve(total, "core", 1, 5)
    total = halve(total, "y", 1, 2)
    total = halve(total, "z_lo", 1, 3)
    total = halve(total, "z_lo", 2, 2)
    total = halve(total, "y", 2, 1)
    total = halve(total, "y", 4, 0)
    return total / replicas


def product(query_grad, w_query):
    return narrow(
        lax.dot_general(
            query_grad, w_query, (((1,), (1,)), ((), ())), preferred_element_type=jnp.float32
        )
    )


def feature_reduce(query_grad, w_query):
    size, sets = lax.axis_size("x"), lax.axis_size("z_hi")
    far = size // 2
    rows = query_grad.shape[0] // (size * sets)
    x, z_hi = lax.axis_index("x"), lax.axis_index("z_hi")
    parity = x % 2
    way = 1 - 2 * parity
    chunk = lax.dynamic_slice_in_dim(query_grad, (x + far) % size * (sets * rows), sets * rows, 0)
    first = product(chunk, w_query).reshape(sets, rows, -1)
    first, query_grad = lax.optimization_barrier((first, query_grad))
    one = swap_even(lax.dynamic_index_in_dim(first, parity, 0, False), "x")
    two = swap_odd(lax.dynamic_index_in_dim(first, 1 - parity, 0, False), "x")
    terms = product(query_grad, w_query).reshape(size, sets, rows, -1)

    def term(step):
        return wide(lax.dynamic_index_in_dim(terms, (x + step + size) % size, 0, False))

    which = jnp.arange(sets)[:, None, None]
    one = jnp.where(which == 1 - parity, one[None], jnp.bfloat16(0))
    two = jnp.where(which == parity, two[None], jnp.bfloat16(0))
    for step in range(far - 1, 0, -1):
        up = narrow(term(way * step) + wide(two))
        down = narrow(term(-way * step) + wide(one))
        up, down = lax.optimization_barrier((up, down))
        one, two = swap_even(up, "x"), swap_odd(down, "x")
    total = term(0) + wide(one) + wide(two)
    own = lax.dynamic_index_in_dim(total, z_hi, 0, False)
    other = lax.dynamic_index_in_dim(total, 1 - z_hi, 0, False)
    return own + wide(swap(narrow(other), "z_hi", 1))


def per_device(inputs, ln_gain, w_query, query_grad, skip_grad):
    d_scaled = feature_reduce(query_grad, w_query)
    values = inputs.astype(jnp.float32)
    mean = jnp.mean(values, axis=1, keepdims=True)
    center = values - mean
    inverse = lax.rsqrt(jnp.mean(center * center, axis=1, keepdims=True) + 1e-06)
    scaled = (center * inverse * ln_gain[None, :]).astype(jnp.bfloat16)
    weight_grad = weight_reduce(
        narrow(
            lax.dot_general(
                scaled, query_grad, (((0,), (0,)), ((), ())), preferred_element_type=jnp.float32
            )
        )
    )

    own_rows = skip_grad.shape[0]
    first = lax.axis_index(TENSOR) * own_rows
    own_values = lax.dynamic_slice_in_dim(inputs, first, own_rows, 0).astype(jnp.float32)
    mean_own = lax.dynamic_slice_in_dim(mean, first, own_rows, 0)
    inverse_own = lax.dynamic_slice_in_dim(inverse, first, own_rows, 0)
    normed_own = (own_values - mean_own) * inverse_own
    gated = d_scaled * ln_gain[None, :]
    mean_g = jnp.mean(gated, axis=1, keepdims=True)
    mean_gn = jnp.mean(gated * normed_own, axis=1, keepdims=True)
    input_grad = skip_grad.astype(jnp.float32) + inverse_own * (
        gated - mean_g - normed_own * mean_gn
    )
    return (input_grad.astype(jnp.bfloat16), weight_grad)


def solution(mesh):
    fine = Mesh(mesh.devices.reshape(SPLIT), DP + TENSOR)
    placed = (P(DP, None), P(), P(None, TENSOR), P(DP, TENSOR), P(DP + TENSOR, None))
    return jax.shard_map(
        per_device,
        mesh=fine,
        in_specs=placed,
        out_specs=(P(DP + TENSOR, None), P(DP, TENSOR)),
        check_vma=False,
    )
```

time: 142 us -> 162 us (1.14)
  the two profiles are of different devices: /device:TPU:16 before, /device:TPU:10 now
where the time goes in v2:
time: 162 us; the launch traced here: 161 us
  starting transfers between devices  71.1 us (44%)
  waiting for transfers between devices  44.1 us (27%)
  other arithmetic  23.7 us (15%)
  local copies, waits for them, and re-layouts  10.6 us (7%)
  matrix products  10.5 us (6%)
    ppermute x11, starting transfers between devices, swap(): lax.ppermute(part, axis, [(i, i ^ bit) for i in range(lax.axis_size(axis))])  52.4 us
    ppermute x11, waiting for transfers between devices, swap(): lax.ppermute(part, axis, [(i, i ^ bit) for i in range(lax.axis_size(axis))])  31.3 us
    ppermute x4, starting transfers between devices, swap_odd(): lax.ppermute(part, axis, [(i, (i + 1 if i % 2 else i - 1) % size) for i i...  18.7 us
    ppermute x4, waiting for transfers between devices, swap_odd(): lax.ppermute(part, axis, [(i, (i + 1 if i % 2 else i - 1) % size) for i i...  12.8 us
    convert_element_type x3, other arithmetic, narrow(): return part.astype(jnp.bfloat16)  7.44 us
    dot_general x2, matrix products, product(): lax.dot_general(query_grad, w_query, (((1,), (1,)), ((), ())), preferred_...  6.15 us
    dot_general x1, matrix products, per_device(): lax.dot_general(scaled, query_grad, (((0,), (0,)), ((), ())), preferred_e...  4.35 us
    add x5, other arithmetic, halve(): return wide(keep) + wide(swap(narrow(send), axis, bit))  3.86 us
  transfers between devices with their start and end apart: 15, of which 9 were waited for; matrix products, arithmetic and copies ran while one was open for 20% of the time, Pallas kernels for 0%

profile of v2, /device:TPU:10, one launch (start us, length us, event | category | flops | bytes accessed | tf_op | source)
XLA Modules:
  0.0 161.3 jit_solution(16644095834458761996)
XLA Ops:
  2.5 2.6 %convolution_convert_fusion.2 = bf16[48,6144]{1,0:T(8,128)(2,1)} fusion(bf16[6144,256]{1,0:T(8,128)(2,1)S(1)} %copy-done, bf16[384,256]{1,0:T(8,128)(2,1)} %param.8, s32[]{:T(128)S(6)} %select_n.171), kind=kOutput, calls=%fused_computation.9 | convolution fusion | flops 151289856 | bytes 3760132 | tf_op jit(solution)/shard_map/dot_general | solution.py:56
  7.0 3.3 %collective-permute-start.1 = (bf16[24,6144]{1,0:T(8,128)(2,1)}, bf16[24,6144]{1,0:T(8,128)(2,1)}, u32[]{:S(2)}, u32[]{:S(2)}) collective-permute-start(bf16[24,6144]{1,0:T(8,128)(2,1)} %get-tuple-element.28), channel_id=1, source_target_pairs={{0,2},{2,0},{4,6},{6,4},{8,10},{10,8},{12,14},{14,12},{1,3},{3,1},... | collective-permute-start | bytes 884744 | tf_op jit(solution)/shard_map/ppermute | solution.py:20
  10.4 1.9 %collective-permute-start = (bf16[24,6144]{1,0:T(8,128)(2,1)}, bf16[24,6144]{1,0:T(8,128)(2,1)}, u32[]{:S(2)}, u32[]{:S(2)}) collective-permute-start(bf16[24,6144]{1,0:T(8,128)(2,1)} %get-tuple-element.29), channel_id=1, source_target_pairs={{0,14},{2,4},{4,2},{6,8},{8,6},{10,12},{12,10},{14,0},{1,15},{3,5}... | collective-permute-start | bytes 884744 | tf_op jit(solution)/shard_map/ppermute | solution.py:29
  12.4 3.6 %convolution_convert_fusion = bf16[384,6144]{1,0:T(8,128)(2,1)} fusion(bf16[384,256]{1,0:T(8,128)(2,1)S(1)} %copy-done.4, bf16[6144,256]{1,0:T(8,128)(2,1)S(1)} %copy-done), kind=kOutput, calls=%fused_computation.7 | convolution fusion | flops 1210318848 | bytes 8060928 | tf_op jit(solution)/shard_map/dot_general | solution.py:56
  16.0 3.0 %convert_reduce_fusion = f32[384]{0:T(512)S(1)} fusion(bf16[384,6144]{1,0:T(8,128)(2,1)} %param.5), kind=kLoop, calls=%fused_computation.1 | loop fusion | flops 4718208 | bytes 4720128 | tf_op jit(solution)/shard_map/reduce_sum | solution.py:96
  19.1 2.0 %collective-permute-done = bf16[24,6144]{1,0:T(8,128)(2,1)} collective-permute-done((bf16[24,6144]{1,0:T(8,128)(2,1)}, bf16[24,6144]{1,0:T(8,128)(2,1)}, u32[]{:S(2)}, u32[]{:S(2)}) %collective-permute-start) | collective-permute-done | bytes 294944 | tf_op jit(solution)/shard_map/ppermute | solution.py:29
  21.0 2.0 %fusion.11 = (bf16[2,24,6144]{2,1,0:T(8,128)(2,1)S(1)}, bf16[2,24,6144]{2,1,0:T(8,128)(2,1)S(1)}) fusion(bf16[8,2,24,6144]{3,2,1,0:T(8,128)(2,1)} %bitcast.74, s32[]{:T(128)S(6)} %select_n.184, pred[2]{0:T(512)(128)(4,1)S(1)} %iota_compare_fusion, bf16[24,6144]{1,0:T(8,128)(2,1)} %collective-permute-done.1, bf16[24,6144]{1,0:T(8,128)(2,1)} %collective-permute-done, ...), kind=kLoop, calls=%fused_computation.23 | loop fusion | flops 2949120 | bytes 2949132 | tf_op jit(solution)/shard_map/convert_element_type | solution.py:16
  23.0 3.8 %collective-permute-start.3 = (bf16[2,24,6144]{2,1,0:T(8,128)(2,1)S(1)}, bf16[2,24,6144]{2,1,0:T(8,128)(2,1)S(1)}, u32[]{:S(2)}, u32[]{:S(2)}) collective-permute-start(bf16[2,24,6144]{2,1,0:T(8,128)(2,1)S(1)} %get-tuple-element.13), channel_id=1, source_target_pairs={{0,2},{2,0},{4,6},{6,4},{8,10},{10,8},{12,14},{14,12},{1,3},{3,1},... | collective-permute-start | bytes 1769480 | tf_op jit(solution)/shard_map/ppermute | solution.py:20
  26.9 10.9 %collective-permute-start.2 = (bf16[2,24,6144]{2,1,0:T(8,128)(2,1)S(1)}, bf16[2,24,6144]{2,1,0:T(8,128)(2,1)S(1)}, u32[]{:S(2)}, u32[]{:S(2)}) collective-permute-start(bf16[2,24,6144]{2,1,0:T(8,128)(2,1)S(1)} %get-tuple-element.12), channel_id=1, source_target_pairs={{0,14},{2,4},{4,2},{6,8},{8,6},{10,12},{12,10},{14,0},{1,15},{3,5}... | collective-permute-start | bytes 1769480 | tf_op jit(solution)/shard_map/ppermute | solution.py:29
  37.8 3.7 %fusion.2 = f32[384]{0:T(512)S(1)} fusion(bf16[384,6144]{1,0:T(8,128)(2,1)} %param.5, f32[384]{0:T(512)S(1)} %broadcast_multiply_fusion), kind=kLoop, calls=%fused_computation.4 | loop fusion | flops 9436800 | bytes 4721664 | tf_op jit(solution)/shard_map/reduce_sum | solution.py:98
  41.5 4.1 %collective-permute-done.2 = bf16[2,24,6144]{2,1,0:T(8,128)(2,1)S(1)} collective-permute-done((bf16[2,24,6144]{2,1,0:T(8,128)(2,1)S(1)}, bf16[2,24,6144]{2,1,0:T(8,128)(2,1)S(1)}, u32[]{:S(2)}, u32[]{:S(2)}) %collective-permute-start.2) | collective-permute-done | bytes 589856 | tf_op jit(solution)/shard_map/ppermute | solution.py:29
  45.6 2.6 %fusion.10 = (bf16[2,24,6144]{2,1,0:T(8,128)(2,1)}, bf16[2,24,6144]{2,1,0:T(8,128)(2,1)}) fusion(bf16[2,24,6144]{2,1,0:T(8,128)(2,1)S(1)} %collective-permute-done.3, bf16[8,2,24,6144]{3,2,1,0:T(8,128)(2,1)} %bitcast.75, s32[]{:T(128)S(6)} %select_n.188, bf16[2,24,6144]{2,1,0:T(8,128)(2,1)S(1)} %collective-permute-done.2, s32[]{:T(128)S(6)} %select_n.178), kind=kLoop, calls=%fused_computation.21 | loop fusion | flops 2359296 | bytes 3538952 | tf_op jit(solution)/shard_map/convert_element_type | solution.py:16
  48.2 5.0 %collective-permute-start.5 = (bf16[2,24,6144]{2,1,0:T(8,128)(2,1)}, bf16[2,24,6144]{2,1,0:T(8,128)(2,1)}, u32[]{:S(2)}, u32[]{:S(2)}) collective-permute-start(bf16[2,24,6144]{2,1,0:T(8,128)(2,1)} %get-tuple-element.15), channel_id=1, source_target_pairs={{0,2},{2,0},{4,6},{6,4},{8,10},{10,8},{12,14},{14,12},{1,3},{3,1},... | collective-permute-start | bytes 1769480 | tf_op jit(solution)/shard_map/ppermute | solution.py:20
  53.3 3.1 %collective-permute-start.4 = (bf16[2,24,6144]{2,1,0:T(8,128)(2,1)}, bf16[2,24,6144]{2,1,0:T(8,128)(2,1)}, u32[]{:S(2)}, u32[]{:S(2)}) collective-permute-start(bf16[2,24,6144]{2,1,0:T(8,128)(2,1)} %get-tuple-element.14), channel_id=1, source_target_pairs={{0,14},{2,4},{4,2},{6,8},{8,6},{10,12},{12,10},{14,0},{1,15},{3,5}... | collective-permute-start | bytes 1769480 | tf_op jit(solution)/shard_map/ppermute | solution.py:29
  56.4 4.4 %convolution_convert_fusion.1 = bf16[6144,256]{1,0:T(8,128)(2,1)} fusion(bf16[384,256]{1,0:T(8,128)(2,1)S(1)} %copy-done.4, bf16[384,6144]{1,0:T(8,128)(2,1)S(1)} %bitcast.79, f32[6144]{0:T(1024)S(1)} %copy-done.6, f32[384]{0:T(512)S(1)} %add_rsqrt_fusion, f32[384]{0:T(512)S(1)} %broadcast_multiply_fusion), kind=kOutput, calls=%fused_computation.8 | convolution fusion | flops 1221328896 | bytes 8088576 | tf_op jit(solution)/shard_map/dot_general | solution.py:102
  60.7 3.5 %constant_dynamic-slice_fusion.1 = (bf16[2,2,2,2,2,1,96,256]{7,6,5,4,3,2,1,0:T(8,128)(2,1)}, bf16[2,2,2,2,2,1,96,256]{7,6,5,4,3,2,1,0:T(8,128)(2,1)S(1)}) fusion(bf16[2,2,2,2,2,2,96,256]{7,6,5,4,3,2,1,0:T(8,128)(2,1)} %bitcast.80, s32[]{:T(128)S(6)} %select_n.194, s32[]{:T(128)S(6)} %select_n.195), kind=kLoop, calls=%fused_computation.58 | loop fusion | bytes 6291464 | tf_op jit(solution)/shard_map/jit(dynamic_index_in_dim)/dynamic_slice | solution.py:37
  67.5 2.9 %fusion.9 = (bf16[2,24,6144]{2,1,0:T(8,128)(2,1)}, bf16[2,24,6144]{2,1,0:T(8,128)(2,1)}) fusion(bf16[2,24,6144]{2,1,0:T(8,128)(2,1)} %collective-permute-done.5, bf16[8,2,24,6144]{3,2,1,0:T(8,128)(2,1)} %bitcast.76, s32[]{:T(128)S(6)} %select_n.190, bf16[2,24,6144]{2,1,0:T(8,128)(2,1)} %collective-permute-done.4, s32[]{:T(128)S(6)} %select_n.176), kind=kLoop, calls=%fused_computation.19 | loop fusion | flops 2359296 | bytes 3538952 | tf_op jit(solution)/shard_map/convert_element_type | solution.py:16
  70.4 2.8 %collective-permute-start.7 = (bf16[2,24,6144]{2,1,0:T(8,128)(2,1)}, bf16[2,24,6144]{2,1,0:T(8,128)(2,1)}, u32[]{:S(2)}, u32[]{:S(2)}) collective-permute-start(bf16[2,24,6144]{2,1,0:T(8,128)(2,1)} %get-tuple-element.17), channel_id=1, source_target_pairs={{0,14},{2,4},{4,2},{6,8},{8,6},{10,12},{12,10},{14,0},{1,15},{3,5}... | collective-permute-start | bytes 1769480 | tf_op jit(solution)/shard_map/ppermute | solution.py:29
  73.2 3.8 %collective-permute-start.6 = (bf16[2,24,6144]{2,1,0:T(8,128)(2,1)}, bf16[2,24,6144]{2,1,0:T(8,128)(2,1)}, u32[]{:S(2)}, u32[]{:S(2)}) collective-permute-start(bf16[2,24,6144]{2,1,0:T(8,128)(2,1)} %get-tuple-element.16), channel_id=1, source_target_pairs={{0,2},{2,0},{4,6},{6,4},{8,10},{10,8},{12,14},{14,12},{1,3},{3,1},... | collective-permute-start | bytes 1769480 | tf_op jit(solution)/shard_map/ppermute | solution.py:20
  77.1 2.4 %convert_add_fusion = f32[2,2,2,2,2,96,256]{6,5,0,1,3,4,2:T(8,128)S(1)} fusion(bf16[2,2,2,2,2,96,256]{6,5,0,1,3,4,2:T(8,128)(2,1)} %collective-permute-done.9, bf16[2,2,2,2,2,1,96,256]{7,6,5,4,3,2,1,0:T(8,128)(2,1)} %get-tuple-element.26), kind=kLoop, calls=%fused_computation.13 | loop fusion | flops 2359296 | bytes 6291456 | tf_op jit(solution)/shard_map/add | solution.py:38
  79.7 1.9 %collective-permute-start.10 = (bf16[2,2,2,2,96,256]{5,4,0,1,2,3:T(8,128)(2,1)S(1)}, bf16[2,2,2,2,96,256]{5,4,0,1,2,3:T(8,128)(2,1)S(1)}, u32[]{:S(2)}, u32[]{:S(2)}) collective-permute-start(bf16[2,2,2,2,96,256]{5,4,0,1,2,3:T(8,128)(2,1)S(1)} %fusion.16), channel_id=1, source_target_pairs={{0,128},{128,0},{256,384},{384,256},{512,640},{640,512},{768,896},... | collective-permute-start | bytes 2359304 | tf_op jit(solution)/shard_map/ppermute | solution.py:20
  81.6 6.7 %collective-permute-done.7 = bf16[2,24,6144]{2,1,0:T(8,128)(2,1)} collective-permute-done((bf16[2,24,6144]{2,1,0:T(8,128)(2,1)}, bf16[2,24,6144]{2,1,0:T(8,128)(2,1)}, u32[]{:S(2)}, u32[]{:S(2)}) %collective-permute-start.7) | collective-permute-done | bytes 589856 | tf_op jit(solution)/shard_map/ppermute | solution.py:29
  88.3 2.7 %collective-permute-done.6 = bf16[2,24,6144]{2,1,0:T(8,128)(2,1)} collective-permute-done((bf16[2,24,6144]{2,1,0:T(8,128)(2,1)}, bf16[2,24,6144]{2,1,0:T(8,128)(2,1)}, u32[]{:S(2)}, u32[]{:S(2)}) %collective-permute-start.6) | collective-permute-done | bytes 589856 | tf_op jit(solution)/shard_map/ppermute | solution.py:20
  92.7 8.3 %collective-permute-done.10 = bf16[2,2,2,2,96,256]{5,4,0,1,2,3:T(8,128)(2,1)S(1)} collective-permute-done((bf16[2,2,2,2,96,256]{5,4,0,1,2,3:T(8,128)(2,1)S(1)}, bf16[2,2,2,2,96,256]{5,4,0,1,2,3:T(8,128)(2,1)S(1)}, u32[]{:S(2)}, u32[]{:S(2)}) %collective-permute-start.10) | collective-permute-done | bytes 786464 | tf_op jit(solution)/shard_map/ppermute | solution.py:20
  103.9 11.7 %collective-permute-start.8 = (bf16[24,6144]{1,0:T(8,128)(2,1)}, bf16[24,6144]{1,0:T(8,128)(2,1)S(1)}, u32[]{:S(2)}, u32[]{:S(2)}) collective-permute-start(bf16[24,6144]{1,0:T(8,128)(2,1)} %fusion.19), channel_id=1, source_target_pairs={{0,1},{1,0},{2,3},{3,2},{4,5},{5,4},{6,7},{7,6},{8,9},{9,8},{10,11... | collective-permute-start | bytes 884744 | tf_op jit(solution)/shard_map/ppermute | solution.py:20
  116.7 6.1 %collective-permute-start.12 = (bf16[2,2,96,256]{3,2,0,1:T(8,128)(2,1)}, bf16[2,2,96,256]{3,2,0,1:T(8,128)(2,1)}, u32[]{:S(2)}, u32[]{:S(2)}) collective-permute-start(bf16[2,2,96,256]{3,2,0,1:T(8,128)(2,1)} %fusion.20), channel_id=1, source_target_pairs={{0,64},{32,96},{64,0},{96,32},{1,65},{33,97},{65,1},{97,33},{2,66}... | collective-permute-start | bytes 589832 | tf_op jit(solution)/shard_map/ppermute | solution.py:20
  123.0 4.1 %collective-permute-done.8 = bf16[24,6144]{1,0:T(8,128)(2,1)S(1)} collective-permute-done((bf16[24,6144]{1,0:T(8,128)(2,1)}, bf16[24,6144]{1,0:T(8,128)(2,1)S(1)}, u32[]{:S(2)}, u32[]{:S(2)}) %collective-permute-start.8) | collective-permute-done | bytes 294944 | tf_op jit(solution)/shard_map/ppermute | solution.py:20
  128.5 11.0 %collective-permute-done.12 = bf16[2,2,96,256]{3,2,0,1:T(8,128)(2,1)} collective-permute-done((bf16[2,2,96,256]{3,2,0,1:T(8,128)(2,1)}, bf16[2,2,96,256]{3,2,0,1:T(8,128)(2,1)}, u32[]{:S(2)}, u32[]{:S(2)}) %collective-permute-start.12) | collective-permute-done | bytes 196640 | tf_op jit(solution)/shard_map/ppermute | solution.py:20
  140.7 4.7 %collective-permute-start.13 = (bf16[2,96,256]{2,1,0:T(8,128)(2,1)S(1)}, bf16[2,96,256]{2,1,0:T(8,128)(2,1)S(1)}, u32[]{:S(2)}, u32[]{:S(2)}) collective-permute-start(bf16[2,96,256]{2,1,0:T(8,128)(2,1)S(1)} %fusion.21), channel_id=1, source_target_pairs={{0,256},{128,384},{256,0},{384,128},{512,768},{640,896},{768,512},... | collective-permute-start | bytes 294920 | tf_op jit(solution)/shard_map/ppermute | solution.py:20
  145.4 5.1 %collective-permute-done.13 = bf16[2,96,256]{2,1,0:T(8,128)(2,1)S(1)} collective-permute-done((bf16[2,96,256]{2,1,0:T(8,128)(2,1)S(1)}, bf16[2,96,256]{2,1,0:T(8,128)(2,1)S(1)}, u32[]{:S(2)}, u32[]{:S(2)}) %collective-permute-start.13) | collective-permute-done | bytes 98336 | tf_op jit(solution)/shard_map/ppermute | solution.py:20
  150.5 8.0 %collective-permute-start.14 = (bf16[96,256]{1,0:T(8,128)(2,1)S(1)}, bf16[96,256]{1,0:T(8,128)(2,1)S(1)}, u32[]{:S(2)}, u32[]{:S(2)}) collective-permute-start(bf16[96,256]{1,0:T(8,128)(2,1)S(1)} %fusion.24), channel_id=1, source_target_pairs={{0,512},{128,640},{256,768},{384,896},{512,0},{640,128},{768,256},... | collective-permute-start | bytes 147464 | tf_op jit(solution)/shard_map/ppermute | solution.py:20
  158.6 2.0 %add_convert_fusion = bf16[24,6144]{1,0:T(8,128)(2,1)} fusion(bf16[24,6144]{1,0:T(8,128)(2,1)S(1)} %copy-done.5, f32[24]{0:T(128)S(1)} %get-tuple-element.30, f32[24]{0:T(128)S(1)} %dynamic-slice.7, f32[24]{0:T(128)S(1)} %get-tuple-element.31, f32[24]{0:T(128)S(1)} %dynamic-slice.6, bf16[384,6144]{1,0:T(8,128)(2,1)} %param.5, s32[]{:T(128)S(6)} %select_n.169, ...), kind=kLoop, calls=%fused_computation.37 | loop fusion | flops 1916928 | bytes 1794440 | tf_op jit(solution)/shard_map/convert_element_type | solution.py:120
  (50 shorter events, 16.2 us)
Async XLA Ops:
  0.6 1.9 %copy-start = (bf16[6144,256]{1,0:T(8,128)(2,1)S(1)}, bf16[6144,256]{1,0:T(8,128)(2,1)}, u32[]{:S(2)}) copy-start(bf16[6144,256]{1,0:T(8,128)(2,1)} %param.7) | copy-start | bytes 9437188
  0.6 11.7 %copy-start.4 = (bf16[384,256]{1,0:T(8,128)(2,1)S(1)}, bf16[384,256]{1,0:T(8,128)(2,1)}, u32[]{:S(2)}) copy-start(bf16[384,256]{1,0:T(8,128)(2,1)} %param.8) | copy-start | bytes 589828
  7.0 12.0 %collective-permute-start.1 = (bf16[24,6144]{1,0:T(8,128)(2,1)}, bf16[24,6144]{1,0:T(8,128)(2,1)}, u32[]{:S(2)}, u32[]{:S(2)}) collective-permute-start(bf16[24,6144]{1,0:T(8,128)(2,1)} %get-tuple-element.28), channel_id=1, source_target_pairs={{0,2},{2,0},{4,6},{6,4},{8,10},{10,8},{12,14},{14,12},{1,3},{3,1},... | collective-permute-start | bytes 884744 | tf_op jit(solution)/shard_map/ppermute | solution.py:20
  10.4 10.7 %collective-permute-start = (bf16[24,6144]{1,0:T(8,128)(2,1)}, bf16[24,6144]{1,0:T(8,128)(2,1)}, u32[]{:S(2)}, u32[]{:S(2)}) collective-permute-start(bf16[24,6144]{1,0:T(8,128)(2,1)} %get-tuple-element.29), channel_id=1, source_target_pairs={{0,14},{2,4},{4,2},{6,8},{8,6},{10,12},{12,10},{14,0},{1,15},{3,5}... | collective-permute-start | bytes 884744 | tf_op jit(solution)/shard_map/ppermute | solution.py:29
  21.0 35.3 %slice-start = ((s8[4718592]{0:T(1024)(128)(4,1)}), s8[4194304]{0:T(1024)(128)(4,1)S(1)}, s32[]{:S(2)}) async-start(s8[4718592]{0:T(1024)(128)(4,1)} %bitcast.78), calls=%async_computation | async-start | bytes 8388608
  23.0 33.4 %slice-start.1 = ((s8[4718592]{0:T(1024)(128)(4,1)}), s8[524288]{0:T(1024)(128)(4,1)S(1)}, s32[]{:S(2)}) async-start(s8[4718592]{0:T(1024)(128)(4,1)} %bitcast.78), calls=%async_computation.1 | async-start | bytes 1048576
  23.0 33.4 %copy-start.6 = (f32[6144]{0:T(1024)S(1)}, f32[6144]{0:T(1024)}, u32[]{:S(2)}) copy-start(f32[6144]{0:T(1024)} %param.6) | copy-start | bytes 73732
  23.0 18.5 %collective-permute-start.3 = (bf16[2,24,6144]{2,1,0:T(8,128)(2,1)S(1)}, bf16[2,24,6144]{2,1,0:T(8,128)(2,1)S(1)}, u32[]{:S(2)}, u32[]{:S(2)}) collective-permute-start(bf16[2,24,6144]{2,1,0:T(8,128)(2,1)S(1)} %get-tuple-element.13), channel_id=1, source_target_pairs={{0,2},{2,0},{4,6},{6,4},{8,10},{10,8},{12,14},{14,12},{1,3},{3,1},... | collective-permute-start | bytes 1769480 | tf_op jit(solution)/shard_map/ppermute | solution.py:20
  26.9 18.8 %collective-permute-start.2 = (bf16[2,24,6144]{2,1,0:T(8,128)(2,1)S(1)}, bf16[2,24,6144]{2,1,0:T(8,128)(2,1)S(1)}, u32[]{:S(2)}, u32[]{:S(2)}) collective-permute-start(bf16[2,24,6144]{2,1,0:T(8,128)(2,1)S(1)} %get-tuple-element.12), channel_id=1, source_target_pairs={{0,14},{2,4},{4,2},{6,8},{8,6},{10,12},{12,10},{14,0},{1,15},{3,5}... | collective-permute-start | bytes 1769480 | tf_op jit(solution)/shard_map/ppermute | solution.py:29
  48.2 19.2 %collective-permute-start.5 = (bf16[2,24,6144]{2,1,0:T(8,128)(2,1)}, bf16[2,24,6144]{2,1,0:T(8,128)(2,1)}, u32[]{:S(2)}, u32[]{:S(2)}) collective-permute-start(bf16[2,24,6144]{2,1,0:T(8,128)(2,1)} %get-tuple-element.15), channel_id=1, source_target_pairs={{0,2},{2,0},{4,6},{6,4},{8,10},{10,8},{12,14},{14,12},{1,3},{3,1},... | collective-permute-start | bytes 1769480 | tf_op jit(solution)/shard_map/ppermute | solution.py:20
  53.3 14.2 %collective-permute-start.4 = (bf16[2,24,6144]{2,1,0:T(8,128)(2,1)}, bf16[2,24,6144]{2,1,0:T(8,128)(2,1)}, u32[]{:S(2)}, u32[]{:S(2)}) collective-permute-start(bf16[2,24,6144]{2,1,0:T(8,128)(2,1)} %get-tuple-element.14), channel_id=1, source_target_pairs={{0,14},{2,4},{4,2},{6,8},{8,6},{10,12},{12,10},{14,0},{1,15},{3,5}... | collective-permute-start | bytes 1769480 | tf_op jit(solution)/shard_map/ppermute | solution.py:29
  65.5 11.6 %collective-permute-start.9 = (bf16[2,2,2,2,2,96,256]{6,5,0,1,3,4,2:T(8,128)(2,1)}, bf16[2,2,2,2,2,96,256]{6,5,0,1,3,4,2:T(8,128)(2,1)}, u32[]{:S(2)}, u32[]{:S(2)}) collective-permute-start(bf16[2,2,2,2,2,96,256]{6,5,0,1,3,4,2:T(8,128)(2,1)} %bitcast.73), channel_id=1, source_target_pairs={{0,16},{16,0},{1,17},{17,1},{2,18},{18,2},{3,19},{19,3},{4,20},{20... | collective-permute-start | bytes 4718600 | tf_op jit(solution)/shard_map/ppermute | solution.py:20
  70.4 17.9 %collective-permute-start.7 = (bf16[2,24,6144]{2,1,0:T(8,128)(2,1)}, bf16[2,24,6144]{2,1,0:T(8,128)(2,1)}, u32[]{:S(2)}, u32[]{:S(2)}) collective-permute-start(bf16[2,24,6144]{2,1,0:T(8,128)(2,1)} %get-tuple-element.17), channel_id=1, source_target_pairs={{0,14},{2,4},{4,2},{6,8},{8,6},{10,12},{12,10},{14,0},{1,15},{3,5}... | collective-permute-start | bytes 1769480 | tf_op jit(solution)/shard_map/ppermute | solution.py:29
  73.2 17.9 %collective-permute-start.6 = (bf16[2,24,6144]{2,1,0:T(8,128)(2,1)}, bf16[2,24,6144]{2,1,0:T(8,128)(2,1)}, u32[]{:S(2)}, u32[]{:S(2)}) collective-permute-start(bf16[2,24,6144]{2,1,0:T(8,128)(2,1)} %get-tuple-element.16), channel_id=1, source_target_pairs={{0,2},{2,0},{4,6},{6,4},{8,10},{10,8},{12,14},{14,12},{1,3},{3,1},... | collective-permute-start | bytes 1769480 | tf_op jit(solution)/shard_map/ppermute | solution.py:20
  79.7 21.3 %collective-permute-start.10 = (bf16[2,2,2,2,96,256]{5,4,0,1,2,3:T(8,128)(2,1)S(1)}, bf16[2,2,2,2,96,256]{5,4,0,1,2,3:T(8,128)(2,1)S(1)}, u32[]{:S(2)}, u32[]{:S(2)}) collective-permute-start(bf16[2,2,2,2,96,256]{5,4,0,1,2,3:T(8,128)(2,1)S(1)} %fusion.16), channel_id=1, source_target_pairs={{0,128},{128,0},{256,384},{384,256},{512,640},{640,512},{768,896},... | collective-permute-start | bytes 2359304 | tf_op jit(solution)/shard_map/ppermute | solution.py:20
  92.7 23.1 %copy-start.1 = (f32[2,24,6144]{2,1,0:T(8,128)}, f32[2,24,6144]{2,1,0:T(8,128)S(1)}, u32[]{:S(2)}) copy-start(f32[2,24,6144]{2,1,0:T(8,128)S(1)} %fusion.15) | copy-start | bytes 3538948
  101.2 14.4 %collective-permute-start.11 = (bf16[2,2,2,96,256]{4,3,0,1,2:T(8,128)(2,1)S(1)}, bf16[2,2,2,96,256]{4,3,0,1,2:T(8,128)(2,1)S(1)}, u32[]{:S(2)}, u32[]{:S(2)}) collective-permute-start(bf16[2,2,2,96,256]{4,3,0,1,2:T(8,128)(2,1)S(1)} %fusion.18), channel_id=1, source_target_pairs={{0,32},{32,0},{64,96},{96,64},{1,33},{33,1},{65,97},{97,65},{2,34}... | collective-permute-start | bytes 1179656 | tf_op jit(solution)/shard_map/ppermute | solution.py:20
  103.9 23.2 %collective-permute-start.8 = (bf16[24,6144]{1,0:T(8,128)(2,1)}, bf16[24,6144]{1,0:T(8,128)(2,1)S(1)}, u32[]{:S(2)}, u32[]{:S(2)}) collective-permute-start(bf16[24,6144]{1,0:T(8,128)(2,1)} %fusion.19), channel_id=1, source_target_pairs={{0,1},{1,0},{2,3},{3,2},{4,5},{5,4},{6,7},{7,6},{8,9},{9,8},{10,11... | collective-permute-start | bytes 884744 | tf_op jit(solution)/shard_map/ppermute | solution.py:20
  115.8 1.0 copy-start.3
  116.7 22.8 %collective-permute-start.12 = (bf16[2,2,96,256]{3,2,0,1:T(8,128)(2,1)}, bf16[2,2,96,256]{3,2,0,1:T(8,128)(2,1)}, u32[]{:S(2)}, u32[]{:S(2)}) collective-permute-start(bf16[2,2,96,256]{3,2,0,1:T(8,128)(2,1)} %fusion.20), channel_id=1, source_target_pairs={{0,64},{32,96},{64,0},{96,32},{1,65},{33,97},{65,1},{97,33},{2,66}... | collective-permute-start | bytes 589832 | tf_op jit(solution)/shard_map/ppermute | solution.py:20
  123.0 35.6 %copy-start.2 = (f32[2,24,6144]{2,1,0:T(8,128)S(1)}, f32[2,24,6144]{2,1,0:T(8,128)}, u32[]{:S(2)}) copy-start(f32[2,24,6144]{2,1,0:T(8,128)} %copy-done.1) | copy-start | bytes 3538948
  123.0 35.6 %copy-start.5 = (bf16[24,6144]{1,0:T(8,128)(2,1)S(1)}, bf16[24,6144]{1,0:T(8,128)(2,1)}, u32[]{:S(2)}) copy-start(bf16[24,6144]{1,0:T(8,128)(2,1)} %param.9) | copy-start | bytes 884740
  140.7 9.8 %collective-permute-start.13 = (bf16[2,96,256]{2,1,0:T(8,128)(2,1)S(1)}, bf16[2,96,256]{2,1,0:T(8,128)(2,1)S(1)}, u32[]{:S(2)}, u32[]{:S(2)}) collective-permute-start(bf16[2,96,256]{2,1,0:T(8,128)(2,1)S(1)} %fusion.21), channel_id=1, source_target_pairs={{0,256},{128,384},{256,0},{384,128},{512,768},{640,896},{768,512},... | collective-permute-start | bytes 294920 | tf_op jit(solution)/shard_map/ppermute | solution.py:20
  150.5 10.1 %collective-permute-start.14 = (bf16[96,256]{1,0:T(8,128)(2,1)S(1)}, bf16[96,256]{1,0:T(8,128)(2,1)S(1)}, u32[]{:S(2)}, u32[]{:S(2)}) collective-permute-start(bf16[96,256]{1,0:T(8,128)(2,1)S(1)} %fusion.24), channel_id=1, source_target_pairs={{0,512},{128,640},{256,768},{384,896},{512,0},{640,128},{768,256},... | collective-permute-start | bytes 147464 | tf_op jit(solution)/shard_map/ppermute | solution.py:20

commit v3 on v1

--- a/solution.py
+++ b/solution.py
@@ -13,30 +13,16 @@
     return lax.ppermute(part, axis, [(i, (i + step) % size) for i in range(size)])
 
 
-def direct_reduce(blocks, axis):
-    size = lax.axis_size(axis)
-    me = lax.axis_index(axis)
-    narrow = blocks.astype(jnp.bfloat16)
-    arrived = [
-        shifted(lax.dynamic_index_in_dim(narrow, (me + step) % size, 0, False), axis, step)
-        for step in range(1, size)
-    ]
-    total = lax.dynamic_index_in_dim(blocks, me, 0, False)
-    for part in arrived:
-        total = total + part.astype(jnp.float32)
-    return total
-
-
 def weight_reduce(term):
-    columns = term.shape[1]
-    replicas = lax.axis_size(DP)
-    cores, z_lo, y = lax.axis_size("core"), lax.axis_size("z_lo"), lax.axis_size("y")
-    rows = term.shape[0] // replicas
-    blocks = term.reshape(y * z_lo, cores, rows, columns).transpose(1, 0, 2, 3)
-    total = direct_reduce(blocks, "core")
-    total = direct_reduce(total.reshape(y, z_lo * rows, columns), "y")
-    total = direct_reduce(total.reshape(z_lo, rows, columns), "z_lo")
-    return total / replicas
+    replicas, cores = lax.axis_size(DP), lax.axis_size("core")
+    rows, columns = term.shape[0] // replicas, term.shape[1]
+    blocks = term.astype(jnp.bfloat16).reshape(replicas // cores, cores, rows, columns)
+    me = lax.axis_index("core")
+    own = lax.dynamic_index_in_dim(blocks, me, 1, False)
+    other = lax.dynamic_index_in_dim(blocks, 1 - me, 1, False)
+    pair = own.astype(jnp.float32) + shifted(other, "core", 1).astype(jnp.float32)
+    parts = lax.all_to_all(pair.astype(jnp.bfloat16), ("y", "z_lo"), 0, 0, tiled=True)
+    return jnp.sum(parts.astype(jnp.float32), axis=0) / replicas
 
 
 def feature_reduce(query_grad, w_query):

time: 142 us -> 122 us (0.86)
  the two profiles are of different devices: /device:TPU:16 before, /device:TPU:128 now
where the time goes in v3:
time: 122 us
  waiting for transfers between devices  53.4 us (44%)
  starting transfers between devices  25.7 us (21%)
  between operations  14.1 us (12%)
  other arithmetic  14 us (11%)
  local copies, waits for them, and re-layouts  7.25 us (6%)
  matrix products  7.21 us (6%)
    reduce_scatter x1, waiting for transfers between devices, feature_reduce(): across = lax.psum_scatter(term, 'x', scatter_dimension=0, tiled=True)  38.7 us
    all_to_all x1, starting transfers between devices, weight_reduce(): lax.all_to_all(pair.astype(jnp.bfloat16), ('y', 'z_lo'), 0, 0, tiled=True)  16 us
    ppermute x2, waiting for transfers between devices, shifted(): lax.ppermute(part, axis, [(i, (i + step) % size) for i in range(size)])  14.7 us
    ppermute x2, starting transfers between devices, shifted(): lax.ppermute(part, axis, [(i, (i + step) % size) for i in range(size)])  9.73 us
    dot_general x1, matrix products, feature_reduce(): lax.dot_general(query_grad, w_query, (((1,), (1,)), ((), ())), preferred_...  4.48 us
    unnamed x10, local copies, waits for them, and re-layouts  4.04 us
    convert_element_type x1, other arithmetic, weight_reduce(): pair.astype(jnp.bfloat16)  3.67 us
    reduce_sum x1, other arithmetic, per_device(): mean = jnp.mean(values, axis=1, keepdims=True)  3.19 us
  transfers between devices with their start and end apart: 4, of which 3 were waited for; matrix products, arithmetic and copies ran while one was open for 14% of the time, Pallas kernels for 0%

profile of v3, /device:TPU:128, one launch (start us, length us, event | category | flops | bytes accessed | tf_op | source)
XLA Modules:
  0.0 121.8 jit_solution(18378330702508291516)
XLA Ops:
  7.2 0.0 copy-start
  7.2 0.0 reduce-scatter.2.cloned.1.call-start
  7.2 1.8 %copy-done = bf16[6144,256]{1,0:T(8,128)(2,1)S(1)} copy-done((bf16[6144,256]{1,0:T(8,128)(2,1)S(1)}, bf16[6144,256]{1,0:T(8,128)(2,1)}, u32[]{:S(2)}) %copy-start) | copy-done | bytes 3145752
  9.1 4.5 %convolution_convert_fusion = bf16[384,6144]{1,0:T(8,128)(2,1)} fusion(bf16[384,256]{1,0:T(8,128)(2,1)} %param.8, bf16[6144,256]{1,0:T(8,128)(2,1)S(1)} %copy-done), kind=kOutput, calls=%fused_computation.7 | convolution fusion | flops 1210318848 | bytes 8060928 | tf_op jit(solution)/shard_map/dot_general | solution.py:29
  13.5 0.0 reduce-scatter.2.cloned.1.call-update
  13.6 0.0 copy-start.1
  13.6 0.0 copy-start.3
  13.6 0.0 copy-start.4
  13.6 3.2 %convert_reduce_fusion = f32[384]{0:T(512)S(1)} fusion(bf16[384,6144]{1,0:T(8,128)(2,1)} %param.5), kind=kLoop, calls=%fused_computation.1 | loop fusion | flops 4718208 | bytes 4720128 | tf_op jit(solution)/shard_map/reduce_sum | solution.py:43
  16.8 0.5 copy-done.1
  17.3 1.4 %fusion.2 = f32[384]{0:T(512)S(1)} fusion(bf16[384,6144]{1,0:T(8,128)(2,1)S(1)} %copy-done.1, f32[384]{0:T(512)S(1)} %broadcast_multiply_fusion.1), kind=kLoop, calls=%fused_computation.4 | loop fusion | flops 9436800 | bytes 4721664 | tf_op jit(solution)/shard_map/reduce_sum | solution.py:45
  18.7 0.0 copy-done.3
  18.7 0.0 copy-done.4
  18.7 2.7 %convolution_convert_fusion.1 = bf16[6144,256]{1,0:T(8,128)(2,1)S(1)} fusion(bf16[384,256]{1,0:T(8,128)(2,1)S(1)} %copy-done.3, bf16[384,6144]{1,0:T(8,128)(2,1)S(1)} %copy-done.1, f32[6144]{0:T(1024)S(1)} %copy-done.4, f32[384]{0:T(512)S(1)} %add_rsqrt_fusion, f32[384]{0:T(512)S(1)} %broadcast_multiply_fusion.1), kind=kOutput, calls=%fused_computation.8 | convolution fusion | flops 1221328896 | bytes 8088576 | tf_op jit(solution)/shard_map/dot_general | solution.py:47
  21.5 0.0 copy-start.2
  21.5 1.7 %copy-done.2 = bf16[6144,256]{1,0:T(8,128)(2,1)} copy-done((bf16[6144,256]{1,0:T(8,128)(2,1)}, bf16[6144,256]{1,0:T(8,128)(2,1)S(1)}, u32[]{:S(2)}) %copy-start.2) | copy-done | bytes 3145752
  23.1 1.4 %dynamic-slice_bitcast_fusion = bf16[32,96,256]{2,1,0:T(8,128)(2,1)} fusion(bf16[32,2,96,256]{3,2,1,0:T(8,128)(2,1)S(1)} %bitcast.17, s32[]{:T(128)S(6)} %select_n.23), kind=kLoop, calls=%fused_computation.15 | loop fusion | bytes 3145732 | tf_op jit(solution)/shard_map/jit(dynamic_index_in_dim)/squeeze | solution.py:22
  24.5 1.9 %collective-permute-start.1 = (bf16[32,96,256]{2,1,0:T(8,128)(2,1)}, bf16[32,96,256]{2,1,0:T(8,128)(2,1)}, u32[]{:S(2)}, u32[]{:S(2)}) collective-permute-start(bf16[32,96,256]{2,1,0:T(8,128)(2,1)} %dynamic-slice_bitcast_fusion), channel_id=1, source_target_pairs={{0,16},{16,0},{1,17},{17,1},{2,18},{18,2},{3,19},{19,3},{4,20},{20... | collective-permute-start | bytes 4718600 | tf_op jit(solution)/shard_map/ppermute | solution.py:13
  26.4 3.7 %collective-permute-done.1 = bf16[32,96,256]{2,1,0:T(8,128)(2,1)} collective-permute-done((bf16[32,96,256]{2,1,0:T(8,128)(2,1)}, bf16[32,96,256]{2,1,0:T(8,128)(2,1)}, u32[]{:S(2)}, u32[]{:S(2)}) %collective-permute-start.1) | collective-permute-done | bytes 1572896 | tf_op jit(solution)/shard_map/ppermute | solution.py:13
  30.1 3.7 %fusion.9 = bf16[32,96,256]{2,1,0:T(8,128)(2,1)} fusion(bf16[32,96,256]{2,1,0:T(8,128)(2,1)} %collective-permute-done.1, bf16[32,2,96,256]{3,2,1,0:T(8,128)(2,1)} %bitcast.18, s32[]{:T(128)S(6)} %select_n.22), kind=kLoop, calls=%fused_computation.13 | loop fusion | flops 3145728 | bytes 4718596 | tf_op jit(solution)/shard_map/convert_element_type | solution.py:24
  33.8 16.0 %all-to-all-start = ((bf16[32,96,256]{2,1,0:T(8,128)(2,1)}), bf16[32,96,256]{2,1,0:T(8,128)(2,1)}, u32[]{:S(2)}, u32[]{:S(2)}) async-start(bf16[32,96,256]{2,1,0:T(8,128)(2,1)} %fusion.9), calls=%async_computation.1 | async-start | bytes 3145728 | tf_op jit(solution)/shard_map/all_to_all | solution.py:24
  49.8 0.1 dynamic-slice.7
  49.9 0.1 dynamic-slice.6
  49.9 38.7 %reduce-scatter.2.cloned.1.call-done = bf16[48,6144]{1,0:T(8,128)(2,1)} async-done(((bf16[384,6144]{1,0:T(8,128)(2,1)}), bf16[48,6144]{1,0:T(8,128)(2,1)}) %reduce-scatter.2.cloned.1.call-update) | async-done | bytes 589840 | tf_op jit(solution)/shard_map/reduce_scatter | solution.py:32
  88.7 1.7 %dynamic-slice_bitcast_fusion.1 = bf16[24,6144]{1,0:T(8,128)(2,1)} fusion(bf16[2,24,6144]{2,1,0:T(8,128)(2,1)} %bitcast.19, s32[]{:T(128)S(6)} %select_n.21), kind=kLoop, calls=%fused_computation.22 | loop fusion | bytes 589828 | tf_op jit(solution)/shard_map/jit(dynamic_index_in_dim)/squeeze | solution.py:36
  90.3 7.8 %collective-permute-start = (bf16[24,6144]{1,0:T(8,128)(2,1)}, bf16[24,6144]{1,0:T(8,128)(2,1)S(1)}, u32[]{:S(2)}, u32[]{:S(2)}) collective-permute-start(bf16[24,6144]{1,0:T(8,128)(2,1)} %dynamic-slice_bitcast_fusion.1), channel_id=1, source_target_pairs={{0,1},{1,0},{2,3},{3,2},{4,5},{5,4},{6,7},{7,6},{8,9},{9,8},{10,11... | collective-permute-start | bytes 884744 | tf_op jit(solution)/shard_map/ppermute | solution.py:13
  98.2 0.0 all-to-all-done
  98.2 1.6 %convert_reduce_fusion.1 = f32[96,256]{1,0:T(8,128)S(1)} fusion(bf16[32,96,256]{2,1,0:T(8,128)(2,1)} %all-to-all-done), kind=kLoop, calls=%fused_computation.14 | loop fusion | flops 1548288 | bytes 1671168 | tf_op jit(solution)/shard_map/reduce_sum | solution.py:25
  99.8 0.6 broadcast_multiply_fusion
  100.5 11.0 %collective-permute-done = bf16[24,6144]{1,0:T(8,128)(2,1)S(1)} collective-permute-done((bf16[24,6144]{1,0:T(8,128)(2,1)}, bf16[24,6144]{1,0:T(8,128)(2,1)S(1)}, u32[]{:S(2)}, u32[]{:S(2)}) %collective-permute-start) | collective-permute-done | bytes 294944 | tf_op jit(solution)/shard_map/ppermute | solution.py:13
  111.5 1.4 %fusion.11 = (f32[24]{0:T(128)S(1)}, f32[24]{0:T(128)S(1)}) fusion(bf16[24,6144]{1,0:T(8,128)(2,1)S(1)} %collective-permute-done, f32[6144]{0:T(1024)S(1)} %copy-done.4, bf16[2,24,6144]{2,1,0:T(8,128)(2,1)} %bitcast.20, s32[]{:T(128)S(6)} %select_n.20, f32[24]{0:T(128)S(1)} %dynamic-slice.6, f32[24]{0:T(128)S(1)} %dynamic-slice.7, ...), kind=kLoop, calls=%fused_computation.21 | loop fusion | flops 1474512 | bytes 909704 | tf_op jit(solution)/shard_map/reduce_sum | solution.py:59
  112.8 2.2 %add_convert_fusion = bf16[24,6144]{1,0:T(8,128)(2,1)} fusion(bf16[24,6144]{1,0:T(8,128)(2,1)} %param.9, bf16[24,6144]{1,0:T(8,128)(2,1)S(1)} %collective-permute-done, f32[24]{0:T(128)S(1)} %get-tuple-element.4, f32[24]{0:T(128)S(1)} %dynamic-slice.7, f32[24]{0:T(128)S(1)} %get-tuple-element.5, f32[6144]{0:T(1024)S(1)} %copy-done.4, ...), kind=kLoop, calls=%fused_computation.18 | loop fusion | flops 2064384 | bytes 1499528 | tf_op jit(solution)/shard_map/convert_element_type | solution.py:64
  (3 shorter events, 0.0 us)
Async XLA Ops:
  7.2 1.9 %copy-start = (bf16[6144,256]{1,0:T(8,128)(2,1)S(1)}, bf16[6144,256]{1,0:T(8,128)(2,1)}, u32[]{:S(2)}) copy-start(bf16[6144,256]{1,0:T(8,128)(2,1)} %param.7) | copy-start | bytes 9437188
  7.2 81.5 %reduce-scatter.2.cloned.1.call-start = ((), (), s32[]{:S(2)}) async-start(), calls=%async_computation.2 | async-start | bytes 5308416 | tf_op jit(solution)/shard_map/reduce_scatter | solution.py:32
  13.6 3.8 %copy-start.1 = (bf16[384,6144]{1,0:T(8,128)(2,1)S(1)}, bf16[384,6144]{1,0:T(8,128)(2,1)}, u32[]{:S(2)}) copy-start(bf16[384,6144]{1,0:T(8,128)(2,1)} %param.5) | copy-start | bytes 14155780
  13.6 5.1 %copy-start.3 = (bf16[384,256]{1,0:T(8,128)(2,1)S(1)}, bf16[384,256]{1,0:T(8,128)(2,1)}, u32[]{:S(2)}) copy-start(bf16[384,256]{1,0:T(8,128)(2,1)} %param.8) | copy-start | bytes 589828
  13.6 5.1 %copy-start.4 = (f32[6144]{0:T(1024)S(1)}, f32[6144]{0:T(1024)}, u32[]{:S(2)}) copy-start(f32[6144]{0:T(1024)} %param.6) | copy-start | bytes 73732
  21.5 1.7 %copy-start.2 = (bf16[6144,256]{1,0:T(8,128)(2,1)}, bf16[6144,256]{1,0:T(8,128)(2,1)S(1)}, u32[]{:S(2)}) copy-start(bf16[6144,256]{1,0:T(8,128)(2,1)S(1)} %convolution_convert_fusion.1) | copy-start | bytes 9437188
  24.5 5.6 %collective-permute-start.1 = (bf16[32,96,256]{2,1,0:T(8,128)(2,1)}, bf16[32,96,256]{2,1,0:T(8,128)(2,1)}, u32[]{:S(2)}, u32[]{:S(2)}) collective-permute-start(bf16[32,96,256]{2,1,0:T(8,128)(2,1)} %dynamic-slice_bitcast_fusion), channel_id=1, source_target_pairs={{0,16},{16,0},{1,17},{17,1},{2,18},{18,2},{3,19},{19,3},{4,20},{20... | collective-permute-start | bytes 4718600 | tf_op jit(solution)/shard_map/ppermute | solution.py:13
  33.8 64.4 %all-to-all-start = ((bf16[32,96,256]{2,1,0:T(8,128)(2,1)}), bf16[32,96,256]{2,1,0:T(8,128)(2,1)}, u32[]{:S(2)}, u32[]{:S(2)}) async-start(bf16[32,96,256]{2,1,0:T(8,128)(2,1)} %fusion.9), calls=%async_computation.1 | async-start | bytes 3145728 | tf_op jit(solution)/shard_map/all_to_all | solution.py:24
  90.3 21.1 %collective-permute-start = (bf16[24,6144]{1,0:T(8,128)(2,1)}, bf16[24,6144]{1,0:T(8,128)(2,1)S(1)}, u32[]{:S(2)}, u32[]{:S(2)}) collective-permute-start(bf16[24,6144]{1,0:T(8,128)(2,1)} %dynamic-slice_bitcast_fusion.1), channel_id=1, source_target_pairs={{0,1},{1,0},{2,3},{3,2},{4,5},{5,4},{6,7},{7,6},{8,9},{9,8},{10,11... | collective-permute-start | bytes 884744 | tf_op jit(solution)/shard_map/ppermute | solution.py:13
Sparse Core Ops, SparseCore 0:
  13.7 74.9 reduce-scatter.1

commit v4 on v2

--- a/solution.py
+++ b/solution.py
@@ -31,24 +31,21 @@
     )
 
 
-def halve(total, axis, bit, dim):
-    mine = (lax.axis_index(axis) // bit) % 2
-    send = lax.dynamic_index_in_dim(total, 1 - mine, dim, False)
-    keep = lax.dynamic_index_in_dim(total, mine, dim, False)
-    return wide(keep) + wide(swap(narrow(send), axis, bit))
+def pair_blocks(term):
+    cores, rows = lax.axis_size("core"), term.shape[0] // lax.axis_size(DP)
+    return term.reshape(-1, cores, rows, term.shape[1])
 
 
-def weight_reduce(term):
-    replicas = lax.axis_size(DP)
-    rows, columns = term.shape[0] // replicas, term.shape[1]
-    total = term.reshape((2,) * 6 + (rows, columns))
-    total = halve(total, "core", 1, 5)
-    total = halve(total, "y", 1, 2)
-    total = halve(total, "z_lo", 1, 3)
-    total = halve(total, "z_lo", 2, 2)
-    total = halve(total, "y", 2, 1)
-    total = halve(total, "y", 4, 0)
-    return total / replicas
+def core_sum(blocks):
+    me = lax.axis_index("core")
+    own = lax.dynamic_index_in_dim(blocks, me, 1, False)
+    other = lax.dynamic_index_in_dim(blocks, 1 - me, 1, False)
+    return narrow(wide(own) + wide(swap(other, "core", 1)))
+
+
+def weight_reduce(pair):
+    parts = lax.all_to_all(pair, ("y", "z_lo"), 0, 0, tiled=True)
+    return jnp.sum(wide(parts), axis=0) / lax.axis_size(DP)
 
 
 def product(query_grad, w_query):
@@ -59,7 +56,16 @@
     )
 
 
-def feature_reduce(query_grad, w_query):
+def across(part, even):
+    size, sets = lax.axis_size("x"), lax.axis_size("z_hi")
+    moves = []
+    for i in range(size):
+        to = (i + (1 if (i % 2 == 0) == even else -1)) % size
+        moves += [(i * sets + j, to * sets + 1 - j) for j in range(sets)]
+    return lax.ppermute(part, TENSOR, moves)
+
+
+def feature_reduce(query_grad, w_query, weight_term):
     size, sets = lax.axis_size("x"), lax.axis_size("z_hi")
     far = size // 2
     rows = query_grad.shape[0] // (size * sets)
@@ -72,38 +78,59 @@
     one = swap_even(lax.dynamic_index_in_dim(first, parity, 0, False), "x")
     two = swap_odd(lax.dynamic_index_in_dim(first, 1 - parity, 0, False), "x")
     terms = product(query_grad, w_query).reshape(size, sets, rows, -1)
+    blocks = pair_blocks(weight_term(query_grad))
 
     def term(step):
-        return wide(lax.dynamic_index_in_dim(terms, (x + step + size) % size, 0, False))
+        return lax.dynamic_index_in_dim(terms, (x + step + size) % size, 0, False)
+
+    def pick(parts, index):
+        return lax.dynamic_index_in_dim(parts, index, 0, False)
 
     which = jnp.arange(sets)[:, None, None]
     one = jnp.where(which == 1 - parity, one[None], jnp.bfloat16(0))
     two = jnp.where(which == parity, two[None], jnp.bfloat16(0))
-    for step in range(far - 1, 0, -1):
-        up = narrow(term(way * step) + wide(two))
-        down = narrow(term(-way * step) + wide(one))
-        up, down = lax.optimization_barrier((up, down))
+    for step in range(far - 1, 1, -1):
+        up = narrow(wide(term(way * step)) + wide(two))
+        down = narrow(wide(term(-way * step)) + wide(one))
+        if step == far - 1:
+            up, down, blocks = lax.optimization_barrier((up, down, blocks))
+        else:
+            up, down = lax.optimization_barrier((up, down))
         one, two = swap_even(up, "x"), swap_odd(down, "x")
-    total = term(0) + wide(one) + wide(two)
-    own = lax.dynamic_index_in_dim(total, z_hi, 0, False)
-    other = lax.dynamic_index_in_dim(total, 1 - z_hi, 0, False)
-    return own + wide(swap(narrow(other), "z_hi", 1))
+        if step == far - 1:
+            pair = core_sum(blocks)
+            one, two, _ = lax.optimization_barrier((one, two, pair))
+            beside = swap(pick(term(0), 1 - z_hi), "z_hi", 1)
+    ups, downs = wide(term(way)) + wide(two), wide(term(-way)) + wide(one)
+    parts = lax.optimization_barrier(
+        tuple(narrow(pick(p, index)) for index in (1 - z_hi, z_hi) for p in (ups, downs))
+    )
+    arrived = (
+        across(parts[0], True),
+        across(parts[1], False),
+        swap_even(parts[2], "x"),
+        swap_odd(parts[3], "x"),
+        beside,
+    )
+    return sum((wide(part) for part in arrived), wide(pick(term(0), z_hi))), pair
 
 
 def per_device(inputs, ln_gain, w_query, query_grad, skip_grad):
-    d_scaled = feature_reduce(query_grad, w_query)
     values = inputs.astype(jnp.float32)
     mean = jnp.mean(values, axis=1, keepdims=True)
     center = values - mean
     inverse = lax.rsqrt(jnp.mean(center * center, axis=1, keepdims=True) + 1e-06)
     scaled = (center * inverse * ln_gain[None, :]).astype(jnp.bfloat16)
-    weight_grad = weight_reduce(
-        narrow(
+
+    def weight_term(grads):
+        return narrow(
             lax.dot_general(
-                scaled, query_grad, (((0,), (0,)), ((), ())), preferred_element_type=jnp.float32
+                scaled, grads, (((0,), (0,)), ((), ())), preferred_element_type=jnp.float32
             )
         )
-    )
+
+    d_scaled, pair = feature_reduce(query_grad, w_query, weight_term)
+    weight_grad = weight_reduce(pair)
 
     own_rows = skip_grad.shape[0]
     first = lax.axis_index(TENSOR) * own_rows

time: 162 us -> 174 us (1.074)
  the two profiles are of different devices: /device:TPU:10 before, /device:TPU:8 now
where the time goes in v4:
time: 174 us; the launch traced here: 173 us
  waiting for transfers between devices  65.7 us (38%)
  starting transfers between devices  64.9 us (37%)
  other arithmetic  21.7 us (12%)
  local copies, waits for them, and re-layouts  10.6 us (6%)
  matrix products  8.78 us (5%)
    ppermute x2, waiting for transfers between devices, across(): return lax.ppermute(part, TENSOR, moves)  55.2 us
    ppermute x6, starting transfers between devices, swap(): lax.ppermute(part, axis, [(i, i ^ bit) for i in range(lax.axis_size(axis))])  26.4 us
    ppermute x4, starting transfers between devices, swap_odd(): lax.ppermute(part, axis, [(i, (i + 1 if i % 2 else i - 1) % size) for i i...  14.1 us
    all_to_all x1, starting transfers between devices, weight_reduce(): parts = lax.all_to_all(pair, ('y', 'z_lo'), 0, 0, tiled=True)  13.5 us
    ppermute x2, starting transfers between devices, across(): return lax.ppermute(part, TENSOR, moves)  11 us
    convert_element_type x3, other arithmetic, narrow(): return part.astype(jnp.bfloat16)  9.07 us
    ppermute x6, waiting for transfers between devices, swap(): lax.ppermute(part, axis, [(i, i ^ bit) for i in range(lax.axis_size(axis))])  6.27 us
    dot_general x1, matrix products, weight_term(): lax.dot_general(scaled, grads, (((0,), (0,)), ((), ())), preferred_elemen...  4.78 us
  transfers between devices with their start and end apart: 13, of which 3 were waited for; matrix products, arithmetic and copies ran while one was open for 13% of the time, Pallas kernels for 0%

profile of v4, /device:TPU:8, one launch (start us, length us, event | category | flops | bytes accessed | tf_op | source)
XLA Modules:
  0.0 172.9 jit_solution(6159397922367060182)
XLA Ops:
  0.7 1.8 %copy-done = bf16[6144,256]{1,0:T(8,128)(2,1)S(1)} copy-done((bf16[6144,256]{1,0:T(8,128)(2,1)S(1)}, bf16[6144,256]{1,0:T(8,128)(2,1)}, u32[]{:S(2)}) %copy-start) | copy-done | bytes 3145752
  2.5 2.6 %convolution_convert_fusion.2 = bf16[48,6144]{1,0:T(8,128)(2,1)} fusion(bf16[6144,256]{1,0:T(8,128)(2,1)S(1)} %copy-done, bf16[384,256]{1,0:T(8,128)(2,1)} %param.8, s32[]{:T(128)S(6)} %select_n.112), kind=kOutput, calls=%fused_computation.9 | convolution fusion | flops 151289856 | bytes 3760132 | tf_op jit(solution)/shard_map/dot_general | solution.py:53
  5.1 1.9 %dynamic-slice_bitcast_fusion.2 = (bf16[24,6144]{1,0:T(8,128)(2,1)}, bf16[24,6144]{1,0:T(8,128)(2,1)}) fusion(bf16[2,24,6144]{2,1,0:T(8,128)(2,1)} %bitcast.55, s32[]{:T(128)S(6)} %select_n.129, s32[]{:T(128)S(6)} %select_n.125), kind=kLoop, calls=%fused_computation.45 | loop fusion | bytes 1179656 | tf_op jit(solution)/shard_map/jit(dynamic_index_in_dim)/squeeze | solution.py:78
  7.0 2.4 %collective-permute-start = (bf16[24,6144]{1,0:T(8,128)(2,1)}, bf16[24,6144]{1,0:T(8,128)(2,1)}, u32[]{:S(2)}, u32[]{:S(2)}) collective-permute-start(bf16[24,6144]{1,0:T(8,128)(2,1)} %get-tuple-element.42), channel_id=1, source_target_pairs={{0,14},{2,4},{4,2},{6,8},{8,6},{10,12},{12,10},{14,0},{1,15},{3,5}... | collective-permute-start | bytes 884744 | tf_op jit(solution)/shard_map/ppermute | solution.py:29
  9.4 2.6 %collective-permute-start.1 = (bf16[24,6144]{1,0:T(8,128)(2,1)}, bf16[24,6144]{1,0:T(8,128)(2,1)}, u32[]{:S(2)}, u32[]{:S(2)}) collective-permute-start(bf16[24,6144]{1,0:T(8,128)(2,1)} %get-tuple-element.41), channel_id=1, source_target_pairs={{0,2},{2,0},{4,6},{6,4},{8,10},{10,8},{12,14},{14,12},{1,3},{3,1},... | collective-permute-start | bytes 884744 | tf_op jit(solution)/shard_map/ppermute | solution.py:20
  12.1 3.2 %convert_reduce_fusion = f32[384]{0:T(512)S(1)} fusion(bf16[384,6144]{1,0:T(8,128)(2,1)} %param.5), kind=kLoop, calls=%fused_computation.1 | loop fusion | flops 4718208 | bytes 4720128 | tf_op jit(solution)/shard_map/reduce_sum | solution.py:120
  15.9 1.4 fusion.2
  17.3 4.8 %convolution_convert_fusion.1 = bf16[6144,256]{1,0:T(8,128)(2,1)S(1)} fusion(bf16[384,256]{1,0:T(8,128)(2,1)S(1)} %copy-done.4, bf16[384,6144]{1,0:T(8,128)(2,1)} %param.5, f32[6144]{0:T(1024)S(1)} %copy-done.5, f32[384]{0:T(512)S(1)} %add_rsqrt_fusion, f32[384]{0:T(512)S(1)} %broadcast_multiply_fusion.1), kind=kOutput, calls=%fused_computation.8 | convolution fusion | flops 1221328896 | bytes 8088576 | tf_op jit(solution)/shard_map/dot_general | solution.py:127
  22.1 1.4 convolution_convert_fusion
  23.5 2.1 %copy-done.1 = bf16[384,6144]{1,0:T(8,128)(2,1)} copy-done((bf16[384,6144]{1,0:T(8,128)(2,1)}, bf16[384,6144]{1,0:T(8,128)(2,1)S(1)}, u32[]{:S(2)}) %copy-start.1) | copy-done | bytes 4718616
  25.6 2.5 %fusion.11 = (bf16[2,24,6144]{2,1,0:T(8,128)(2,1)}, bf16[2,24,6144]{2,1,0:T(8,128)(2,1)}) fusion(bf16[8,2,24,6144]{3,2,1,0:T(8,128)(2,1)S(1)} %bitcast.48, s32[]{:T(128)S(6)} %select_n.128, pred[2]{0:T(512)(128)(4,1)S(1)} %iota_compare_fusion, bf16[24,6144]{1,0:T(8,128)(2,1)} %collective-permute-done.1, bf16[24,6144]{1,0:T(8,128)(2,1)} %collective-permute-done, ...), kind=kLoop, calls=%fused_computation.21 | loop fusion | flops 2949120 | bytes 2949132 | tf_op jit(solution)/shard_map/convert_element_type | solution.py:16
  29.4 1.9 %collective-permute-start.4 = (bf16[32,96,256]{2,1,0:T(8,128)(2,1)}, bf16[32,96,256]{2,1,0:T(8,128)(2,1)}, u32[]{:S(2)}, u32[]{:S(2)}) collective-permute-start(bf16[32,96,256]{2,1,0:T(8,128)(2,1)} %dynamic-slice_bitcast_fusion), channel_id=1, source_target_pairs={{0,16},{16,0},{1,17},{17,1},{2,18},{18,2},{3,19},{19,3},{4,20},{20... | collective-permute-start | bytes 4718600 | tf_op jit(solution)/shard_map/ppermute | solution.py:20
  31.4 3.3 %collective-permute-start.2 = (bf16[2,24,6144]{2,1,0:T(8,128)(2,1)}, bf16[2,24,6144]{2,1,0:T(8,128)(2,1)}, u32[]{:S(2)}, u32[]{:S(2)}) collective-permute-start(bf16[2,24,6144]{2,1,0:T(8,128)(2,1)} %get-tuple-element.17), channel_id=1, source_target_pairs={{0,2},{2,0},{4,6},{6,4},{8,10},{10,8},{12,14},{14,12},{1,3},{3,1},... | collective-permute-start | bytes 1769480 | tf_op jit(solution)/shard_map/ppermute | solution.py:20
  34.6 4.6 %collective-permute-start.3 = (bf16[2,24,6144]{2,1,0:T(8,128)(2,1)}, bf16[2,24,6144]{2,1,0:T(8,128)(2,1)}, u32[]{:S(2)}, u32[]{:S(2)}) collective-permute-start(bf16[2,24,6144]{2,1,0:T(8,128)(2,1)} %get-tuple-element.18), channel_id=1, source_target_pairs={{0,14},{2,4},{4,2},{6,8},{8,6},{10,12},{12,10},{14,0},{1,15},{3,5}... | collective-permute-start | bytes 1769480 | tf_op jit(solution)/shard_map/ppermute | solution.py:29
  39.3 3.7 %fusion.9 = bf16[32,96,256]{2,1,0:T(8,128)(2,1)} fusion(bf16[32,96,256]{2,1,0:T(8,128)(2,1)} %collective-permute-done.4, bf16[32,2,96,256]{3,2,1,0:T(8,128)(2,1)} %bitcast.54, s32[]{:T(128)S(6)} %select_n.131), kind=kLoop, calls=%fused_computation.14 | loop fusion | flops 3145728 | bytes 4718596 | tf_op jit(solution)/shard_map/convert_element_type | solution.py:16
  43.0 6.3 %collective-permute-done.2 = bf16[2,24,6144]{2,1,0:T(8,128)(2,1)} collective-permute-done((bf16[2,24,6144]{2,1,0:T(8,128)(2,1)}, bf16[2,24,6144]{2,1,0:T(8,128)(2,1)}, u32[]{:S(2)}, u32[]{:S(2)}) %collective-permute-start.2) | collective-permute-done | bytes 589856 | tf_op jit(solution)/shard_map/ppermute | solution.py:20
  49.3 4.2 %collective-permute-done.3 = bf16[2,24,6144]{2,1,0:T(8,128)(2,1)} collective-permute-done((bf16[2,24,6144]{2,1,0:T(8,128)(2,1)}, bf16[2,24,6144]{2,1,0:T(8,128)(2,1)}, u32[]{:S(2)}, u32[]{:S(2)}) %collective-permute-start.3) | collective-permute-done | bytes 589856 | tf_op jit(solution)/shard_map/ppermute | solution.py:29
  53.5 2.9 %fusion.10 = (bf16[2,24,6144]{2,1,0:T(8,128)(2,1)}, bf16[2,24,6144]{2,1,0:T(8,128)(2,1)}) fusion(bf16[2,24,6144]{2,1,0:T(8,128)(2,1)} %collective-permute-done.2, bf16[8,2,24,6144]{3,2,1,0:T(8,128)(2,1)} %bitcast.49, s32[]{:T(128)S(6)} %select_n.134, bf16[2,24,6144]{2,1,0:T(8,128)(2,1)} %collective-permute-done.3, s32[]{:T(128)S(6)} %select_n.122), kind=kLoop, calls=%fused_computation.19 | loop fusion | flops 2359296 | bytes 3538952 | tf_op jit(solution)/shard_map/convert_element_type | solution.py:16
  56.4 4.6 %collective-permute-start.5 = (bf16[2,24,6144]{2,1,0:T(8,128)(2,1)}, bf16[2,24,6144]{2,1,0:T(8,128)(2,1)}, u32[]{:S(2)}, u32[]{:S(2)}) collective-permute-start(bf16[2,24,6144]{2,1,0:T(8,128)(2,1)} %get-tuple-element.22), channel_id=1, source_target_pairs={{0,14},{2,4},{4,2},{6,8},{8,6},{10,12},{12,10},{14,0},{1,15},{3,5}... | collective-permute-start | bytes 1769480 | tf_op jit(solution)/shard_map/ppermute | solution.py:29
  61.1 10.5 %collective-permute-start.6 = (bf16[2,24,6144]{2,1,0:T(8,128)(2,1)}, bf16[2,24,6144]{2,1,0:T(8,128)(2,1)}, u32[]{:S(2)}, u32[]{:S(2)}) collective-permute-start(bf16[2,24,6144]{2,1,0:T(8,128)(2,1)} %get-tuple-element.23), channel_id=1, source_target_pairs={{0,2},{2,0},{4,6},{6,4},{8,10},{10,8},{12,14},{14,12},{1,3},{3,1},... | collective-permute-start | bytes 1769480 | tf_op jit(solution)/shard_map/ppermute | solution.py:20
  71.6 1.7 dynamic-slice_bitcast_fusion.1
  73.3 5.9 %collective-permute-start.11 = (bf16[24,6144]{1,0:T(8,128)(2,1)}, bf16[24,6144]{1,0:T(8,128)(2,1)S(1)}, u32[]{:S(2)}, u32[]{:S(2)}) collective-permute-start(bf16[24,6144]{1,0:T(8,128)(2,1)} %dynamic-slice_bitcast_fusion.1), channel_id=1, source_target_pairs={{0,1},{1,0},{2,3},{3,2},{4,5},{5,4},{6,7},{7,6},{8,9},{9,8},{10,11... | collective-permute-start | bytes 884744 | tf_op jit(solution)/shard_map/ppermute | solution.py:20
  79.3 13.5 %all-to-all-start = ((bf16[32,96,256]{2,1,0:T(8,128)(2,1)}), bf16[32,96,256]{2,1,0:T(8,128)(2,1)}, u32[]{:S(2)}, u32[]{:S(2)}) async-start(bf16[32,96,256]{2,1,0:T(8,128)(2,1)} %fusion.9), calls=%async_computation | async-start | bytes 3145728 | tf_op jit(solution)/shard_map/all_to_all | solution.py:47
  92.8 1.9 %convert_add_fusion.1 = (bf16[2,24,6144]{2,1,0:T(8,128)(2,1)S(1)}, bf16[2,24,6144]{2,1,0:T(8,128)(2,1)S(1)}) fusion(bf16[2,24,6144]{2,1,0:T(8,128)(2,1)} %collective-permute-done.6, bf16[8,2,24,6144]{3,2,1,0:T(8,128)(2,1)} %bitcast.51, s32[]{:T(128)S(6)} %select_n.137, bf16[2,24,6144]{2,1,0:T(8,128)(2,1)} %collective-permute-done.5, s32[]{:T(128)S(6)} %select_n.120), kind=kLoop, calls=%fused_computation.17 | loop fusion | flops 2359296 | bytes 3538952 | tf_op jit(solution)/shard_map/add | solution.py:104
  95.8 2.4 %collective-permute-start.10 = (bf16[24,6144]{1,0:T(8,128)(2,1)}, bf16[24,6144]{1,0:T(8,128)(2,1)}, u32[]{:S(2)}, u32[]{:S(2)}) collective-permute-start(bf16[24,6144]{1,0:T(8,128)(2,1)} %get-tuple-element.27), channel_id=1, source_target_pairs={{0,14},{2,4},{4,2},{6,8},{8,6},{10,12},{12,10},{14,0},{1,15},{3,5}... | collective-permute-start | bytes 884744 | tf_op jit(solution)/shard_map/ppermute | solution.py:29
  98.2 2.8 %collective-permute-start.7 = (bf16[24,6144]{1,0:T(8,128)(2,1)}, bf16[24,6144]{1,0:T(8,128)(2,1)}, u32[]{:S(2)}, u32[]{:S(2)}) collective-permute-start(bf16[24,6144]{1,0:T(8,128)(2,1)} %get-tuple-element.24), channel_id=1, source_target_pairs={{0,3},{1,2},{2,1},{3,0},{4,7},{5,6},{6,5},{7,4},{8,11},{9,10},{10,... | collective-permute-start | bytes 884744 | tf_op jit(solution)/shard_map/ppermute | solution.py:65
  101.1 8.1 %collective-permute-start.8 = (bf16[24,6144]{1,0:T(8,128)(2,1)}, bf16[24,6144]{1,0:T(8,128)(2,1)}, u32[]{:S(2)}, u32[]{:S(2)}) collective-permute-start(bf16[24,6144]{1,0:T(8,128)(2,1)} %get-tuple-element.25), channel_id=1, source_target_pairs={{0,15},{1,14},{2,5},{3,4},{4,3},{5,2},{6,9},{7,8},{8,7},{9,6},{10,... | collective-permute-start | bytes 884744 | tf_op jit(solution)/shard_map/ppermute | solution.py:65
  109.2 2.1 %collective-permute-start.9 = (bf16[24,6144]{1,0:T(8,128)(2,1)}, bf16[24,6144]{1,0:T(8,128)(2,1)}, u32[]{:S(2)}, u32[]{:S(2)}) collective-permute-start(bf16[24,6144]{1,0:T(8,128)(2,1)} %get-tuple-element.26), channel_id=1, source_target_pairs={{0,2},{2,0},{4,6},{6,4},{8,10},{10,8},{12,14},{14,12},{1,3},{3,1},... | collective-permute-start | bytes 884744 | tf_op jit(solution)/shard_map/ppermute | solution.py:20
  111.5 55.2 %collective-permute-done.7 = bf16[24,6144]{1,0:T(8,128)(2,1)} collective-permute-done((bf16[24,6144]{1,0:T(8,128)(2,1)}, bf16[24,6144]{1,0:T(8,128)(2,1)}, u32[]{:S(2)}, u32[]{:S(2)}) %collective-permute-start.7) | collective-permute-done | bytes 294944 | tf_op jit(solution)/shard_map/ppermute | solution.py:65
  166.7 1.9 %fusion.25 = (f32[24]{0:T(128)S(1)}, f32[24]{0:T(128)S(1)}, f32[24,6144]{1,0:T(8,128)S(1)}) fusion(f32[24]{0:T(128)S(1)} %dynamic-slice.10, f32[24]{0:T(128)S(1)} %dynamic-slice.11, bf16[384,6144]{1,0:T(8,128)(2,1)} %param.5, s32[]{:T(128)S(6)} %select_n.110, f32[6144]{0:T(1024)S(1)} %copy-done.5, bf16[24,6144]{1,0:T(8,128)(2,1)S(1)} %collective-permute-done.11, ...), kind=kLoop, calls=%fused_computation.56 | loop fusion | flops 2654160 | bytes 2679180 | tf_op jit(solution)/shard_map/reduce_sum | solution.py:142
  168.6 2.0 %add_convert_fusion = bf16[24,6144]{1,0:T(8,128)(2,1)} fusion(f32[24,6144]{1,0:T(8,128)S(1)} %get-tuple-element.30, bf16[24,6144]{1,0:T(8,128)(2,1)} %param.9, f32[24]{0:T(128)S(1)} %broadcast_multiply_fusion.2, f32[24]{0:T(128)S(1)} %dynamic-slice.11, f32[24]{0:T(128)S(1)} %broadcast_multiply_fusion.3, f32[24]{0:T(128)S(1)} %dynamic-slice.10, ...), kind=kLoop, calls=%fused_computation.33 | loop fusion | flops 1474560 | bytes 1474948 | tf_op jit(solution)/shard_map/convert_element_type | solution.py:147
  170.6 1.6 convert_reduce_fusion.1
  (31 shorter events, 3.8 us)
Async XLA Ops:
  0.6 1.9 %copy-start = (bf16[6144,256]{1,0:T(8,128)(2,1)S(1)}, bf16[6144,256]{1,0:T(8,128)(2,1)}, u32[]{:S(2)}) copy-start(bf16[6144,256]{1,0:T(8,128)(2,1)} %param.7) | copy-start | bytes 9437188
  7.0 16.5 %collective-permute-start = (bf16[24,6144]{1,0:T(8,128)(2,1)}, bf16[24,6144]{1,0:T(8,128)(2,1)}, u32[]{:S(2)}, u32[]{:S(2)}) collective-permute-start(bf16[24,6144]{1,0:T(8,128)(2,1)} %get-tuple-element.42), channel_id=1, source_target_pairs={{0,14},{2,4},{4,2},{6,8},{8,6},{10,12},{12,10},{14,0},{1,15},{3,5}... | collective-permute-start | bytes 884744 | tf_op jit(solution)/shard_map/ppermute | solution.py:29
  9.4 14.1 %collective-permute-start.1 = (bf16[24,6144]{1,0:T(8,128)(2,1)}, bf16[24,6144]{1,0:T(8,128)(2,1)}, u32[]{:S(2)}, u32[]{:S(2)}) collective-permute-start(bf16[24,6144]{1,0:T(8,128)(2,1)} %get-tuple-element.41), channel_id=1, source_target_pairs={{0,2},{2,0},{4,6},{6,4},{8,10},{10,8},{12,14},{14,12},{1,3},{3,1},... | collective-permute-start | bytes 884744 | tf_op jit(solution)/shard_map/ppermute | solution.py:20
  12.1 3.8 %copy-start.2 = (bf16[384,6144]{1,0:T(8,128)(2,1)S(1)}, bf16[384,6144]{1,0:T(8,128)(2,1)}, u32[]{:S(2)}) copy-start(bf16[384,6144]{1,0:T(8,128)(2,1)} %param.5) | copy-start | bytes 14155780
  15.3 1.9 %copy-start.4 = (bf16[384,256]{1,0:T(8,128)(2,1)S(1)}, bf16[384,256]{1,0:T(8,128)(2,1)}, u32[]{:S(2)}) copy-start(bf16[384,256]{1,0:T(8,128)(2,1)} %param.8) | copy-start | bytes 589828
  15.3 1.9 %copy-start.5 = (f32[6144]{0:T(1024)S(1)}, f32[6144]{0:T(1024)}, u32[]{:S(2)}) copy-start(f32[6144]{0:T(1024)} %param.6) | copy-start | bytes 73732
  22.0 6.0 %copy-start.3 = (bf16[6144,256]{1,0:T(8,128)(2,1)}, bf16[6144,256]{1,0:T(8,128)(2,1)S(1)}, u32[]{:S(2)}) copy-start(bf16[6144,256]{1,0:T(8,128)(2,1)S(1)} %convolution_convert_fusion.1) | copy-start | bytes 9437188
  23.5 2.1 %copy-start.1 = (bf16[384,6144]{1,0:T(8,128)(2,1)}, bf16[384,6144]{1,0:T(8,128)(2,1)S(1)}, u32[]{:S(2)}) copy-start(bf16[384,6144]{1,0:T(8,128)(2,1)S(1)} %convolution_convert_fusion) | copy-start | bytes 14155780
  29.4 9.9 %collective-permute-start.4 = (bf16[32,96,256]{2,1,0:T(8,128)(2,1)}, bf16[32,96,256]{2,1,0:T(8,128)(2,1)}, u32[]{:S(2)}, u32[]{:S(2)}) collective-permute-start(bf16[32,96,256]{2,1,0:T(8,128)(2,1)} %dynamic-slice_bitcast_fusion), channel_id=1, source_target_pairs={{0,16},{16,0},{1,17},{17,1},{2,18},{18,2},{3,19},{19,3},{4,20},{20... | collective-permute-start | bytes 4718600 | tf_op jit(solution)/shard_map/ppermute | solution.py:20
  31.4 17.9 %collective-permute-start.2 = (bf16[2,24,6144]{2,1,0:T(8,128)(2,1)}, bf16[2,24,6144]{2,1,0:T(8,128)(2,1)}, u32[]{:S(2)}, u32[]{:S(2)}) collective-permute-start(bf16[2,24,6144]{2,1,0:T(8,128)(2,1)} %get-tuple-element.17), channel_id=1, source_target_pairs={{0,2},{2,0},{4,6},{6,4},{8,10},{10,8},{12,14},{14,12},{1,3},{3,1},... | collective-permute-start | bytes 1769480 | tf_op jit(solution)/shard_map/ppermute | solution.py:20
  34.6 18.9 %collective-permute-start.3 = (bf16[2,24,6144]{2,1,0:T(8,128)(2,1)}, bf16[2,24,6144]{2,1,0:T(8,128)(2,1)}, u32[]{:S(2)}, u32[]{:S(2)}) collective-permute-start(bf16[2,24,6144]{2,1,0:T(8,128)(2,1)} %get-tuple-element.18), channel_id=1, source_target_pairs={{0,14},{2,4},{4,2},{6,8},{8,6},{10,12},{12,10},{14,0},{1,15},{3,5}... | collective-permute-start | bytes 1769480 | tf_op jit(solution)/shard_map/ppermute | solution.py:29
  56.4 36.4 %collective-permute-start.5 = (bf16[2,24,6144]{2,1,0:T(8,128)(2,1)}, bf16[2,24,6144]{2,1,0:T(8,128)(2,1)}, u32[]{:S(2)}, u32[]{:S(2)}) collective-permute-start(bf16[2,24,6144]{2,1,0:T(8,128)(2,1)} %get-tuple-element.22), channel_id=1, source_target_pairs={{0,14},{2,4},{4,2},{6,8},{8,6},{10,12},{12,10},{14,0},{1,15},{3,5}... | collective-permute-start | bytes 1769480 | tf_op jit(solution)/shard_map/ppermute | solution.py:29
  61.1 31.8 %collective-permute-start.6 = (bf16[2,24,6144]{2,1,0:T(8,128)(2,1)}, bf16[2,24,6144]{2,1,0:T(8,128)(2,1)}, u32[]{:S(2)}, u32[]{:S(2)}) collective-permute-start(bf16[2,24,6144]{2,1,0:T(8,128)(2,1)} %get-tuple-element.23), channel_id=1, source_target_pairs={{0,2},{2,0},{4,6},{6,4},{8,10},{10,8},{12,14},{14,12},{1,3},{3,1},... | collective-permute-start | bytes 1769480 | tf_op jit(solution)/shard_map/ppermute | solution.py:20
  73.3 38.2 %collective-permute-start.11 = (bf16[24,6144]{1,0:T(8,128)(2,1)}, bf16[24,6144]{1,0:T(8,128)(2,1)S(1)}, u32[]{:S(2)}, u32[]{:S(2)}) collective-permute-start(bf16[24,6144]{1,0:T(8,128)(2,1)} %dynamic-slice_bitcast_fusion.1), channel_id=1, source_target_pairs={{0,1},{1,0},{2,3},{3,2},{4,5},{5,4},{6,7},{7,6},{8,9},{9,8},{10,11... | collective-permute-start | bytes 884744 | tf_op jit(solution)/shard_map/ppermute | solution.py:20
  79.3 91.3 %all-to-all-start = ((bf16[32,96,256]{2,1,0:T(8,128)(2,1)}), bf16[32,96,256]{2,1,0:T(8,128)(2,1)}, u32[]{:S(2)}, u32[]{:S(2)}) async-start(bf16[32,96,256]{2,1,0:T(8,128)(2,1)} %fusion.9), calls=%async_computation | async-start | bytes 3145728 | tf_op jit(solution)/shard_map/all_to_all | solution.py:47
  95.8 15.8 %collective-permute-start.10 = (bf16[24,6144]{1,0:T(8,128)(2,1)}, bf16[24,6144]{1,0:T(8,128)(2,1)}, u32[]{:S(2)}, u32[]{:S(2)}) collective-permute-start(bf16[24,6144]{1,0:T(8,128)(2,1)} %get-tuple-element.27), channel_id=1, source_target_pairs={{0,14},{2,4},{4,2},{6,8},{8,6},{10,12},{12,10},{14,0},{1,15},{3,5}... | collective-permute-start | bytes 884744 | tf_op jit(solution)/shard_map/ppermute | solution.py:29
  98.2 68.5 %collective-permute-start.7 = (bf16[24,6144]{1,0:T(8,128)(2,1)}, bf16[24,6144]{1,0:T(8,128)(2,1)}, u32[]{:S(2)}, u32[]{:S(2)}) collective-permute-start(bf16[24,6144]{1,0:T(8,128)(2,1)} %get-tuple-element.24), channel_id=1, source_target_pairs={{0,3},{1,2},{2,1},{3,0},{4,7},{5,6},{6,5},{7,4},{8,11},{9,10},{10,... | collective-permute-start | bytes 884744 | tf_op jit(solution)/shard_map/ppermute | solution.py:65
  101.1 65.6 %collective-permute-start.8 = (bf16[24,6144]{1,0:T(8,128)(2,1)}, bf16[24,6144]{1,0:T(8,128)(2,1)}, u32[]{:S(2)}, u32[]{:S(2)}) collective-permute-start(bf16[24,6144]{1,0:T(8,128)(2,1)} %get-tuple-element.25), channel_id=1, source_target_pairs={{0,15},{1,14},{2,5},{3,4},{4,3},{5,2},{6,9},{7,8},{8,7},{9,6},{10,... | collective-permute-start | bytes 884744 | tf_op jit(solution)/shard_map/ppermute | solution.py:65
  109.2 57.5 %collective-permute-start.9 = (bf16[24,6144]{1,0:T(8,128)(2,1)}, bf16[24,6144]{1,0:T(8,128)(2,1)}, u32[]{:S(2)}, u32[]{:S(2)}) collective-permute-start(bf16[24,6144]{1,0:T(8,128)(2,1)} %get-tuple-element.26), channel_id=1, source_target_pairs={{0,2},{2,0},{4,6},{6,4},{8,10},{10,8},{12,14},{14,12},{1,3},{3,1},... | collective-permute-start | bytes 884744 | tf_op jit(solution)/shard_map/ppermute | solution.py:20

commit v5 on v3

v5 whole, which is shorter than its diff:
```python
import jax
import jax.numpy as jnp
from jax import lax
from jax.experimental import pallas as pl
from jax.experimental.pallas import tpu as pltpu
from jax.sharding import Mesh, PartitionSpec as P

DP = ("y", "z_lo", "core")
TENSOR = ("x", "z_hi")
SPLIT = (8, 4, 2, 8, 2)


def shifted(part, axis, step):
    size = lax.axis_size(axis)
    return lax.ppermute(part, axis, [(i, (i + step) % size) for i in range(size)])


def weight_reduce(term):
    replicas, cores = lax.axis_size(DP), lax.axis_size("core")
    rows, columns = term.shape[0] // replicas, term.shape[1]
    blocks = term.astype(jnp.bfloat16).reshape(replicas // cores, cores, rows, columns)
    me = lax.axis_index("core")
    own = lax.dynamic_index_in_dim(blocks, me, 1, False)
    other = lax.dynamic_index_in_dim(blocks, 1 - me, 1, False)
    pair = own.astype(jnp.float32) + shifted(other, "core", 1).astype(jnp.float32)
    parts = lax.all_to_all(pair.astype(jnp.bfloat16), ("y", "z_lo"), 0, 0, tiled=True)
    return jnp.sum(parts.astype(jnp.float32), axis=0) / replicas


def product_kernel(grads_ref, weights_ref, out_ref):
    out_ref[...] = lax.dot_general(
        grads_ref[...],
        weights_ref[...],
        (((1,), (1,)), ((), ())),
        preferred_element_type=jnp.float32,
    ).astype(out_ref.dtype)


def product(query_grad, w_query):
    rows, depth = query_grad.shape
    features = w_query.shape[0]
    block = features // 6
    return pl.pallas_call(
        product_kernel,
        grid=(features // block,),
        in_specs=[
            pl.BlockSpec((rows, depth), lambda i: (0, 0)),
            pl.BlockSpec((block, depth), lambda i: (i, 0)),
        ],
        out_specs=pl.BlockSpec((rows, block), lambda i: (0, i)),
        out_shape=jax.ShapeDtypeStruct((rows, features), jnp.bfloat16),
        compiler_params=pltpu.CompilerParams(vmem_limit_bytes=60 << 20),
        cost_estimate=pl.CostEstimate(
            flops=2 * rows * depth * features,
            bytes_accessed=2 * (rows * depth + features * depth + rows * features),
            transcendentals=0,
        ),
    )(query_grad, w_query)


def finish_kernel(
    place_ref, sums_ref, arrived_ref, inputs_ref, skip_ref, gain_ref, out_ref
):
    del place_ref
    values = inputs_ref[0].astype(jnp.float32)
    center = values - jnp.mean(values, axis=1, keepdims=True)
    inverse = lax.rsqrt(jnp.mean(center * center, axis=1, keepdims=True) + 1e-06)
    normed = center * inverse
    summed = sums_ref[0].astype(jnp.float32) + arrived_ref[...].astype(jnp.float32)
    gated = summed * gain_ref[...]
    mean_g = jnp.mean(gated, axis=1, keepdims=True)
    mean_gn = jnp.mean(gated * normed, axis=1, keepdims=True)
    grad = skip_ref[...].astype(jnp.float32) + inverse * (gated - mean_g - normed * mean_gn)
    out_ref[...] = grad.astype(out_ref.dtype)


def finish(sums, arrived, inputs, skip_grad, ln_gain):
    rows, features = skip_grad.shape
    place = jnp.stack([lax.axis_index("z_hi"), lax.axis_index(TENSOR)]).astype(jnp.int32)
    whole = pl.BlockSpec((rows, features), lambda i, place: (0, 0))
    return pl.pallas_call(
        finish_kernel,
        grid_spec=pltpu.PrefetchScalarGridSpec(
            num_scalar_prefetch=1,
            grid=(1,),
            in_specs=[
                pl.BlockSpec((1, rows, features), lambda i, place: (place[0], 0, 0)),
                whole,
                pl.BlockSpec((1, rows, features), lambda i, place: (place[1], 0, 0)),
                whole,
                pl.BlockSpec((1, features), lambda i, place: (0, 0)),
            ],
            out_specs=whole,
        ),
        out_shape=jax.ShapeDtypeStruct(skip_grad.shape, jnp.bfloat16),
        compiler_params=pltpu.CompilerParams(vmem_limit_bytes=60 << 20),
    )(
        place,
        sums,
        arrived,
        inputs.reshape(-1, rows, features),
        skip_grad,
        ln_gain.reshape(1, features),
    )


def per_device(inputs, ln_gain, w_query, query_grad, skip_grad):
    term = product(query_grad, w_query)
    across = lax.psum_scatter(term, "x", scatter_dimension=0, tiled=True)
    sums = across.reshape(2, across.shape[0] // 2, across.shape[1])
    other = lax.dynamic_index_in_dim(sums, 1 - lax.axis_index("z_hi"), 0, False)
    arrived = shifted(other, "z_hi", 1)

    values = inputs.astype(jnp.float32)
    center = values - jnp.mean(values, axis=1, keepdims=True)
    inverse = lax.rsqrt(jnp.mean(center * center, axis=1, keepdims=True) + 1e-06)
    scaled = (center * inverse * ln_gain[None, :]).astype(jnp.bfloat16)
    weight_grad = weight_reduce(
        lax.dot_general(
            scaled, query_grad, (((0,), (0,)), ((), ())), preferred_element_type=jnp.float32
        )
    )
    input_grad = finish(sums, arrived, inputs, skip_grad, ln_gain)
    return (input_grad, weight_grad)


def solution(mesh):
    fine = Mesh(mesh.devices.reshape(SPLIT), DP + TENSOR)
    placed = (P(DP, None), P(), P(None, TENSOR), P(DP, TENSOR), P(DP + TENSOR, None))
    return jax.shard_map(
        per_device,
        mesh=fine,
        in_specs=placed,
        out_specs=(P(DP + TENSOR, None), P(DP, TENSOR)),
        check_vma=False,
    )
```

time: 122 us -> 122 us (level)
  Pallas kernels: 0 us -> 9.88 us
  matrix products: 7.21 us -> 2.47 us
  local copies, waits for them, and re-layouts: 7.25 us -> 3.5 us
  other arithmetic: 14 us -> 11.6 us
  waiting for transfers between devices: 53.4 us -> 55.2 us
    pallas_call x0 -> x2, Pallas kernels: none -> 9.88 us  [the longest x1 6.61 us: product(): pl.pallas_call(product_kernel, grid=(features // block,), in_specs=[pl.Bl...]
    dot_general x1 -> x0, matrix products: 4.48 us -> none  [feature_reduce(): lax.dot_general(query_grad, w_query, (((1,), (1,)), ((), ())), preferred_...]
    reduce_sum x1, other arithmetic: 1.37 us -> 3.71 us  [per_device(): jnp.mean(center * center, axis=1, keepdims=True) + 1e-06]
    convert_element_type x1 -> x0, other arithmetic: 2.15 us -> none  [per_device(): return (input_grad.astype(jnp.bfloat16), weight_grad)]
    unnamed x10 -> x12, local copies, waits for them, and re-layouts: 4.04 us -> 2.39 us
    reduce_sum x1, other arithmetic: 1.64 us -> 0.22 us  [weight_reduce(): return jnp.sum(parts.astype(jnp.float32), axis=0) / replicas]
    reduce_sum x2 -> x1, other arithmetic: 4.56 us -> 3.19 us  [per_device(): center = values - jnp.mean(values, axis=1, keepdims=True)]
    squeeze x1, local copies, waits for them, and re-layouts: 1.37 us -> 0.13 us  [weight_reduce(): other = lax.dynamic_index_in_dim(blocks, 1 - me, 1, False)]
  transfers between devices with their start and end apart: 4 -> 4, of which waited for: 3 -> 3; matrix products, arithmetic and copies ran while one was open for 14% -> 12% of each run, Pallas kernels for 0% -> 0%
where the time goes in v5:
time: 122 us
  waiting for transfers between devices  55.2 us (45%)
  starting transfers between devices  24.8 us (20%)
  between operations  14.2 us (12%)
  other arithmetic  11.6 us (10%)
  Pallas kernels  9.88 us (8%)
  local copies, waits for them, and re-layouts  3.5 us (3%)
  matrix products  2.47 us (2%)
    reduce_scatter x1, waiting for transfers between devices, per_device(): across = lax.psum_scatter(term, 'x', scatter_dimension=0, tiled=True)  39.6 us
    ppermute x2, waiting for transfers between devices, shifted(): lax.ppermute(part, axis, [(i, (i + step) % size) for i in range(size)])  15.6 us
    all_to_all x1, starting transfers between devices, weight_reduce(): lax.all_to_all(pair.astype(jnp.bfloat16), ('y', 'z_lo'), 0, 0, tiled=True)  15.1 us
    ppermute x2, starting transfers between devices, shifted(): lax.ppermute(part, axis, [(i, (i + step) % size) for i in range(size)])  9.75 us
    pallas_call x1, Pallas kernels, product(): pl.pallas_call(product_kernel, grid=(features // block,), in_specs=[pl.Bl...  6.61 us
    reduce_sum x1, other arithmetic, per_device(): jnp.mean(center * center, axis=1, keepdims=True) + 1e-06  3.71 us
    pallas_call x1, Pallas kernels, finish(): pl.pallas_call(finish_kernel, grid_spec=pltpu.PrefetchScalarGridSpec(num_...  3.27 us
    reduce_sum x1, other arithmetic, per_device(): center = values - jnp.mean(values, axis=1, keepdims=True)  3.19 us
  transfers between devices with their start and end apart: 4, of which 3 were waited for; matrix products, arithmetic and copies ran while one was open for 12% of the time, Pallas kernels for 0%

profile of v5, /device:TPU:128, one launch (start us, length us, event | category | flops | bytes accessed | tf_op | source)
XLA Modules:
  0.0 121.7 jit_solution(13660291465248527707)
XLA Ops:
  7.2 0.0 reduce-scatter.2.cloned.1.call-start
  7.2 6.6 %shard_map.68 = bf16[384,6144]{1,0:T(8,128)(2,1)} custom-call(bf16[384,256]{1,0:T(8,128)(2,1)} %grads_ref.1, bf16[6144,256]{1,0:T(8,128)(2,1)} %weights_ref.1), custom_call_target="tpu_custom_call" | custom-call | flops 1207959552 | bytes 8060928 | tf_op jit(solution)/shard_map/pallas_call | solution.py:43
  13.8 0.0 slice-start
  13.8 0.0 reduce-scatter.2.cloned.1.call-update
  13.8 0.0 slice-start.1
  13.9 0.0 copy-start.2
  13.9 0.0 copy-start.3
  13.9 3.2 %convert_reduce_fusion = f32[384]{0:T(512)S(1)} fusion(bf16[384,6144]{1,0:T(8,128)(2,1)} %param.5), kind=kLoop, calls=%fused_computation.1 | loop fusion | flops 4718208 | bytes 4720128 | tf_op jit(solution)/shard_map/reduce_sum | solution.py:115
  17.1 3.7 %fusion.2 = f32[384]{0:T(512)S(1)} fusion(bf16[384,6144]{1,0:T(8,128)(2,1)} %param.5, f32[384]{0:T(512)S(1)} %broadcast_multiply_fusion.1), kind=kLoop, calls=%fused_computation.4 | loop fusion | flops 9436800 | bytes 4721664 | tf_op jit(solution)/shard_map/reduce_sum | solution.py:116
  20.8 0.0 slice-done
  20.8 0.0 slice-done.1
  20.8 0.0 copy-done.2
  20.8 0.0 copy-done.3
  20.9 2.5 %convolution_convert_fusion = bf16[6144,256]{1,0:T(8,128)(2,1)S(1)} fusion(bf16[384,256]{1,0:T(8,128)(2,1)S(1)} %copy-done.2, bf16[384,6144]{1,0:T(8,128)(2,1)S(1)} %bitcast.16, f32[6144]{0:T(1024)S(1)} %copy-done.3, f32[384]{0:T(512)S(1)} %add_rsqrt_fusion, f32[384]{0:T(512)S(1)} %broadcast_multiply_fusion.1), kind=kOutput, calls=%fused_computation.7 | convolution fusion | flops 1221328896 | bytes 8088576 | tf_op jit(solution)/shard_map/dot_general | solution.py:119
  23.3 0.0 copy-start
  23.3 1.7 %copy-done = bf16[6144,256]{1,0:T(8,128)(2,1)} copy-done((bf16[6144,256]{1,0:T(8,128)(2,1)}, bf16[6144,256]{1,0:T(8,128)(2,1)S(1)}, u32[]{:S(2)}) %copy-start) | copy-done | bytes 3145752
  25.0 0.1 dynamic-slice_bitcast_fusion
  25.1 1.9 %collective-permute-start.1 = (bf16[32,96,256]{2,1,0:T(8,128)(2,1)S(1)}, bf16[32,96,256]{2,1,0:T(8,128)(2,1)S(1)}, u32[]{:S(2)}, u32[]{:S(2)}) collective-permute-start(bf16[32,96,256]{2,1,0:T(8,128)(2,1)S(1)} %dynamic-slice_bitcast_fusion), channel_id=1, source_target_pairs={{0,16},{16,0},{1,17},{17,1},{2,18},{18,2},{3,19},{19,3},{4,20},{20... | collective-permute-start | bytes 4718600 | tf_op jit(solution)/shard_map/ppermute | solution.py:15
  27.1 3.4 %collective-permute-done.1 = bf16[32,96,256]{2,1,0:T(8,128)(2,1)S(1)} collective-permute-done((bf16[32,96,256]{2,1,0:T(8,128)(2,1)S(1)}, bf16[32,96,256]{2,1,0:T(8,128)(2,1)S(1)}, u32[]{:S(2)}, u32[]{:S(2)}) %collective-permute-start.1) | collective-permute-done | bytes 1572896 | tf_op jit(solution)/shard_map/ppermute | solution.py:15
  30.4 3.2 %fusion.9 = bf16[32,96,256]{2,1,0:T(8,128)(2,1)} fusion(bf16[32,96,256]{2,1,0:T(8,128)(2,1)S(1)} %collective-permute-done.1, bf16[32,2,96,256]{3,2,1,0:T(8,128)(2,1)} %bitcast.18, s32[]{:T(128)S(6)} %select_n.12), kind=kLoop, calls=%fused_computation.12 | loop fusion | flops 3145728 | bytes 4718596 | tf_op jit(solution)/shard_map/convert_element_type | solution.py:26
  33.6 15.1 %all-to-all-start = ((bf16[32,96,256]{2,1,0:T(8,128)(2,1)}), bf16[32,96,256]{2,1,0:T(8,128)(2,1)S(1)}, u32[]{:S(2)}, u32[]{:S(2)}) async-start(bf16[32,96,256]{2,1,0:T(8,128)(2,1)} %fusion.9), calls=%async_computation.1 | async-start | bytes 3145728 | tf_op jit(solution)/shard_map/all_to_all | solution.py:26
  48.7 0.6 pad_add_fusion.place_ref
  49.3 39.6 %reduce-scatter.2.cloned.1.call-done = bf16[48,6144]{1,0:T(8,128)(2,1)} async-done(((bf16[384,6144]{1,0:T(8,128)(2,1)}), bf16[48,6144]{1,0:T(8,128)(2,1)}) %reduce-scatter.2.cloned.1.call-update) | async-done | bytes 589840 | tf_op jit(solution)/shard_map/reduce_scatter | solution.py:109
  89.0 1.0 dynamic-slice_bitcast_fusion.1
  89.9 7.8 %collective-permute-start = (bf16[24,6144]{1,0:T(8,128)(2,1)S(1)}, bf16[24,6144]{1,0:T(8,128)(2,1)S(1)}, u32[]{:S(2)}, u32[]{:S(2)}) collective-permute-start(bf16[24,6144]{1,0:T(8,128)(2,1)S(1)} %dynamic-slice_bitcast_fusion.1), channel_id=1, source_target_pairs={{0,1},{1,0},{2,3},{3,2},{4,5},{5,4},{6,7},{7,6},{8,9},{9,8},{10,11... | collective-permute-start | bytes 884744 | tf_op jit(solution)/shard_map/ppermute | solution.py:15
  97.8 0.0 all-to-all-done
  97.8 0.2 convert_reduce_fusion.1
  98.0 0.6 broadcast_multiply_fusion
  98.7 12.2 %collective-permute-done.arrived_ref = bf16[24,6144]{1,0:T(8,128)(2,1)S(1)} collective-permute-done((bf16[24,6144]{1,0:T(8,128)(2,1)S(1)}, bf16[24,6144]{1,0:T(8,128)(2,1)S(1)}, u32[]{:S(2)}, u32[]{:S(2)}) %collective-permute-start) | collective-permute-done | bytes 294944 | tf_op jit(solution)/shard_map/ppermute | solution.py:15
  110.9 0.0 copy-start.1
  110.9 0.7 copy-done.1
  111.6 3.3 %shard_map.69 = bf16[24,6144]{1,0:T(8,128)(2,1)} custom-call(s32[2]{0:T(128)} %pad_add_fusion.place_ref, bf16[2,24,6144]{2,1,0:T(8,128)(2,1)} %bitcast.20, bf16[24,6144]{1,0:T(8,128)(2,1)} %copy-done.1, bf16[16,24,6144]{2,1,0:T(8,128)(2,1)} %bitcast.14, bf16[24,6144]{1,0:T(8,128)(2,1)} %skip_ref.1, f32[1,6144]{1,0:T(1,128)} %bitcast.21), custom_call_target="tpu_custom_call" | custom-call | tf_op jit(solution)/shard_map/pallas_call | solution.py:81
  (3 shorter events, 0.0 us)
Async XLA Ops:
  7.2 81.8 %reduce-scatter.2.cloned.1.call-start = ((), (), s32[]{:S(2)}) async-start(), calls=%async_computation.2 | async-start | bytes 5308416 | tf_op jit(solution)/shard_map/reduce_scatter | solution.py:109
  13.8 7.0 %slice-start = ((s8[4718592]{0:T(1024)(128)(4,1)}), s8[524288]{0:T(1024)(128)(4,1)S(1)}, s32[]{:S(2)}) async-start(s8[4718592]{0:T(1024)(128)(4,1)} %bitcast.15), calls=%async_computation.3 | async-start | bytes 1048576
  13.8 7.0 %slice-start.1 = ((s8[4718592]{0:T(1024)(128)(4,1)}), s8[4194304]{0:T(1024)(128)(4,1)S(1)}, s32[]{:S(2)}) async-start(s8[4718592]{0:T(1024)(128)(4,1)} %bitcast.15), calls=%async_computation.4 | async-start | bytes 8388608
  13.9 7.0 %copy-start.2 = (bf16[384,256]{1,0:T(8,128)(2,1)S(1)}, bf16[384,256]{1,0:T(8,128)(2,1)}, u32[]{:S(2)}) copy-start(bf16[384,256]{1,0:T(8,128)(2,1)} %grads_ref.1) | copy-start | bytes 589828
  13.9 7.0 %copy-start.3 = (f32[6144]{0:T(1024)S(1)}, f32[6144]{0:T(1024)}, u32[]{:S(2)}) copy-start(f32[6144]{0:T(1024)} %param.6) | copy-start | bytes 73732
  23.3 1.7 %copy-start = (bf16[6144,256]{1,0:T(8,128)(2,1)}, bf16[6144,256]{1,0:T(8,128)(2,1)S(1)}, u32[]{:S(2)}) copy-start(bf16[6144,256]{1,0:T(8,128)(2,1)S(1)} %convolution_convert_fusion) | copy-start | bytes 9437188
  25.1 5.3 %collective-permute-start.1 = (bf16[32,96,256]{2,1,0:T(8,128)(2,1)S(1)}, bf16[32,96,256]{2,1,0:T(8,128)(2,1)S(1)}, u32[]{:S(2)}, u32[]{:S(2)}) collective-permute-start(bf16[32,96,256]{2,1,0:T(8,128)(2,1)S(1)} %dynamic-slice_bitcast_fusion), channel_id=1, source_target_pairs={{0,16},{16,0},{1,17},{17,1},{2,18},{18,2},{3,19},{19,3},{4,20},{20... | collective-permute-start | bytes 4718600 | tf_op jit(solution)/shard_map/ppermute | solution.py:15
  33.6 64.2 %all-to-all-start = ((bf16[32,96,256]{2,1,0:T(8,128)(2,1)}), bf16[32,96,256]{2,1,0:T(8,128)(2,1)S(1)}, u32[]{:S(2)}, u32[]{:S(2)}) async-start(bf16[32,96,256]{2,1,0:T(8,128)(2,1)} %fusion.9), calls=%async_computation.1 | async-start | bytes 3145728 | tf_op jit(solution)/shard_map/all_to_all | solution.py:26
  89.9 20.9 %collective-permute-start = (bf16[24,6144]{1,0:T(8,128)(2,1)S(1)}, bf16[24,6144]{1,0:T(8,128)(2,1)S(1)}, u32[]{:S(2)}, u32[]{:S(2)}) collective-permute-start(bf16[24,6144]{1,0:T(8,128)(2,1)S(1)} %dynamic-slice_bitcast_fusion.1), channel_id=1, source_target_pairs={{0,1},{1,0},{2,3},{3,2},{4,5},{5,4},{6,7},{7,6},{8,9},{9,8},{10,11... | collective-permute-start | bytes 884744 | tf_op jit(solution)/shard_map/ppermute | solution.py:15
  110.9 0.7 copy-start.1
Sparse Core Ops, SparseCore 0:
  14.0 74.9 reduce-scatter.1

commit v6 on v5

v6 whole, which is shorter than its diff:
```python
import jax
import jax.numpy as jnp
from jax import lax
from jax.experimental import pallas as pl
from jax.experimental.pallas import tpu as pltpu
from jax.sharding import Mesh, PartitionSpec as P

DP = ("y", "z_lo", "core")
TENSOR = ("x", "z_hi")
SPLIT = (8, 4, 2, 8, 2)


def shifted(part, axis, step):
    size = lax.axis_size(axis)
    return lax.ppermute(part, axis, [(i, (i + step) % size) for i in range(size)])


def core_sum(term):
    replicas, cores = lax.axis_size(DP), lax.axis_size("core")
    rows, columns = term.shape[0] // replicas, term.shape[1]
    blocks = term.astype(jnp.bfloat16).reshape(replicas // cores, cores, rows, columns)
    me = lax.axis_index("core")
    own = lax.dynamic_index_in_dim(blocks, me, 1, False)
    other = lax.dynamic_index_in_dim(blocks, 1 - me, 1, False)
    pair = own.astype(jnp.float32) + shifted(other, "core", 1).astype(jnp.float32)
    return pair.astype(jnp.bfloat16)


def weight_reduce(pair):
    parts = lax.all_to_all(pair, ("y", "z_lo"), 0, 0, tiled=True)
    return jnp.sum(parts.astype(jnp.float32), axis=0) / lax.axis_size(DP)


PIECES = 4
DIRECT = 1024


def product_kernel(grads_hbm, weights_hbm, out_hbm, grads, weights, out, took, loaded, stored):
    pieces, block = weights.shape[:2]
    first = pltpu.make_async_copy(grads_hbm, grads, took)
    first.start()
    loads = []
    for i in range(pieces):
        load = pltpu.make_async_copy(
            weights_hbm.at[pl.ds(i * block, block)], weights.at[i], loaded.at[i]
        )
        load.start()
        loads.append(load)
    first.wait()
    stores = []
    for i in range(pieces):
        loads[i].wait()
        out[i] = lax.dot_general(
            grads[...],
            weights[i],
            (((1,), (1,)), ((), ())),
            preferred_element_type=jnp.float32,
        ).astype(out.dtype)
        store = pltpu.make_async_copy(
            out.at[i], out_hbm.at[:, pl.ds(i * block, block)], stored.at[i]
        )
        store.start()
        stores.append(store)
    for store in stores:
        store.wait()


def product(query_grad, w_query, features):
    rows, depth = query_grad.shape
    block = features // PIECES
    return pl.pallas_call(
        product_kernel,
        in_specs=[pl.BlockSpec(memory_space=pl.ANY)] * 2,
        out_specs=pl.BlockSpec(memory_space=pl.ANY),
        out_shape=jax.ShapeDtypeStruct((rows, features), jnp.bfloat16),
        scratch_shapes=[
            pltpu.VMEM((rows, depth), jnp.bfloat16),
            pltpu.VMEM((PIECES, block, depth), jnp.bfloat16),
            pltpu.VMEM((PIECES, rows, block), jnp.bfloat16),
            pltpu.SemaphoreType.DMA,
            pltpu.SemaphoreType.DMA((PIECES,)),
            pltpu.SemaphoreType.DMA((PIECES,)),
        ],
        compiler_params=pltpu.CompilerParams(vmem_limit_bytes=60 << 20),
        cost_estimate=pl.CostEstimate(
            flops=2 * rows * depth * features,
            bytes_accessed=2 * (rows * depth + features * depth + rows * features),
            transcendentals=0,
        ),
    )(query_grad, w_query)


def finish_kernel(
    place_ref, sums_ref, arrived_ref, direct_ref, inputs_ref, skip_ref, gain_ref, out_ref
):
    del place_ref
    values = inputs_ref[0].astype(jnp.float32)
    center = values - jnp.mean(values, axis=1, keepdims=True)
    inverse = lax.rsqrt(jnp.mean(center * center, axis=1, keepdims=True) + 1e-06)
    normed = center * inverse
    summed = sums_ref[0].astype(jnp.float32) + arrived_ref[...].astype(jnp.float32)
    gated = jnp.concatenate([summed, direct_ref[...]], axis=1) * gain_ref[...]
    mean_g = jnp.mean(gated, axis=1, keepdims=True)
    mean_gn = jnp.mean(gated * normed, axis=1, keepdims=True)
    grad = skip_ref[...].astype(jnp.float32) + inverse * (gated - mean_g - normed * mean_gn)
    out_ref[...] = grad.astype(out_ref.dtype)


def finish(sums, arrived, direct, inputs, skip_grad, ln_gain):
    rows, features = skip_grad.shape
    ringed = sums.shape[2]
    place = jnp.stack([lax.axis_index("z_hi"), lax.axis_index(TENSOR)]).astype(jnp.int32)
    whole = pl.BlockSpec((rows, features), lambda i, place: (0, 0))
    return pl.pallas_call(
        finish_kernel,
        grid_spec=pltpu.PrefetchScalarGridSpec(
            num_scalar_prefetch=1,
            grid=(1,),
            in_specs=[
                pl.BlockSpec((1, rows, ringed), lambda i, place: (place[0], 0, 0)),
                pl.BlockSpec((rows, ringed), lambda i, place: (0, 0)),
                pl.BlockSpec((rows, features - ringed), lambda i, place: (0, 0)),
                pl.BlockSpec((1, rows, features), lambda i, place: (place[1], 0, 0)),
                whole,
                pl.BlockSpec((1, features), lambda i, place: (0, 0)),
            ],
            out_specs=whole,
        ),
        out_shape=jax.ShapeDtypeStruct(skip_grad.shape, jnp.bfloat16),
        compiler_params=pltpu.CompilerParams(vmem_limit_bytes=60 << 20),
    )(
        place,
        sums,
        arrived,
        direct,
        inputs.reshape(-1, rows, features),
        skip_grad,
        ln_gain.reshape(1, features),
    )


def per_device(inputs, ln_gain, w_query, query_grad, skip_grad):
    rows, features = skip_grad.shape
    ringed = features - DIRECT
    term = product(query_grad, w_query, ringed)
    across = lax.psum_scatter(term, "x", scatter_dimension=0, tiled=True)
    sums = across.reshape(2, rows, ringed)
    other = lax.dynamic_index_in_dim(sums, 1 - lax.axis_index("z_hi"), 0, False)
    arrived = shifted(other, "z_hi", 1)

    values = inputs.astype(jnp.float32)
    center = values - jnp.mean(values, axis=1, keepdims=True)
    inverse = lax.rsqrt(jnp.mean(center * center, axis=1, keepdims=True) + 1e-06)
    scaled = (center * inverse * ln_gain[None, :]).astype(jnp.bfloat16)
    pair = core_sum(
        lax.dot_general(
            scaled, query_grad, (((0,), (0,)), ((), ())), preferred_element_type=jnp.float32
        )
    )
    blocks = (
        lax.dot_general(
            query_grad,
            w_query[ringed:],
            (((1,), (1,)), ((), ())),
            preferred_element_type=jnp.float32,
        )
        .astype(jnp.bfloat16)
        .reshape(-1, rows, DIRECT)
    )
    pair, blocks = lax.optimization_barrier((pair, blocks))
    weight_grad = weight_reduce(pair)
    parts = lax.all_to_all(blocks, TENSOR, 0, 0, tiled=True)
    direct = jnp.sum(parts.astype(jnp.float32), axis=0)
    input_grad = finish(sums, arrived, direct, inputs, skip_grad, ln_gain)
    return (input_grad, weight_grad)


def solution(mesh):
    fine = Mesh(mesh.devices.reshape(SPLIT), DP + TENSOR)
    placed = (P(DP, None), P(), P(None, TENSOR), P(DP, TENSOR), P(DP + TENSOR, None))
    return jax.shard_map(
        per_device,
        mesh=fine,
        in_specs=placed,
        out_specs=(P(DP + TENSOR, None), P(DP, TENSOR)),
        check_vma=False,
    )
```

time: 122 us -> 158 us (1.30)
  the two profiles are of different devices: /device:TPU:128 before, /device:TPU:16 now
where the time goes in v6:
time: 158 us
  blocking collectives  55.3 us (35%)
  waiting for transfers between devices  40.5 us (26%)
  starting transfers between devices  20 us (13%)
  between operations  14.2 us (9%)
  other arithmetic  12.4 us (8%)
  Pallas kernels  7.92 us (5%)
  matrix products  3.91 us (2%)
  local copies, waits for them, and re-layouts  3.47 us (2%)
    all_to_all x1, blocking collectives, per_device(): parts = lax.all_to_all(blocks, TENSOR, 0, 0, tiled=True)  55.3 us
    all_to_all x1, waiting for transfers between devices, weight_reduce(): parts = lax.all_to_all(pair, ('y', 'z_lo'), 0, 0, tiled=True)  38.6 us
    all_to_all x1, starting transfers between devices, weight_reduce(): parts = lax.all_to_all(pair, ('y', 'z_lo'), 0, 0, tiled=True)  13.8 us
    ppermute x2, starting transfers between devices, shifted(): lax.ppermute(part, axis, [(i, (i + step) % size) for i in range(size)])  6.19 us
    pallas_call x1, Pallas kernels, product(): pl.pallas_call(product_kernel, in_specs=[pl.BlockSpec(memory_space=pl.ANY...  4.63 us
    reduce_sum x1, other arithmetic, per_device(): jnp.mean(center * center, axis=1, keepdims=True) + 1e-06  3.74 us
    pallas_call x1, Pallas kernels, finish(): pl.pallas_call(finish_kernel, grid_spec=pltpu.PrefetchScalarGridSpec(num_...  3.3 us
    reduce_sum x1, other arithmetic, per_device(): center = values - jnp.mean(values, axis=1, keepdims=True)  3.19 us
  transfers between devices with their start and end apart: 4, of which 2 were waited for; matrix products, arithmetic and copies ran while one was open for 11% of the time, Pallas kernels for 0%

profile of v6, /device:TPU:16, one launch (start us, length us, event | category | flops | bytes accessed | tf_op | source)
XLA Modules:
  0.0 157.7 jit_solution(1262686298868580365)
XLA Ops:
  7.2 0.0 reduce-scatter.2.cloned.1.call-start
  7.2 4.6 %shard_map.68 = bf16[384,5120]{1,0:T(8,128)(2,1)} custom-call(bf16[384,256]{1,0:T(8,128)(2,1)} %grads_hbm.1, bf16[6144,256]{1,0:T(8,128)(2,1)} %weights_hbm.1), custom_call_target="tpu_custom_call" | custom-call | flops 1006632960 | bytes 6750208 | tf_op jit(solution)/shard_map/pallas_call | solution.py:71
  11.8 0.0 slice-start
  11.9 0.0 reduce-scatter.2.cloned.1.call-update
  11.9 0.0 slice-start.1
  11.9 3.2 %convert_reduce_fusion = f32[384]{0:T(512)S(1)} fusion(bf16[384,6144]{1,0:T(8,128)(2,1)} %param.5), kind=kLoop, calls=%fused_computation.1 | loop fusion | flops 4718208 | bytes 4720128 | tf_op jit(solution)/shard_map/reduce_sum | solution.py:152
  15.1 0.0 copy-start.3
  15.1 3.7 %fusion.2 = f32[384]{0:T(512)S(1)} fusion(bf16[384,6144]{1,0:T(8,128)(2,1)} %param.5, f32[384]{0:T(512)S(1)} %broadcast_multiply_fusion.1), kind=kLoop, calls=%fused_computation.4 | loop fusion | flops 9436800 | bytes 4721664 | tf_op jit(solution)/shard_map/reduce_sum | solution.py:153
  18.9 0.0 slice-done
  18.9 0.0 slice-done.1
  18.9 0.0 copy-done.1
  18.9 0.0 copy-done.3
  18.9 2.5 %convolution_convert_fusion = bf16[6144,256]{1,0:T(8,128)(2,1)S(1)} fusion(bf16[384,256]{1,0:T(8,128)(2,1)S(1)} %copy-done.1, bf16[384,6144]{1,0:T(8,128)(2,1)S(1)} %bitcast.18, f32[6144]{0:T(1024)S(1)} %copy-done.3, f32[384]{0:T(512)S(1)} %add_rsqrt_fusion, f32[384]{0:T(512)S(1)} %broadcast_multiply_fusion.1), kind=kOutput, calls=%fused_computation.7 | convolution fusion | flops 1221328896 | bytes 8088576 | tf_op jit(solution)/shard_map/dot_general | solution.py:156
  21.4 0.0 copy-start
  21.4 1.7 %copy-done = bf16[6144,256]{1,0:T(8,128)(2,1)} copy-done((bf16[6144,256]{1,0:T(8,128)(2,1)}, bf16[6144,256]{1,0:T(8,128)(2,1)S(1)}, u32[]{:S(2)}) %copy-start) | copy-done | bytes 3145752
  23.1 0.1 dynamic-slice_bitcast_fusion
  23.2 1.9 %collective-permute-start.1 = (bf16[32,96,256]{2,1,0:T(8,128)(2,1)S(1)}, bf16[32,96,256]{2,1,0:T(8,128)(2,1)S(1)}, u32[]{:S(2)}, u32[]{:S(2)}) collective-permute-start(bf16[32,96,256]{2,1,0:T(8,128)(2,1)S(1)} %dynamic-slice_bitcast_fusion), channel_id=1, source_target_pairs={{0,16},{16,0},{1,17},{17,1},{2,18},{18,2},{3,19},{19,3},{4,20},{20... | collective-permute-start | bytes 4718600 | tf_op jit(solution)/shard_map/ppermute | solution.py:15
  25.1 1.4 convolution_convert_fusion.1
  26.6 1.9 %collective-permute-done.1 = bf16[32,96,256]{2,1,0:T(8,128)(2,1)S(1)} collective-permute-done((bf16[32,96,256]{2,1,0:T(8,128)(2,1)S(1)}, bf16[32,96,256]{2,1,0:T(8,128)(2,1)S(1)}, u32[]{:S(2)}, u32[]{:S(2)}) %collective-permute-start.1) | collective-permute-done | bytes 1572896 | tf_op jit(solution)/shard_map/ppermute | solution.py:15
  28.5 3.2 %fusion.9 = bf16[32,96,256]{2,1,0:T(8,128)(2,1)} fusion(bf16[32,96,256]{2,1,0:T(8,128)(2,1)S(1)} %collective-permute-done.1, bf16[32,2,96,256]{3,2,1,0:T(8,128)(2,1)} %bitcast.20, s32[]{:T(128)S(6)} %select_n.12), kind=kLoop, calls=%fused_computation.12 | loop fusion | flops 3145728 | bytes 4718596 | tf_op jit(solution)/shard_map/convert_element_type | solution.py:26
  31.7 55.3 %all_to_all.10 = bf16[16,24,1024]{2,1,0:T(8,128)(2,1)S(1)} all-to-all(bf16[16,24,1024]{2,1,0:T(8,128)(2,1)S(1)} %bitcast.21), channel_id=1, replica_groups=mesh['y'=8,'z_lo'=4,'core'=2,'x'=8,'z_hi'=2] {'x','z_hi'}, dimensions={0} | all-to-all | bytes 1572864 | tf_op jit(solution)/shard_map/all_to_all | solution.py:172
  87.0 13.8 %all-to-all-start.1 = ((bf16[32,96,256]{2,1,0:T(8,128)(2,1)}), bf16[32,96,256]{2,1,0:T(8,128)(2,1)S(1)}, u32[]{:S(2)}, u32[]{:S(2)}) async-start(bf16[32,96,256]{2,1,0:T(8,128)(2,1)} %fusion.9), calls=%async_computation.2 | async-start | bytes 3145728 | tf_op jit(solution)/shard_map/all_to_all | solution.py:30
  100.8 0.6 pad_add_fusion.place_ref
  101.4 0.8 convert_reduce_fusion.2.direct_ref
  102.1 1.0 dynamic-slice_bitcast_fusion.1
  103.1 4.3 %collective-permute-start = (bf16[24,5120]{1,0:T(8,128)(2,1)S(1)}, bf16[24,5120]{1,0:T(8,128)(2,1)S(1)}, u32[]{:S(2)}, u32[]{:S(2)}) collective-permute-start(bf16[24,5120]{1,0:T(8,128)(2,1)S(1)} %dynamic-slice_bitcast_fusion.1), channel_id=1, source_target_pairs={{0,1},{1,0},{2,3},{3,2},{4,5},{5,4},{6,7},{7,6},{8,9},{9,8},{10,11... | collective-permute-start | bytes 737288 | tf_op jit(solution)/shard_map/ppermute | solution.py:15
  107.4 38.6 %all-to-all-done.1 = bf16[32,96,256]{2,1,0:T(8,128)(2,1)S(1)} async-done(((bf16[32,96,256]{2,1,0:T(8,128)(2,1)}), bf16[32,96,256]{2,1,0:T(8,128)(2,1)S(1)}, u32[]{:S(2)}, u32[]{:S(2)}) %all-to-all-start.1) | async-done | bytes 1572896 | tf_op jit(solution)/shard_map/all_to_all | solution.py:30
  146.0 0.2 convert_reduce_fusion.1
  146.2 0.6 broadcast_multiply_fusion
  146.8 0.0 collective-permute-done.arrived_ref
  146.9 0.7 copy-done.2
  147.5 3.3 %shard_map.69 = bf16[24,6144]{1,0:T(8,128)(2,1)} custom-call(s32[2]{0:T(128)} %pad_add_fusion.place_ref, bf16[2,24,5120]{2,1,0:T(8,128)(2,1)} %bitcast.23, bf16[24,5120]{1,0:T(8,128)(2,1)} %copy-done.2, f32[24,1024]{1,0:T(8,128)} %convert_reduce_fusion.2.direct_ref, bf16[16,24,6144]{2,1,0:T(8,128)(2,1)} %bitcast.16, bf16[24,6144]{1,0:T(8,128)(2,1)} %skip_ref.1, ...), custom_call_target="tpu_custom_call" | custom-call | tf_op jit(solution)/shard_map/pallas_call | solution.py:114
  (6 shorter events, 0.0 us)
Async XLA Ops:
  7.2 95.0 %reduce-scatter.2.cloned.1.call-start = ((), (), s32[]{:S(2)}) async-start(), calls=%async_computation.3 | async-start | bytes 4423680 | tf_op jit(solution)/shard_map/reduce_scatter | solution.py:146
  11.8 7.0 %slice-start = ((s8[4718592]{0:T(1024)(128)(4,1)}), s8[524288]{0:T(1024)(128)(4,1)S(1)}, s32[]{:S(2)}) async-start(s8[4718592]{0:T(1024)(128)(4,1)} %bitcast.17), calls=%async_computation.4 | async-start | bytes 1048576
  11.9 7.0 %slice-start.1 = ((s8[4718592]{0:T(1024)(128)(4,1)}), s8[4194304]{0:T(1024)(128)(4,1)S(1)}, s32[]{:S(2)}) async-start(s8[4718592]{0:T(1024)(128)(4,1)} %bitcast.17), calls=%async_computation.5 | async-start | bytes 8388608
  15.1 3.8 %copy-start.1 = (bf16[384,256]{1,0:T(8,128)(2,1)S(1)}, bf16[384,256]{1,0:T(8,128)(2,1)}, u32[]{:S(2)}) copy-start(bf16[384,256]{1,0:T(8,128)(2,1)} %grads_hbm.1) | copy-start | bytes 589828
  15.1 3.8 %copy-start.3 = (f32[6144]{0:T(1024)S(1)}, f32[6144]{0:T(1024)}, u32[]{:S(2)}) copy-start(f32[6144]{0:T(1024)} %param.6) | copy-start | bytes 73732
  21.4 1.7 %copy-start = (bf16[6144,256]{1,0:T(8,128)(2,1)}, bf16[6144,256]{1,0:T(8,128)(2,1)S(1)}, u32[]{:S(2)}) copy-start(bf16[6144,256]{1,0:T(8,128)(2,1)S(1)} %convolution_convert_fusion) | copy-start | bytes 9437188
  23.2 5.3 %collective-permute-start.1 = (bf16[32,96,256]{2,1,0:T(8,128)(2,1)S(1)}, bf16[32,96,256]{2,1,0:T(8,128)(2,1)S(1)}, u32[]{:S(2)}, u32[]{:S(2)}) collective-permute-start(bf16[32,96,256]{2,1,0:T(8,128)(2,1)S(1)} %dynamic-slice_bitcast_fusion), channel_id=1, source_target_pairs={{0,16},{16,0},{1,17},{17,1},{2,18},{18,2},{3,19},{19,3},{4,20},{20... | collective-permute-start | bytes 4718600 | tf_op jit(solution)/shard_map/ppermute | solution.py:15
  87.0 59.0 %all-to-all-start.1 = ((bf16[32,96,256]{2,1,0:T(8,128)(2,1)}), bf16[32,96,256]{2,1,0:T(8,128)(2,1)S(1)}, u32[]{:S(2)}, u32[]{:S(2)}) async-start(bf16[32,96,256]{2,1,0:T(8,128)(2,1)} %fusion.9), calls=%async_computation.2 | async-start | bytes 3145728 | tf_op jit(solution)/shard_map/all_to_all | solution.py:30
  103.1 43.7 %collective-permute-start = (bf16[24,5120]{1,0:T(8,128)(2,1)S(1)}, bf16[24,5120]{1,0:T(8,128)(2,1)S(1)}, u32[]{:S(2)}, u32[]{:S(2)}) collective-permute-start(bf16[24,5120]{1,0:T(8,128)(2,1)S(1)} %dynamic-slice_bitcast_fusion.1), channel_id=1, source_target_pairs={{0,1},{1,0},{2,3},{3,2},{4,5},{5,4},{6,7},{7,6},{8,9},{9,8},{10,11... | collective-permute-start | bytes 737288 | tf_op jit(solution)/shard_map/ppermute | solution.py:15
  146.9 0.7 copy-start.2
Sparse Core Ops, SparseCore 0:
  12.0 85.6 reduce-scatter.1

commit v7 on v3

v7 whole, which is shorter than its diff:
```python
import jax
import jax.numpy as jnp
from jax import lax
from jax.experimental import pallas as pl
from jax.experimental.pallas import tpu as pltpu
from jax.sharding import Mesh, PartitionSpec as P

DP = ("y", "z_lo", "core")
TENSOR = ("x", "z_hi")
SPLIT = (8, 4, 2, 8, 2)


def shifted(part, axis, step):
    size = lax.axis_size(axis)
    return lax.ppermute(part, axis, [(i, (i + step) % size) for i in range(size)])


def core_sum(term):
    rows, columns = term.shape[0] // lax.axis_size(DP), term.shape[1]
    sizes = [lax.axis_size(axis) for axis in DP]
    blocks = term.astype(jnp.bfloat16).reshape(*sizes, rows, columns)
    me = lax.axis_index("core")
    own = lax.dynamic_index_in_dim(blocks, me, 2, False)
    other = lax.dynamic_index_in_dim(blocks, 1 - me, 2, False)
    pair = own.astype(jnp.float32) + shifted(other, "core", 1).astype(jnp.float32)
    return pair.astype(jnp.bfloat16).swapaxes(0, 1)


def exchange(total, axis):
    return jnp.sum(lax.all_to_all(total, axis, 0, 0, tiled=True).astype(jnp.float32), axis=0)


PIECES = 4


def product_kernel(grads_hbm, weights_hbm, out_hbm, grads, weights, out, took, loaded, stored):
    pieces, block = weights.shape[:2]
    first = pltpu.make_async_copy(grads_hbm, grads, took)
    first.start()
    loads = []
    for i in range(pieces):
        load = pltpu.make_async_copy(
            weights_hbm.at[pl.ds(i * block, block)], weights.at[i], loaded.at[i]
        )
        load.start()
        loads.append(load)
    first.wait()
    stores = []
    for i in range(pieces):
        loads[i].wait()
        out[i] = lax.dot_general(
            grads[...],
            weights[i],
            (((1,), (1,)), ((), ())),
            preferred_element_type=jnp.float32,
        ).astype(out.dtype)
        store = pltpu.make_async_copy(
            out.at[i], out_hbm.at[:, pl.ds(i * block, block)], stored.at[i]
        )
        store.start()
        stores.append(store)
    for store in stores:
        store.wait()


def product(query_grad, w_query, features):
    rows, depth = query_grad.shape
    block = features // PIECES
    return pl.pallas_call(
        product_kernel,
        in_specs=[pl.BlockSpec(memory_space=pl.ANY)] * 2,
        out_specs=pl.BlockSpec(memory_space=pl.ANY),
        out_shape=jax.ShapeDtypeStruct((rows, features), jnp.bfloat16),
        scratch_shapes=[
            pltpu.VMEM((rows, depth), jnp.bfloat16),
            pltpu.VMEM((PIECES, block, depth), jnp.bfloat16),
            pltpu.VMEM((PIECES, rows, block), jnp.bfloat16),
            pltpu.SemaphoreType.DMA,
            pltpu.SemaphoreType.DMA((PIECES,)),
            pltpu.SemaphoreType.DMA((PIECES,)),
        ],
        compiler_params=pltpu.CompilerParams(vmem_limit_bytes=60 << 20),
        cost_estimate=pl.CostEstimate(
            flops=2 * rows * depth * features,
            bytes_accessed=2 * (rows * depth + features * depth + rows * features),
            transcendentals=0,
        ),
    )(query_grad, w_query)


def per_device(inputs, ln_gain, w_query, query_grad, skip_grad):
    own_rows, features = skip_grad.shape
    term = product(query_grad, w_query, features)
    across = lax.psum_scatter(term, "x", scatter_dimension=0, tiled=True)

    values = inputs.astype(jnp.float32)
    mean = jnp.mean(values, axis=1, keepdims=True)
    center = values - mean
    inverse = lax.rsqrt(jnp.mean(center * center, axis=1, keepdims=True) + 1e-06)
    scaled = (center * inverse * ln_gain[None, :]).astype(jnp.bfloat16)
    pair = core_sum(
        lax.dot_general(
            scaled, query_grad, (((0,), (0,)), ((), ())), preferred_element_type=jnp.float32
        )
    )
    column = exchange(pair, "z_lo").astype(jnp.bfloat16)
    across, _ = lax.optimization_barrier((across, column))
    weight_grad = exchange(column, "y") / lax.axis_size(DP)

    halves = across.reshape(2, own_rows, features)
    me = lax.axis_index("z_hi")
    other = lax.dynamic_index_in_dim(halves, 1 - me, 0, False)
    own = lax.dynamic_index_in_dim(halves, me, 0, False)
    d_scaled = own.astype(jnp.float32) + shifted(other, "z_hi", 1).astype(jnp.float32)

    first = lax.axis_index(TENSOR) * own_rows
    own_values = lax.dynamic_slice_in_dim(inputs, first, own_rows, 0).astype(jnp.float32)
    mean_own = lax.dynamic_slice_in_dim(mean, first, own_rows, 0)
    inverse_own = lax.dynamic_slice_in_dim(inverse, first, own_rows, 0)
    normed_own = (own_values - mean_own) * inverse_own
    gated = d_scaled * ln_gain[None, :]
    mean_g = jnp.mean(gated, axis=1, keepdims=True)
    mean_gn = jnp.mean(gated * normed_own, axis=1, keepdims=True)
    input_grad = skip_grad.astype(jnp.float32) + inverse_own * (
        gated - mean_g - normed_own * mean_gn
    )
    return (input_grad.astype(jnp.bfloat16), weight_grad)


def solution(mesh):
    fine = Mesh(mesh.devices.reshape(SPLIT), DP + TENSOR)
    placed = (P(DP, None), P(), P(None, TENSOR), P(DP, TENSOR), P(DP + TENSOR, None))
    return jax.shard_map(
        per_device,
        mesh=fine,
        in_specs=placed,
        out_specs=(P(DP + TENSOR, None), P(DP, TENSOR)),
        check_vma=False,
    )
```

time: 122 us -> 120 us (0.984)
  blocking collectives: 0 us -> 49.7 us
  waiting for transfers between devices: 53.4 us -> 20.7 us
  starting transfers between devices: 25.7 us -> 13.2 us
  local copies, waits for them, and re-layouts: 7.25 us -> 1.48 us
  Pallas kernels: 0 us -> 4.75 us
  matrix products: 7.21 us -> 2.47 us
  other arithmetic: 14 us -> 12.7 us
    all_to_all x0 -> x1, blocking collectives: none -> 49.7 us  [exchange(): lax.all_to_all(total, axis, 0, 0, tiled=True).astype(jnp.float32)]
    reduce_scatter x1, waiting for transfers between devices: 38.7 us -> 4.95 us  [per_device(): across = lax.psum_scatter(term, 'x', scatter_dimension=0, tiled=True)]
    all_to_all x1, starting transfers between devices: 16 us -> 3.45 us  [exchange(): lax.all_to_all(total, axis, 0, 0, tiled=True).astype(jnp.float32)]
    pallas_call x0 -> x1, Pallas kernels: none -> 4.75 us  [product(): pl.pallas_call(product_kernel, in_specs=[pl.BlockSpec(memory_space=pl.ANY...]
    dot_general x1 -> x0, matrix products: 4.48 us -> none  [feature_reduce(): lax.dot_general(query_grad, w_query, (((1,), (1,)), ((), ())), preferred_...]
    unnamed x10, local copies, waits for them, and re-layouts: 4.04 us -> 0.03 us
    convert_element_type x1 -> x0, other arithmetic: 3.67 us -> none  [weight_reduce(): pair.astype(jnp.bfloat16)]
    reduce_sum x1, other arithmetic: 1.37 us -> 3.71 us  [per_device(): jnp.mean(center * center, axis=1, keepdims=True) + 1e-06]
  transfers between devices with their start and end apart: 4 -> 4, of which waited for: 3 -> 4; matrix products, arithmetic and copies ran while one was open for 14% -> 11% of each run, Pallas kernels for 0% -> 0%
where the time goes in v7:
time: 120 us; the launch traced here: 119 us
  blocking collectives  49.7 us (41%)
  waiting for transfers between devices  20.7 us (17%)
  between operations  14.2 us (12%)
  starting transfers between devices  13.2 us (11%)
  other arithmetic  12.7 us (11%)
  Pallas kernels  4.75 us (4%)
  matrix products  2.47 us (2%)
  local copies, waits for them, and re-layouts  1.48 us (1%)
    all_to_all x1, blocking collectives, exchange(): lax.all_to_all(total, axis, 0, 0, tiled=True).astype(jnp.float32)  49.7 us
    ppermute x2, waiting for transfers between devices, shifted(): lax.ppermute(part, axis, [(i, (i + step) % size) for i in range(size)])  15.6 us
    ppermute x2, starting transfers between devices, shifted(): lax.ppermute(part, axis, [(i, (i + step) % size) for i in range(size)])  9.75 us
    reduce_scatter x1, waiting for transfers between devices, per_device(): across = lax.psum_scatter(term, 'x', scatter_dimension=0, tiled=True)  4.95 us
    pallas_call x1, Pallas kernels, product(): pl.pallas_call(product_kernel, in_specs=[pl.BlockSpec(memory_space=pl.ANY...  4.75 us
    reduce_sum x1, other arithmetic, per_device(): jnp.mean(center * center, axis=1, keepdims=True) + 1e-06  3.71 us
    all_to_all x1, starting transfers between devices, exchange(): lax.all_to_all(total, axis, 0, 0, tiled=True).astype(jnp.float32)  3.45 us
    reduce_sum x1, other arithmetic, per_device(): mean = jnp.mean(values, axis=1, keepdims=True)  3.19 us
  transfers between devices with their start and end apart: 4, of which 4 were waited for; matrix products, arithmetic and copies ran while one was open for 11% of the time, Pallas kernels for 0%

profile of v7, /device:TPU:128, one launch (start us, length us, event | category | flops | bytes accessed | tf_op | source)
XLA Modules:
  0.0 119.3 jit_solution(14151633572367230057)
XLA Ops:
  7.2 0.0 reduce-scatter.2.cloned.1.call-start
  7.2 4.7 %shard_map.68 = bf16[384,6144]{1,0:T(8,128)(2,1)} custom-call(bf16[384,256]{1,0:T(8,128)(2,1)} %grads_hbm.1, bf16[6144,256]{1,0:T(8,128)(2,1)} %weights_hbm.1), custom_call_target="tpu_custom_call" | custom-call | flops 1207959552 | bytes 8060928 | tf_op jit(solution)/shard_map/pallas_call | solution.py:69
  12.0 0.0 slice-start
  12.0 0.0 reduce-scatter.2.cloned.1.call-update
  12.0 0.0 slice-start.1
  12.0 0.0 copy-start.1
  12.0 0.0 copy-start.2
  12.0 3.2 %convert_reduce_fusion = f32[384]{0:T(512)S(1)} fusion(bf16[384,6144]{1,0:T(8,128)(2,1)} %param.5), kind=kLoop, calls=%fused_computation.1 | loop fusion | flops 4718208 | bytes 4720128 | tf_op jit(solution)/shard_map/reduce_sum | solution.py:97
  15.2 3.7 %fusion.2 = f32[384]{0:T(512)S(1)} fusion(bf16[384,6144]{1,0:T(8,128)(2,1)} %param.5, f32[384]{0:T(512)S(1)} %broadcast_multiply_fusion.1), kind=kLoop, calls=%fused_computation.4 | loop fusion | flops 9436800 | bytes 4721664 | tf_op jit(solution)/shard_map/reduce_sum | solution.py:99
  19.0 0.0 slice-done
  19.0 0.0 slice-done.1
  19.0 2.5 %convolution_convert_fusion = bf16[6144,256]{1,0:T(8,128)(2,1)S(1)} fusion(bf16[384,256]{1,0:T(8,128)(2,1)S(1)} %copy-done.1, bf16[384,6144]{1,0:T(8,128)(2,1)S(1)} %bitcast.21, f32[6144]{0:T(1024)S(1)} %copy-done.2, f32[384]{0:T(512)S(1)} %add_rsqrt_fusion, f32[384]{0:T(512)S(1)} %broadcast_multiply_fusion.1), kind=kOutput, calls=%fused_computation.7 | convolution fusion | flops 1221328896 | bytes 8088576 | tf_op jit(solution)/shard_map/dot_general | solution.py:102
  21.5 0.2 constant_dynamic-slice_fusion.1
  21.7 0.1 copy.16
  21.8 1.9 %collective-permute-start = (bf16[8,4,96,256]{3,2,0,1:T(8,128)(2,1)S(1)}, bf16[8,4,96,256]{3,2,0,1:T(8,128)(2,1)S(1)}, u32[]{:S(2)}, u32[]{:S(2)}) collective-permute-start(bf16[8,4,96,256]{3,2,0,1:T(8,128)(2,1)S(1)} %bitcast.23), channel_id=1, source_target_pairs={{0,16},{16,0},{1,17},{17,1},{2,18},{18,2},{3,19},{19,3},{4,20},{20... | collective-permute-start | bytes 4718600 | tf_op jit(solution)/shard_map/ppermute | solution.py:15
  23.7 3.4 %collective-permute-done = bf16[8,4,96,256]{3,2,0,1:T(8,128)(2,1)S(1)} collective-permute-done((bf16[8,4,96,256]{3,2,0,1:T(8,128)(2,1)S(1)}, bf16[8,4,96,256]{3,2,0,1:T(8,128)(2,1)S(1)}, u32[]{:S(2)}, u32[]{:S(2)}) %collective-permute-start) | collective-permute-done | bytes 1572896 | tf_op jit(solution)/shard_map/ppermute | solution.py:15
  27.1 0.6 fusion.10
  27.7 0.0 copy-start
  27.7 49.7 %all_to_all.10 = bf16[4,8,96,256]{3,2,1,0:T(8,128)(2,1)S(1)} all-to-all(bf16[4,8,96,256]{3,2,1,0:T(8,128)(2,1)S(1)} %fusion.10), channel_id=1, replica_groups=mesh['y'=8,'z_lo'=4,'core'=2,'x'=8,'z_hi'=2] {'z_lo'}, dimensions={0} | all-to-all | bytes 3145728 | tf_op jit(solution)/shard_map/all_to_all | solution.py:30
  77.4 1.1 reduce_sum.59
  78.5 3.5 %all-to-all-start.1 = ((bf16[8,96,256]{2,1,0:T(8,128)(2,1)}), bf16[8,96,256]{2,1,0:T(8,128)(2,1)S(1)}, u32[]{:S(2)}, u32[]{:S(2)}) async-start(bf16[8,96,256]{2,1,0:T(8,128)(2,1)} %reduce_sum.59), calls=%async_computation.2 | async-start | bytes 786432 | tf_op jit(solution)/shard_map/all_to_all | solution.py:30
  82.0 0.1 dynamic-slice.7
  82.1 0.1 dynamic-slice.6
  82.1 4.9 %reduce-scatter.2.cloned.1.call-done = bf16[48,6144]{1,0:T(8,128)(2,1)} async-done(((bf16[384,6144]{1,0:T(8,128)(2,1)}), bf16[48,6144]{1,0:T(8,128)(2,1)}) %reduce-scatter.2.cloned.1.call-update) | async-done | bytes 589840 | tf_op jit(solution)/shard_map/reduce_scatter | solution.py:94
  87.1 1.0 dynamic-slice_bitcast_fusion
  88.1 7.8 %collective-permute-start.1 = (bf16[24,6144]{1,0:T(8,128)(2,1)S(1)}, bf16[24,6144]{1,0:T(8,128)(2,1)S(1)}, u32[]{:S(2)}, u32[]{:S(2)}) collective-permute-start(bf16[24,6144]{1,0:T(8,128)(2,1)S(1)} %dynamic-slice_bitcast_fusion), channel_id=1, source_target_pairs={{0,1},{1,0},{2,3},{3,2},{4,5},{5,4},{6,7},{7,6},{8,9},{9,8},{10,11... | collective-permute-start | bytes 884744 | tf_op jit(solution)/shard_map/ppermute | solution.py:15
  95.9 0.2 all-to-all-done.1
  96.1 0.1 convert_reduce_fusion.1
  96.1 0.6 broadcast_multiply_fusion
  96.8 12.2 %collective-permute-done.1 = bf16[24,6144]{1,0:T(8,128)(2,1)S(1)} collective-permute-done((bf16[24,6144]{1,0:T(8,128)(2,1)S(1)}, bf16[24,6144]{1,0:T(8,128)(2,1)S(1)}, u32[]{:S(2)}, u32[]{:S(2)}) %collective-permute-start.1) | collective-permute-done | bytes 294944 | tf_op jit(solution)/shard_map/ppermute | solution.py:15
  109.0 1.4 %fusion.12 = (f32[24]{0:T(128)S(1)}, f32[24]{0:T(128)S(1)}) fusion(bf16[24,6144]{1,0:T(8,128)(2,1)S(1)} %collective-permute-done.1, f32[6144]{0:T(1024)S(1)} %copy-done.2, bf16[2,24,6144]{2,1,0:T(8,128)(2,1)} %bitcast.25, s32[]{:T(128)S(6)} %select_n.22, f32[24]{0:T(128)S(1)} %dynamic-slice.6, f32[24]{0:T(128)S(1)} %dynamic-slice.7, ...), kind=kLoop, calls=%fused_computation.22 | loop fusion | flops 1474512 | bytes 909704 | tf_op jit(solution)/shard_map/reduce_sum | solution.py:122
  110.4 2.1 %add_convert_fusion = bf16[24,6144]{1,0:T(8,128)(2,1)} fusion(bf16[24,6144]{1,0:T(8,128)(2,1)S(1)} %copy-done, bf16[24,6144]{1,0:T(8,128)(2,1)S(1)} %collective-permute-done.1, f32[24]{0:T(128)S(1)} %get-tuple-element.8, f32[24]{0:T(128)S(1)} %dynamic-slice.7, f32[24]{0:T(128)S(1)} %get-tuple-element.9, f32[6144]{0:T(1024)S(1)} %copy-done.2, ...), kind=kLoop, calls=%fused_computation.19 | loop fusion | flops 2064384 | bytes 1499528 | tf_op jit(solution)/shard_map/convert_element_type | solution.py:127
  (7 shorter events, 0.0 us)
Async XLA Ops:
  7.2 79.9 %reduce-scatter.2.cloned.1.call-start = ((), (), s32[]{:S(2)}) async-start(), calls=%async_computation.3 | async-start | bytes 5308416 | tf_op jit(solution)/shard_map/reduce_scatter | solution.py:94
  12.0 7.0 %slice-start = ((s8[4718592]{0:T(1024)(128)(4,1)}), s8[524288]{0:T(1024)(128)(4,1)S(1)}, s32[]{:S(2)}) async-start(s8[4718592]{0:T(1024)(128)(4,1)} %bitcast.20), calls=%async_computation.4 | async-start | bytes 1048576
  12.0 7.0 %slice-start.1 = ((s8[4718592]{0:T(1024)(128)(4,1)}), s8[4194304]{0:T(1024)(128)(4,1)S(1)}, s32[]{:S(2)}) async-start(s8[4718592]{0:T(1024)(128)(4,1)} %bitcast.20), calls=%async_computation.5 | async-start | bytes 8388608
  12.0 7.0 %copy-start.1 = (bf16[384,256]{1,0:T(8,128)(2,1)S(1)}, bf16[384,256]{1,0:T(8,128)(2,1)}, u32[]{:S(2)}) copy-start(bf16[384,256]{1,0:T(8,128)(2,1)} %grads_hbm.1) | copy-start | bytes 589828
  12.0 7.0 %copy-start.2 = (f32[6144]{0:T(1024)S(1)}, f32[6144]{0:T(1024)}, u32[]{:S(2)}) copy-start(f32[6144]{0:T(1024)} %param.6) | copy-start | bytes 73732
  21.8 5.3 %collective-permute-start = (bf16[8,4,96,256]{3,2,0,1:T(8,128)(2,1)S(1)}, bf16[8,4,96,256]{3,2,0,1:T(8,128)(2,1)S(1)}, u32[]{:S(2)}, u32[]{:S(2)}) collective-permute-start(bf16[8,4,96,256]{3,2,0,1:T(8,128)(2,1)S(1)} %bitcast.23), channel_id=1, source_target_pairs={{0,16},{16,0},{1,17},{17,1},{2,18},{18,2},{3,19},{19,3},{4,20},{20... | collective-permute-start | bytes 4718600 | tf_op jit(solution)/shard_map/ppermute | solution.py:15
  27.7 82.7 %copy-start = (bf16[24,6144]{1,0:T(8,128)(2,1)S(1)}, bf16[24,6144]{1,0:T(8,128)(2,1)}, u32[]{:S(2)}) copy-start(bf16[24,6144]{1,0:T(8,128)(2,1)} %param.9) | copy-start | bytes 884740
  78.5 17.6 %all-to-all-start.1 = ((bf16[8,96,256]{2,1,0:T(8,128)(2,1)}), bf16[8,96,256]{2,1,0:T(8,128)(2,1)S(1)}, u32[]{:S(2)}, u32[]{:S(2)}) async-start(bf16[8,96,256]{2,1,0:T(8,128)(2,1)} %reduce_sum.59), calls=%async_computation.2 | async-start | bytes 786432 | tf_op jit(solution)/shard_map/all_to_all | solution.py:30
  88.1 20.9 %collective-permute-start.1 = (bf16[24,6144]{1,0:T(8,128)(2,1)S(1)}, bf16[24,6144]{1,0:T(8,128)(2,1)S(1)}, u32[]{:S(2)}, u32[]{:S(2)}) collective-permute-start(bf16[24,6144]{1,0:T(8,128)(2,1)S(1)} %dynamic-slice_bitcast_fusion), channel_id=1, source_target_pairs={{0,1},{1,0},{2,3},{3,2},{4,5},{5,4},{6,7},{7,6},{8,9},{9,8},{10,11... | collective-permute-start | bytes 884744 | tf_op jit(solution)/shard_map/ppermute | solution.py:15
Sparse Core Ops, SparseCore 0:
  12.1 74.9 reduce-scatter.1

commit v8 on v2

v8 whole, which is shorter than its diff:
```python
import jax
import jax.numpy as jnp
from jax import lax
from jax.sharding import Mesh, PartitionSpec as P

DP = ("y", "z_lo", "core")
TENSOR = ("x", "z_hi")
SPLIT = (8, 4, 2, 8, 2)


def wide(part):
    return part.astype(jnp.float32)


def narrow(part):
    return part.astype(jnp.bfloat16)


def swap(part, axis, bit):
    return lax.ppermute(part, axis, [(i, i ^ bit) for i in range(lax.axis_size(axis))])


def swap_even(part, axis):
    return swap(part, axis, 1)


def swap_odd(part, axis):
    size = lax.axis_size(axis)
    return lax.ppermute(
        part, axis, [(i, (i + 1 if i % 2 else i - 1) % size) for i in range(size)]
    )


def pair_blocks(term):
    cores, rows = lax.axis_size("core"), term.shape[0] // lax.axis_size(DP)
    return term.reshape(-1, cores, rows, term.shape[1])


def core_half(blocks, index):
    return lax.dynamic_index_in_dim(blocks, index, 1, False)


def weight_reduce(pair):
    parts = lax.all_to_all(pair, ("y", "z_lo"), 0, 0, tiled=True)
    return jnp.sum(wide(parts), axis=0) / lax.axis_size(DP)


def product(query_grad, w_query):
    return narrow(
        lax.dot_general(
            query_grad, w_query, (((1,), (1,)), ((), ())), preferred_element_type=jnp.float32
        )
    )


def pick(parts, index):
    return lax.dynamic_index_in_dim(parts, index, 0, False)


def per_device(inputs, ln_gain, w_query, query_grad, skip_grad):
    size, sets = lax.axis_size("x"), lax.axis_size("z_hi")
    far = size // 2
    own_rows = skip_grad.shape[0]
    x, z_hi, core = lax.axis_index("x"), lax.axis_index("z_hi"), lax.axis_index("core")
    parity = x % 2
    way = 1 - 2 * parity
    chunk_rows = sets * own_rows
    chunk = lax.dynamic_slice_in_dim(query_grad, (x + far) % size * chunk_rows, chunk_rows, 0)
    farthest = product(chunk, w_query).reshape(sets, own_rows, -1)
    farthest, query_grad, inputs = lax.optimization_barrier((farthest, query_grad, inputs))
    one = swap_even(pick(farthest, parity), "x")
    two = swap_odd(pick(farthest, 1 - parity), "x")

    terms = product(query_grad, w_query).reshape(size, sets, own_rows, -1)
    values = wide(inputs)
    mean = jnp.mean(values, axis=1, keepdims=True)

    def term(step):
        return pick(terms, (x + step + size) % size)

    which = jnp.arange(sets)[:, None, None]
    one = jnp.where(which == 1 - parity, one[None], jnp.bfloat16(0))
    two = jnp.where(which == parity, two[None], jnp.bfloat16(0))
    up = narrow(wide(term(way * (far - 1))) + wide(two))
    down = narrow(wide(term(-way * (far - 1))) + wide(one))
    up, down, mean = lax.optimization_barrier((up, down, mean))
    one, two = swap_even(up, "x"), swap_odd(down, "x")

    center = values - mean
    inverse = lax.rsqrt(jnp.mean(center * center, axis=1, keepdims=True) + 1e-06)
    scaled = narrow(center * inverse * ln_gain[None, :])
    blocks = pair_blocks(
        narrow(
            lax.dot_general(
                scaled, query_grad, (((0,), (0,)), ((), ())), preferred_element_type=jnp.float32
            )
        )
    )
    received = swap(core_half(blocks, 1 - core), "core", 1)
    pair = narrow(wide(core_half(blocks, core)) + wide(received))
    one, two, _ = lax.optimization_barrier((one, two, pair))
    up = narrow(wide(term(way * 2)) + wide(two))
    down = narrow(wide(term(-way * 2)) + wide(one))
    up, down = lax.optimization_barrier((up, down))
    one, two = swap_even(up, "x"), swap_odd(down, "x")

    weight_grad = weight_reduce(pair)
    up = narrow(wide(term(way)) + wide(two))
    down = narrow(wide(term(-way)) + wide(one))
    up, down = lax.optimization_barrier((up, down))
    one, two = swap_even(up, "x"), swap_odd(down, "x")

    def total(index):
        return wide(pick(term(0), index)) + wide(pick(one, index)) + wide(pick(two, index))

    d_scaled = total(z_hi) + wide(swap(narrow(total(1 - z_hi)), "z_hi", 1))

    first = lax.axis_index(TENSOR) * own_rows
    own_values = lax.dynamic_slice_in_dim(inputs, first, own_rows, 0).astype(jnp.float32)
    mean_own = lax.dynamic_slice_in_dim(mean, first, own_rows, 0)
    inverse_own = lax.dynamic_slice_in_dim(inverse, first, own_rows, 0)
    normed_own = (own_values - mean_own) * inverse_own
    gated = d_scaled * ln_gain[None, :]
    mean_g = jnp.mean(gated, axis=1, keepdims=True)
    mean_gn = jnp.mean(gated * normed_own, axis=1, keepdims=True)
    input_grad = skip_grad.astype(jnp.float32) + inverse_own * (
        gated - mean_g - normed_own * mean_gn
    )
    return (input_grad.astype(jnp.bfloat16), weight_grad)


def solution(mesh):
    fine = Mesh(mesh.devices.reshape(SPLIT), DP + TENSOR)
    placed = (P(DP, None), P(), P(None, TENSOR), P(DP, TENSOR), P(DP + TENSOR, None))
    return jax.shard_map(
        per_device,
        mesh=fine,
        in_specs=placed,
        out_specs=(P(DP + TENSOR, None), P(DP, TENSOR)),
        check_vma=False,
    )
```

time: 162 us -> 170 us (1.049)
  the two profiles are of different devices: /device:TPU:10 before, /device:TPU:4 now
where the time goes in v8:
time: 170 us; the launch traced here: 169 us
  waiting for transfers between devices  70.5 us (41%)
  starting transfers between devices  54.2 us (32%)
  other arithmetic  26 us (15%)
  matrix products  8.8 us (5%)
  local copies, waits for them, and re-layouts  8.68 us (5%)
    ppermute x6, waiting for transfers between devices, swap(): lax.ppermute(part, axis, [(i, i ^ bit) for i in range(lax.axis_size(axis))])  63.6 us
    ppermute x6, starting transfers between devices, swap(): lax.ppermute(part, axis, [(i, i ^ bit) for i in range(lax.axis_size(axis))])  23.8 us
    ppermute x4, starting transfers between devices, swap_odd(): lax.ppermute(part, axis, [(i, (i + 1 if i % 2 else i - 1) % size) for i i...  22 us
    convert_element_type x5, other arithmetic, narrow(): return part.astype(jnp.bfloat16)  13.2 us
    all_to_all x1, starting transfers between devices, weight_reduce(): parts = lax.all_to_all(pair, ('y', 'z_lo'), 0, 0, tiled=True)  8.44 us
    ppermute x4, waiting for transfers between devices, swap_odd(): lax.ppermute(part, axis, [(i, (i + 1 if i % 2 else i - 1) % size) for i i...  6.92 us
    unnamed x10, local copies, waits for them, and re-layouts  5.23 us
    dot_general x1, matrix products, per_device(): lax.dot_general(scaled, query_grad, (((0,), (0,)), ((), ())), preferred_e...  4.78 us
  transfers between devices with their start and end apart: 11, of which 8 were waited for; matrix products, arithmetic and copies ran while one was open for 8% of the time, Pallas kernels for 0%

profile of v8, /device:TPU:4, one launch (start us, length us, event | category | flops | bytes accessed | tf_op | source)
XLA Modules:
  0.0 169.3 jit_solution(3567582883078953692)
XLA Ops:
  0.7 1.8 %copy-done = bf16[6144,256]{1,0:T(8,128)(2,1)S(1)} copy-done((bf16[6144,256]{1,0:T(8,128)(2,1)S(1)}, bf16[6144,256]{1,0:T(8,128)(2,1)}, u32[]{:S(2)}) %copy-start) | copy-done | bytes 3145752
  2.5 2.6 %convolution_convert_fusion.2 = bf16[48,6144]{1,0:T(8,128)(2,1)} fusion(bf16[6144,256]{1,0:T(8,128)(2,1)S(1)} %copy-done, bf16[384,256]{1,0:T(8,128)(2,1)} %param.8, s32[]{:T(128)S(6)} %select_n.110), kind=kOutput, calls=%fused_computation.9 | convolution fusion | flops 151289856 | bytes 3760132 | tf_op jit(solution)/shard_map/dot_general | solution.py:50
  5.1 1.9 %dynamic-slice_bitcast_fusion.1 = (bf16[24,6144]{1,0:T(8,128)(2,1)}, bf16[24,6144]{1,0:T(8,128)(2,1)}) fusion(bf16[2,24,6144]{2,1,0:T(8,128)(2,1)} %bitcast.64, s32[]{:T(128)S(6)} %select_n.118, s32[]{:T(128)S(6)} %select_n.114), kind=kLoop, calls=%fused_computation.39 | loop fusion | bytes 1179656 | tf_op jit(solution)/shard_map/jit(dynamic_index_in_dim)/squeeze | solution.py:57
  7.1 3.4 %collective-permute-start.1 = (bf16[24,6144]{1,0:T(8,128)(2,1)}, bf16[24,6144]{1,0:T(8,128)(2,1)}, u32[]{:S(2)}, u32[]{:S(2)}) collective-permute-start(bf16[24,6144]{1,0:T(8,128)(2,1)} %get-tuple-element.35), channel_id=1, source_target_pairs={{0,2},{2,0},{4,6},{6,4},{8,10},{10,8},{12,14},{14,12},{1,3},{3,1},... | collective-permute-start | bytes 884744 | tf_op jit(solution)/shard_map/ppermute | solution.py:20
  10.5 14.1 %collective-permute-start = (bf16[24,6144]{1,0:T(8,128)(2,1)}, bf16[24,6144]{1,0:T(8,128)(2,1)}, u32[]{:S(2)}, u32[]{:S(2)}) collective-permute-start(bf16[24,6144]{1,0:T(8,128)(2,1)} %get-tuple-element.36), channel_id=1, source_target_pairs={{0,14},{2,4},{4,2},{6,8},{8,6},{10,12},{12,10},{14,0},{1,15},{3,5}... | collective-permute-start | bytes 884744 | tf_op jit(solution)/shard_map/ppermute | solution.py:29
  24.7 3.0 %convert_reduce_fusion = f32[384]{0:T(512)S(1)} fusion(bf16[384,6144]{1,0:T(8,128)(2,1)} %param.5), kind=kLoop, calls=%fused_computation.1 | loop fusion | flops 4718208 | bytes 4720128 | tf_op jit(solution)/shard_map/reduce_sum | solution.py:76
  29.6 1.7 %copy-done.1 = bf16[384,6144]{1,0:T(8,128)(2,1)} copy-done((bf16[384,6144]{1,0:T(8,128)(2,1)}, bf16[384,6144]{1,0:T(8,128)(2,1)S(1)}, u32[]{:S(2)}) %copy-start.1) | copy-done | bytes 4718616
  31.3 2.5 %fusion.14 = (bf16[2,24,6144]{2,1,0:T(8,128)(2,1)}, bf16[2,24,6144]{2,1,0:T(8,128)(2,1)}) fusion(bf16[8,2,24,6144]{3,2,1,0:T(8,128)(2,1)S(1)} %bitcast.57, s32[]{:T(128)S(6)} %select_n.117, pred[2]{0:T(512)(128)(4,1)S(1)} %get-tuple-element.37, bf16[24,6144]{1,0:T(8,128)(2,1)} %collective-permute-done.1, bf16[24,6144]{1,0:T(8,128)(2,1)} %collective-permute-done, ...), kind=kLoop, calls=%fused_computation.26 | loop fusion | flops 2949120 | bytes 2949132 | tf_op jit(solution)/shard_map/convert_element_type | solution.py:16
  33.8 3.7 %fusion.2 = f32[384]{0:T(512)S(1)} fusion(bf16[384,6144]{1,0:T(8,128)(2,1)} %param.5, f32[384]{0:T(512)S(1)} %reduce), kind=kLoop, calls=%fused_computation.4 | loop fusion | flops 9436800 | bytes 4721664 | tf_op jit(solution)/shard_map/reduce_sum | solution.py:90
  37.6 4.8 %convolution_convert_fusion.1 = bf16[6144,256]{1,0:T(8,128)(2,1)S(1)} fusion(bf16[384,256]{1,0:T(8,128)(2,1)S(1)} %copy-done.3, bf16[384,6144]{1,0:T(8,128)(2,1)} %param.5, f32[6144]{0:T(1024)S(1)} %copy-done.4, f32[384]{0:T(512)S(1)} %add_rsqrt_fusion, f32[384]{0:T(512)S(1)} %reduce), kind=kOutput, calls=%fused_computation.8 | convolution fusion | flops 1221328896 | bytes 8088576 | tf_op jit(solution)/shard_map/dot_general | solution.py:94
  42.4 1.6 copy-done.2
  45.4 1.9 %collective-permute-start.4 = (bf16[32,96,256]{2,1,0:T(8,128)(2,1)}, bf16[32,96,256]{2,1,0:T(8,128)(2,1)}, u32[]{:S(2)}, u32[]{:S(2)}) collective-permute-start(bf16[32,96,256]{2,1,0:T(8,128)(2,1)} %dynamic-slice_bitcast_fusion), channel_id=1, source_target_pairs={{0,16},{16,0},{1,17},{17,1},{2,18},{18,2},{3,19},{19,3},{4,20},{20... | collective-permute-start | bytes 4718600 | tf_op jit(solution)/shard_map/ppermute | solution.py:20
  47.3 1.9 %collective-permute-start.2 = (bf16[2,24,6144]{2,1,0:T(8,128)(2,1)}, bf16[2,24,6144]{2,1,0:T(8,128)(2,1)}, u32[]{:S(2)}, u32[]{:S(2)}) collective-permute-start(bf16[2,24,6144]{2,1,0:T(8,128)(2,1)} %get-tuple-element.18), channel_id=1, source_target_pairs={{0,2},{2,0},{4,6},{6,4},{8,10},{10,8},{12,14},{14,12},{1,3},{3,1},... | collective-permute-start | bytes 1769480 | tf_op jit(solution)/shard_map/ppermute | solution.py:20
  49.2 3.4 %collective-permute-start.3 = (bf16[2,24,6144]{2,1,0:T(8,128)(2,1)}, bf16[2,24,6144]{2,1,0:T(8,128)(2,1)}, u32[]{:S(2)}, u32[]{:S(2)}) collective-permute-start(bf16[2,24,6144]{2,1,0:T(8,128)(2,1)} %get-tuple-element.19), channel_id=1, source_target_pairs={{0,14},{2,4},{4,2},{6,8},{8,6},{10,12},{12,10},{14,0},{1,15},{3,5}... | collective-permute-start | bytes 1769480 | tf_op jit(solution)/shard_map/ppermute | solution.py:29
  52.7 3.7 %fusion.9 = bf16[32,96,256]{2,1,0:T(8,128)(2,1)} fusion(bf16[32,96,256]{2,1,0:T(8,128)(2,1)} %collective-permute-done.4, bf16[32,2,96,256]{3,2,1,0:T(8,128)(2,1)} %bitcast.63, s32[]{:T(128)S(6)} %select_n.130), kind=kLoop, calls=%fused_computation.14 | loop fusion | flops 3145728 | bytes 4718596 | tf_op jit(solution)/shard_map/convert_element_type | solution.py:16
  56.4 8.9 %collective-permute-done.2 = bf16[2,24,6144]{2,1,0:T(8,128)(2,1)} collective-permute-done((bf16[2,24,6144]{2,1,0:T(8,128)(2,1)}, bf16[2,24,6144]{2,1,0:T(8,128)(2,1)}, u32[]{:S(2)}, u32[]{:S(2)}) %collective-permute-start.2) | collective-permute-done | bytes 589856 | tf_op jit(solution)/shard_map/ppermute | solution.py:20
  65.2 1.9 %collective-permute-done.3 = bf16[2,24,6144]{2,1,0:T(8,128)(2,1)} collective-permute-done((bf16[2,24,6144]{2,1,0:T(8,128)(2,1)}, bf16[2,24,6144]{2,1,0:T(8,128)(2,1)}, u32[]{:S(2)}, u32[]{:S(2)}) %collective-permute-start.3) | collective-permute-done | bytes 589856 | tf_op jit(solution)/shard_map/ppermute | solution.py:29
  67.1 2.9 %fusion.11 = (bf16[2,24,6144]{2,1,0:T(8,128)(2,1)}, bf16[2,24,6144]{2,1,0:T(8,128)(2,1)}) fusion(bf16[2,24,6144]{2,1,0:T(8,128)(2,1)} %collective-permute-done.2, bf16[8,2,24,6144]{3,2,1,0:T(8,128)(2,1)} %bitcast.58, s32[]{:T(128)S(6)} %select_n.133, bf16[2,24,6144]{2,1,0:T(8,128)(2,1)} %collective-permute-done.3, s32[]{:T(128)S(6)} %select_n.129), kind=kLoop, calls=%fused_computation.20 | loop fusion | flops 2359296 | bytes 3538952 | tf_op jit(solution)/shard_map/convert_element_type | solution.py:16
  70.0 4.8 %collective-permute-start.6 = (bf16[2,24,6144]{2,1,0:T(8,128)(2,1)}, bf16[2,24,6144]{2,1,0:T(8,128)(2,1)}, u32[]{:S(2)}, u32[]{:S(2)}) collective-permute-start(bf16[2,24,6144]{2,1,0:T(8,128)(2,1)} %get-tuple-element.23), channel_id=1, source_target_pairs={{0,2},{2,0},{4,6},{6,4},{8,10},{10,8},{12,14},{14,12},{1,3},{3,1},... | collective-permute-start | bytes 1769480 | tf_op jit(solution)/shard_map/ppermute | solution.py:20
  74.9 2.2 %collective-permute-start.5 = (bf16[2,24,6144]{2,1,0:T(8,128)(2,1)}, bf16[2,24,6144]{2,1,0:T(8,128)(2,1)}, u32[]{:S(2)}, u32[]{:S(2)}) collective-permute-start(bf16[2,24,6144]{2,1,0:T(8,128)(2,1)} %get-tuple-element.22), channel_id=1, source_target_pairs={{0,14},{2,4},{4,2},{6,8},{8,6},{10,12},{12,10},{14,0},{1,15},{3,5}... | collective-permute-start | bytes 1769480 | tf_op jit(solution)/shard_map/ppermute | solution.py:29
  77.1 10.9 %collective-permute-done.6 = bf16[2,24,6144]{2,1,0:T(8,128)(2,1)} collective-permute-done((bf16[2,24,6144]{2,1,0:T(8,128)(2,1)}, bf16[2,24,6144]{2,1,0:T(8,128)(2,1)}, u32[]{:S(2)}, u32[]{:S(2)}) %collective-permute-start.6) | collective-permute-done | bytes 589856 | tf_op jit(solution)/shard_map/ppermute | solution.py:20
  88.1 3.4 %collective-permute-done.5 = bf16[2,24,6144]{2,1,0:T(8,128)(2,1)} collective-permute-done((bf16[2,24,6144]{2,1,0:T(8,128)(2,1)}, bf16[2,24,6144]{2,1,0:T(8,128)(2,1)}, u32[]{:S(2)}, u32[]{:S(2)}) %collective-permute-start.5) | collective-permute-done | bytes 589856 | tf_op jit(solution)/shard_map/ppermute | solution.py:29
  91.5 2.9 %fusion.10 = (bf16[2,24,6144]{2,1,0:T(8,128)(2,1)}, bf16[2,24,6144]{2,1,0:T(8,128)(2,1)}) fusion(bf16[2,24,6144]{2,1,0:T(8,128)(2,1)} %collective-permute-done.6, bf16[8,2,24,6144]{3,2,1,0:T(8,128)(2,1)} %bitcast.59, s32[]{:T(128)S(6)} %select_n.135, bf16[2,24,6144]{2,1,0:T(8,128)(2,1)} %collective-permute-done.5, s32[]{:T(128)S(6)} %select_n.127), kind=kLoop, calls=%fused_computation.18 | loop fusion | flops 2359296 | bytes 3538952 | tf_op jit(solution)/shard_map/convert_element_type | solution.py:16
  94.4 2.2 %collective-permute-start.8 = (bf16[2,24,6144]{2,1,0:T(8,128)(2,1)}, bf16[2,24,6144]{2,1,0:T(8,128)(2,1)}, u32[]{:S(2)}, u32[]{:S(2)}) collective-permute-start(bf16[2,24,6144]{2,1,0:T(8,128)(2,1)} %get-tuple-element.25), channel_id=1, source_target_pairs={{0,14},{2,4},{4,2},{6,8},{8,6},{10,12},{12,10},{14,0},{1,15},{3,5}... | collective-permute-start | bytes 1769480 | tf_op jit(solution)/shard_map/ppermute | solution.py:29
  96.6 3.7 %collective-permute-start.7 = (bf16[2,24,6144]{2,1,0:T(8,128)(2,1)}, bf16[2,24,6144]{2,1,0:T(8,128)(2,1)}, u32[]{:S(2)}, u32[]{:S(2)}) collective-permute-start(bf16[2,24,6144]{2,1,0:T(8,128)(2,1)} %get-tuple-element.24), channel_id=1, source_target_pairs={{0,2},{2,0},{4,6},{6,4},{8,10},{10,8},{12,14},{14,12},{1,3},{3,1},... | collective-permute-start | bytes 1769480 | tf_op jit(solution)/shard_map/ppermute | solution.py:20
  100.3 8.4 %all-to-all-start = ((bf16[32,96,256]{2,1,0:T(8,128)(2,1)}), bf16[32,96,256]{2,1,0:T(8,128)(2,1)}, u32[]{:S(2)}, u32[]{:S(2)}) async-start(bf16[32,96,256]{2,1,0:T(8,128)(2,1)} %fusion.9), calls=%async_computation | async-start | bytes 3145728 | tf_op jit(solution)/shard_map/all_to_all | solution.py:44
  110.0 2.6 %collective-permute-done.7 = bf16[2,24,6144]{2,1,0:T(8,128)(2,1)} collective-permute-done((bf16[2,24,6144]{2,1,0:T(8,128)(2,1)}, bf16[2,24,6144]{2,1,0:T(8,128)(2,1)}, u32[]{:S(2)}, u32[]{:S(2)}) %collective-permute-start.7) | collective-permute-done | bytes 589856 | tf_op jit(solution)/shard_map/ppermute | solution.py:20
  113.9 8.0 %collective-permute-start.9 = (bf16[24,6144]{1,0:T(8,128)(2,1)S(1)}, bf16[24,6144]{1,0:T(8,128)(2,1)}, u32[]{:S(2)}, u32[]{:S(2)}) collective-permute-start(bf16[24,6144]{1,0:T(8,128)(2,1)S(1)} %fusion.16), channel_id=1, source_target_pairs={{0,1},{1,0},{2,3},{3,2},{4,5},{5,4},{6,7},{7,6},{8,9},{9,8},{10,11... | collective-permute-start | bytes 884744 | tf_op jit(solution)/shard_map/ppermute | solution.py:20
  122.1 41.1 %collective-permute-done.9 = bf16[24,6144]{1,0:T(8,128)(2,1)} collective-permute-done((bf16[24,6144]{1,0:T(8,128)(2,1)S(1)}, bf16[24,6144]{1,0:T(8,128)(2,1)}, u32[]{:S(2)}, u32[]{:S(2)}) %collective-permute-start.9) | collective-permute-done | bytes 294944 | tf_op jit(solution)/shard_map/ppermute | solution.py:20
  163.2 1.7 %fusion.22 = (f32[24]{0:T(128)S(1)}, f32[24]{0:T(128)S(1)}, f32[24,6144]{1,0:T(8,128)S(1)}) fusion(f32[24]{0:T(128)S(1)} %dynamic-slice.7, f32[24]{0:T(128)S(1)} %fusion.21, bf16[384,6144]{1,0:T(8,128)(2,1)} %param.5, s32[]{:T(128)S(6)} %select_n.120, f32[6144]{0:T(1024)S(1)} %copy-done.4, bf16[24,6144]{1,0:T(8,128)(2,1)} %collective-permute-done.9, ...), kind=kLoop, calls=%fused_computation.52 | loop fusion | flops 2064336 | bytes 2089360 | tf_op jit(solution)/shard_map/reduce_sum | solution.py:124
  165.0 2.0 %add_convert_fusion = bf16[24,6144]{1,0:T(8,128)(2,1)} fusion(f32[24,6144]{1,0:T(8,128)S(1)} %get-tuple-element.28, bf16[24,6144]{1,0:T(8,128)(2,1)} %param.9, f32[24]{0:T(128)S(1)} %broadcast_multiply_fusion.2, f32[24]{0:T(128)S(1)} %fusion.21, f32[24]{0:T(128)S(1)} %broadcast_multiply_fusion.3, f32[24]{0:T(128)S(1)} %dynamic-slice.7, ...), kind=kLoop, calls=%fused_computation.36 | loop fusion | flops 1474560 | bytes 1474948 | tf_op jit(solution)/shard_map/convert_element_type | solution.py:129
  167.0 1.6 convert_reduce_fusion.1
  (25 shorter events, 6.5 us)
Async XLA Ops:
  0.6 1.9 %copy-start = (bf16[6144,256]{1,0:T(8,128)(2,1)S(1)}, bf16[6144,256]{1,0:T(8,128)(2,1)}, u32[]{:S(2)}) copy-start(bf16[6144,256]{1,0:T(8,128)(2,1)} %param.7) | copy-start | bytes 9437188
  5.1 22.6 %copy-start.3 = (bf16[384,256]{1,0:T(8,128)(2,1)S(1)}, bf16[384,256]{1,0:T(8,128)(2,1)}, u32[]{:S(2)}) copy-start(bf16[384,256]{1,0:T(8,128)(2,1)} %param.8) | copy-start | bytes 589828
  7.1 22.1 %collective-permute-start.1 = (bf16[24,6144]{1,0:T(8,128)(2,1)}, bf16[24,6144]{1,0:T(8,128)(2,1)}, u32[]{:S(2)}, u32[]{:S(2)}) collective-permute-start(bf16[24,6144]{1,0:T(8,128)(2,1)} %get-tuple-element.35), channel_id=1, source_target_pairs={{0,2},{2,0},{4,6},{6,4},{8,10},{10,8},{12,14},{14,12},{1,3},{3,1},... | collective-permute-start | bytes 884744 | tf_op jit(solution)/shard_map/ppermute | solution.py:20
  10.5 19.1 %collective-permute-start = (bf16[24,6144]{1,0:T(8,128)(2,1)}, bf16[24,6144]{1,0:T(8,128)(2,1)}, u32[]{:S(2)}, u32[]{:S(2)}) collective-permute-start(bf16[24,6144]{1,0:T(8,128)(2,1)} %get-tuple-element.36), channel_id=1, source_target_pairs={{0,14},{2,4},{4,2},{6,8},{8,6},{10,12},{12,10},{14,0},{1,15},{3,5}... | collective-permute-start | bytes 884744 | tf_op jit(solution)/shard_map/ppermute | solution.py:29
  29.2 2.1 %copy-start.1 = (bf16[384,6144]{1,0:T(8,128)(2,1)}, bf16[384,6144]{1,0:T(8,128)(2,1)S(1)}, u32[]{:S(2)}) copy-start(bf16[384,6144]{1,0:T(8,128)(2,1)S(1)} %convolution_convert_fusion) | copy-start | bytes 14155780
  31.3 6.2 %copy-start.4 = (f32[6144]{0:T(1024)S(1)}, f32[6144]{0:T(1024)}, u32[]{:S(2)}) copy-start(f32[6144]{0:T(1024)} %param.6) | copy-start | bytes 73732
  42.3 1.7 copy-start.2
  45.4 7.3 %collective-permute-start.4 = (bf16[32,96,256]{2,1,0:T(8,128)(2,1)}, bf16[32,96,256]{2,1,0:T(8,128)(2,1)}, u32[]{:S(2)}, u32[]{:S(2)}) collective-permute-start(bf16[32,96,256]{2,1,0:T(8,128)(2,1)} %dynamic-slice_bitcast_fusion), channel_id=1, source_target_pairs={{0,16},{16,0},{1,17},{17,1},{2,18},{18,2},{3,19},{19,3},{4,20},{20... | collective-permute-start | bytes 4718600 | tf_op jit(solution)/shard_map/ppermute | solution.py:20
  47.3 17.9 %collective-permute-start.2 = (bf16[2,24,6144]{2,1,0:T(8,128)(2,1)}, bf16[2,24,6144]{2,1,0:T(8,128)(2,1)}, u32[]{:S(2)}, u32[]{:S(2)}) collective-permute-start(bf16[2,24,6144]{2,1,0:T(8,128)(2,1)} %get-tuple-element.18), channel_id=1, source_target_pairs={{0,2},{2,0},{4,6},{6,4},{8,10},{10,8},{12,14},{14,12},{1,3},{3,1},... | collective-permute-start | bytes 1769480 | tf_op jit(solution)/shard_map/ppermute | solution.py:20
  49.2 17.9 %collective-permute-start.3 = (bf16[2,24,6144]{2,1,0:T(8,128)(2,1)}, bf16[2,24,6144]{2,1,0:T(8,128)(2,1)}, u32[]{:S(2)}, u32[]{:S(2)}) collective-permute-start(bf16[2,24,6144]{2,1,0:T(8,128)(2,1)} %get-tuple-element.19), channel_id=1, source_target_pairs={{0,14},{2,4},{4,2},{6,8},{8,6},{10,12},{12,10},{14,0},{1,15},{3,5}... | collective-permute-start | bytes 1769480 | tf_op jit(solution)/shard_map/ppermute | solution.py:29
  70.0 18.0 %collective-permute-start.6 = (bf16[2,24,6144]{2,1,0:T(8,128)(2,1)}, bf16[2,24,6144]{2,1,0:T(8,128)(2,1)}, u32[]{:S(2)}, u32[]{:S(2)}) collective-permute-start(bf16[2,24,6144]{2,1,0:T(8,128)(2,1)} %get-tuple-element.23), channel_id=1, source_target_pairs={{0,2},{2,0},{4,6},{6,4},{8,10},{10,8},{12,14},{14,12},{1,3},{3,1},... | collective-permute-start | bytes 1769480 | tf_op jit(solution)/shard_map/ppermute | solution.py:20
  74.9 16.6 %collective-permute-start.5 = (bf16[2,24,6144]{2,1,0:T(8,128)(2,1)}, bf16[2,24,6144]{2,1,0:T(8,128)(2,1)}, u32[]{:S(2)}, u32[]{:S(2)}) collective-permute-start(bf16[2,24,6144]{2,1,0:T(8,128)(2,1)} %get-tuple-element.22), channel_id=1, source_target_pairs={{0,14},{2,4},{4,2},{6,8},{8,6},{10,12},{12,10},{14,0},{1,15},{3,5}... | collective-permute-start | bytes 1769480 | tf_op jit(solution)/shard_map/ppermute | solution.py:29
  94.4 15.6 %collective-permute-start.8 = (bf16[2,24,6144]{2,1,0:T(8,128)(2,1)}, bf16[2,24,6144]{2,1,0:T(8,128)(2,1)}, u32[]{:S(2)}, u32[]{:S(2)}) collective-permute-start(bf16[2,24,6144]{2,1,0:T(8,128)(2,1)} %get-tuple-element.25), channel_id=1, source_target_pairs={{0,14},{2,4},{4,2},{6,8},{8,6},{10,12},{12,10},{14,0},{1,15},{3,5}... | collective-permute-start | bytes 1769480 | tf_op jit(solution)/shard_map/ppermute | solution.py:29
  96.6 16.1 %collective-permute-start.7 = (bf16[2,24,6144]{2,1,0:T(8,128)(2,1)}, bf16[2,24,6144]{2,1,0:T(8,128)(2,1)}, u32[]{:S(2)}, u32[]{:S(2)}) collective-permute-start(bf16[2,24,6144]{2,1,0:T(8,128)(2,1)} %get-tuple-element.24), channel_id=1, source_target_pairs={{0,2},{2,0},{4,6},{6,4},{8,10},{10,8},{12,14},{14,12},{1,3},{3,1},... | collective-permute-start | bytes 1769480 | tf_op jit(solution)/shard_map/ppermute | solution.py:20
  100.3 66.7 %all-to-all-start = ((bf16[32,96,256]{2,1,0:T(8,128)(2,1)}), bf16[32,96,256]{2,1,0:T(8,128)(2,1)}, u32[]{:S(2)}, u32[]{:S(2)}) async-start(bf16[32,96,256]{2,1,0:T(8,128)(2,1)} %fusion.9), calls=%async_computation | async-start | bytes 3145728 | tf_op jit(solution)/shard_map/all_to_all | solution.py:44
  113.9 49.3 %collective-permute-start.9 = (bf16[24,6144]{1,0:T(8,128)(2,1)S(1)}, bf16[24,6144]{1,0:T(8,128)(2,1)}, u32[]{:S(2)}, u32[]{:S(2)}) collective-permute-start(bf16[24,6144]{1,0:T(8,128)(2,1)S(1)} %fusion.16), channel_id=1, source_target_pairs={{0,1},{1,0},{2,3},{3,2},{4,5},{5,4},{6,7},{7,6},{8,9},{9,8},{10,11... | collective-permute-start | bytes 884744 | tf_op jit(solution)/shard_map/ppermute | solution.py:20

commit v9 on v7

--- a/solution.py
+++ b/solution.py
@@ -88,6 +88,28 @@
     )(query_grad, w_query)
 
 
+def finish_kernel(own_ref, arrived_ref, normed_ref, inverse_ref, skip_ref, gain_ref, out_ref):
+    normed = normed_ref[...]
+    summed = own_ref[...].astype(jnp.float32) + arrived_ref[...].astype(jnp.float32)
+    gated = summed * gain_ref[...]
+    mean_g = jnp.mean(gated, axis=1, keepdims=True)
+    mean_gn = jnp.mean(gated * normed, axis=1, keepdims=True)
+    grad = skip_ref[...].astype(jnp.float32) + inverse_ref[...] * (
+        gated - mean_g - normed * mean_gn
+    )
+    out_ref[...] = grad.astype(out_ref.dtype)
+
+
+def finish(own, arrived, normed, inverse, skip_grad, ln_gain):
+    return pl.pallas_call(
+        finish_kernel,
+        in_specs=[pl.BlockSpec(memory_space=pltpu.VMEM)] * 6,
+        out_specs=pl.BlockSpec(memory_space=pltpu.VMEM),
+        out_shape=jax.ShapeDtypeStruct(skip_grad.shape, jnp.bfloat16),
+        compiler_params=pltpu.CompilerParams(vmem_limit_bytes=16 << 20),
+    )(own, arrived, normed, inverse, skip_grad, ln_gain[None, :])
+
+
 def per_device(inputs, ln_gain, w_query, query_grad, skip_grad):
     own_rows, features = skip_grad.shape
     term = product(query_grad, w_query, features)
@@ -111,20 +133,15 @@
     me = lax.axis_index("z_hi")
     other = lax.dynamic_index_in_dim(halves, 1 - me, 0, False)
     own = lax.dynamic_index_in_dim(halves, me, 0, False)
-    d_scaled = own.astype(jnp.float32) + shifted(other, "z_hi", 1).astype(jnp.float32)
+    arrived = shifted(other, "z_hi", 1)
 
     first = lax.axis_index(TENSOR) * own_rows
     own_values = lax.dynamic_slice_in_dim(inputs, first, own_rows, 0).astype(jnp.float32)
     mean_own = lax.dynamic_slice_in_dim(mean, first, own_rows, 0)
     inverse_own = lax.dynamic_slice_in_dim(inverse, first, own_rows, 0)
     normed_own = (own_values - mean_own) * inverse_own
-    gated = d_scaled * ln_gain[None, :]
-    mean_g = jnp.mean(gated, axis=1, keepdims=True)
-    mean_gn = jnp.mean(gated * normed_own, axis=1, keepdims=True)
-    input_grad = skip_grad.astype(jnp.float32) + inverse_own * (
-        gated - mean_g - normed_own * mean_gn
-    )
-    return (input_grad.astype(jnp.bfloat16), weight_grad)
+    input_grad = finish(own, arrived, normed_own, inverse_own, skip_grad, ln_gain)
+    return (input_grad, weight_grad)
 
 
 def solution(mesh):

time: 120 us -> 118 us (0.983)
  the two profiles are of different devices: /device:TPU:128 before, /device:TPU:24 now
where the time goes in v9:
time: 118 us
  waiting for transfers between devices  50.2 us (43%)
  starting transfers between devices  31.3 us (27%)
  between operations  14.2 us (12%)
  other arithmetic  11.6 us (10%)
  Pallas kernels  5.99 us (5%)
  matrix products  2.8 us (2%)
  local copies, waits for them, and re-layouts  1.75 us (1%)
    all_to_all x2, waiting for transfers between devices, exchange(): lax.all_to_all(total, axis, 0, 0, tiled=True).astype(jnp.float32)  36 us
    all_to_all x2, starting transfers between devices, exchange(): lax.all_to_all(total, axis, 0, 0, tiled=True).astype(jnp.float32)  18 us
    ppermute x2, waiting for transfers between devices, shifted(): lax.ppermute(part, axis, [(i, (i + step) % size) for i in range(size)])  13.7 us
    ppermute x2, starting transfers between devices, shifted(): lax.ppermute(part, axis, [(i, (i + step) % size) for i in range(size)])  13.3 us
    pallas_call x1, Pallas kernels, product(): pl.pallas_call(product_kernel, in_specs=[pl.BlockSpec(memory_space=pl.ANY...  4.81 us
    reduce_sum x1, other arithmetic, per_device(): jnp.mean(center * center, axis=1, keepdims=True) + 1e-06  3.71 us
    reduce_sum x1, other arithmetic, per_device(): mean = jnp.mean(values, axis=1, keepdims=True)  3.19 us
    dot_general x1, matrix products, per_device(): lax.dot_general(scaled, query_grad, (((0,), (0,)), ((), ())), preferred_e...  2.8 us
  transfers between devices with their start and end apart: 5, of which 4 were waited for; matrix products, arithmetic and copies ran while one was open for 14% of the time, Pallas kernels for 0%

profile of v9, /device:TPU:24, one launch (start us, length us, event | category | flops | bytes accessed | tf_op | source)
XLA Modules:
  0.0 117.8 jit_solution(3547609885650719940)
XLA Ops:
  7.2 0.0 reduce-scatter.2.cloned.1.call-start
  7.2 4.8 %shard_map.68 = bf16[384,6144]{1,0:T(8,128)(2,1)} custom-call(bf16[384,256]{1,0:T(8,128)(2,1)} %grads_hbm.1, bf16[6144,256]{1,0:T(8,128)(2,1)} %weights_hbm.1), custom_call_target="tpu_custom_call" | custom-call | flops 1207959552 | bytes 8060928 | tf_op jit(solution)/shard_map/pallas_call | solution.py:69
  12.0 0.0 slice-start
  12.0 0.0 reduce-scatter.2.cloned.1.call-update
  12.1 0.0 copy-start.1
  12.1 0.0 slice-start.1
  12.1 0.0 copy-start.2
  12.1 3.2 %convert_reduce_fusion = f32[384]{0:T(512)S(1)} fusion(bf16[384,6144]{1,0:T(8,128)(2,1)} %param.5), kind=kLoop, calls=%fused_computation.1 | loop fusion | flops 4718208 | bytes 4720128 | tf_op jit(solution)/shard_map/reduce_sum | solution.py:119
  15.3 3.7 %fusion.2 = f32[384]{0:T(512)S(1)} fusion(bf16[384,6144]{1,0:T(8,128)(2,1)} %param.5, f32[384]{0:T(512)S(1)} %broadcast_multiply_fusion.1), kind=kLoop, calls=%fused_computation.4 | loop fusion | flops 9436800 | bytes 4721664 | tf_op jit(solution)/shard_map/reduce_sum | solution.py:121
  19.1 2.8 %convolution_convert_fusion = bf16[6144,256]{1,0:T(8,128)(2,1)S(1)} fusion(bf16[384,256]{1,0:T(8,128)(2,1)S(1)} %copy-done.2, bf16[384,6144]{1,0:T(8,128)(2,1)S(1)} %bitcast.22, f32[6144]{0:T(1024)S(1)} %copy-done.1, f32[384]{0:T(512)S(1)} %add_rsqrt_fusion, f32[384]{0:T(512)S(1)} %broadcast_multiply_fusion.1), kind=kOutput, calls=%fused_computation.7 | convolution fusion | flops 1221328896 | bytes 8088576 | tf_op jit(solution)/shard_map/dot_general | solution.py:124
  21.9 0.2 constant_dynamic-slice_fusion.1
  22.1 0.1 copy.19
  22.2 1.9 %collective-permute-start = (bf16[8,4,96,256]{3,2,0,1:T(8,128)(2,1)S(1)}, bf16[8,4,96,256]{3,2,0,1:T(8,128)(2,1)S(1)}, u32[]{:S(2)}, u32[]{:S(2)}) collective-permute-start(bf16[8,4,96,256]{3,2,0,1:T(8,128)(2,1)S(1)} %bitcast.24), channel_id=1, source_target_pairs={{0,16},{16,0},{1,17},{17,1},{2,18},{18,2},{3,19},{19,3},{4,20},{20... | collective-permute-start | bytes 4718600 | tf_op jit(solution)/shard_map/ppermute | solution.py:15
  24.1 3.4 %collective-permute-done = bf16[8,4,96,256]{3,2,0,1:T(8,128)(2,1)S(1)} collective-permute-done((bf16[8,4,96,256]{3,2,0,1:T(8,128)(2,1)S(1)}, bf16[8,4,96,256]{3,2,0,1:T(8,128)(2,1)S(1)}, u32[]{:S(2)}, u32[]{:S(2)}) %collective-permute-start) | collective-permute-done | bytes 1572896 | tf_op jit(solution)/shard_map/ppermute | solution.py:15
  27.5 1.7 %fusion.10 = bf16[4,8,96,256]{3,2,1,0:T(8,128)(2,1)} fusion(bf16[8,4,96,256]{3,2,0,1:T(8,128)(2,1)S(1)} %collective-permute-done, bf16[8,4,1,96,256]{4,3,2,1,0:T(8,128)(2,1)S(1)} %get-tuple-element.4), kind=kLoop, calls=%fused_computation.13 | loop fusion | flops 3145728 | bytes 4718592 | tf_op jit(solution)/shard_map/transpose | solution.py:26
  29.2 10.1 %all-to-all-start = ((bf16[4,8,96,256]{3,2,1,0:T(8,128)(2,1)}), bf16[4,8,96,256]{3,2,1,0:T(8,128)(2,1)S(1)}, u32[]{:S(2)}, u32[]{:S(2)}) async-start(bf16[4,8,96,256]{3,2,1,0:T(8,128)(2,1)} %fusion.10), calls=%async_computation.1 | async-start | bytes 3145728 | tf_op jit(solution)/shard_map/all_to_all | solution.py:30
  39.4 0.1 dynamic-slice.7
  39.4 0.1 dynamic-slice.6
  39.5 1.2 subtract_multiply_fusion.normed_ref
  40.7 36.0 %all-to-all-done = bf16[4,8,96,256]{3,2,1,0:T(8,128)(2,1)S(1)} async-done(((bf16[4,8,96,256]{3,2,1,0:T(8,128)(2,1)}), bf16[4,8,96,256]{3,2,1,0:T(8,128)(2,1)S(1)}, u32[]{:S(2)}, u32[]{:S(2)}) %all-to-all-start) | async-done | bytes 1572896 | tf_op jit(solution)/shard_map/all_to_all | solution.py:30
  76.6 1.1 reduce_sum.41
  77.7 7.9 %all-to-all-start.1 = ((bf16[8,96,256]{2,1,0:T(8,128)(2,1)}), bf16[8,96,256]{2,1,0:T(8,128)(2,1)S(1)}, u32[]{:S(2)}, u32[]{:S(2)}) async-start(bf16[8,96,256]{2,1,0:T(8,128)(2,1)} %reduce_sum.41), calls=%async_computation.2 | async-start | bytes 786432 | tf_op jit(solution)/shard_map/all_to_all | solution.py:30
  85.6 0.1 dynamic-slice_bitcast_fusion.2
  85.7 0.1 copy.13.inverse_ref
  85.8 0.5 reduce-scatter.2.cloned.1.call-done
  86.3 1.1 dynamic-slice_bitcast_fusion
  87.4 11.4 %collective-permute-start.1 = (bf16[24,6144]{1,0:T(8,128)(2,1)S(1)}, bf16[24,6144]{1,0:T(8,128)(2,1)S(1)}, u32[]{:S(2)}, u32[]{:S(2)}) collective-permute-start(bf16[24,6144]{1,0:T(8,128)(2,1)S(1)} %get-tuple-element.6), channel_id=1, source_target_pairs={{0,1},{1,0},{2,3},{3,2},{4,5},{5,4},{6,7},{7,6},{8,9},{9,8},{10,11... | collective-permute-start | bytes 884744 | tf_op jit(solution)/shard_map/ppermute | solution.py:15
  98.7 0.0 all-to-all-done.1
  98.8 0.1 convert_reduce_fusion.1
  98.8 0.6 broadcast_multiply_fusion
  99.5 10.3 %collective-permute-done.1.arrived_ref = bf16[24,6144]{1,0:T(8,128)(2,1)S(1)} collective-permute-done((bf16[24,6144]{1,0:T(8,128)(2,1)S(1)}, bf16[24,6144]{1,0:T(8,128)(2,1)S(1)}, u32[]{:S(2)}, u32[]{:S(2)}) %collective-permute-start.1) | collective-permute-done | bytes 294944 | tf_op jit(solution)/shard_map/ppermute | solution.py:15
  109.8 1.2 shard_map.69
  (9 shorter events, 0.0 us)
Async XLA Ops:
  7.2 79.1 %reduce-scatter.2.cloned.1.call-start = ((), (), s32[]{:S(2)}) async-start(), calls=%async_computation.3 | async-start | bytes 5308416 | tf_op jit(solution)/shard_map/reduce_scatter | solution.py:116
  12.0 7.0 %slice-start = ((s8[4718592]{0:T(1024)(128)(4,1)}), s8[524288]{0:T(1024)(128)(4,1)S(1)}, s32[]{:S(2)}) async-start(s8[4718592]{0:T(1024)(128)(4,1)} %bitcast.21), calls=%async_computation.4 | async-start | bytes 1048576
  12.1 7.0 %copy-start.1 = (f32[6144]{0:T(1024)S(1)}, f32[6144]{0:T(1024)}, u32[]{:S(2)}) copy-start(f32[6144]{0:T(1024)} %param.6) | copy-start | bytes 73732
  12.1 7.0 %slice-start.1 = ((s8[4718592]{0:T(1024)(128)(4,1)}), s8[4194304]{0:T(1024)(128)(4,1)S(1)}, s32[]{:S(2)}) async-start(s8[4718592]{0:T(1024)(128)(4,1)} %bitcast.21), calls=%async_computation.5 | async-start | bytes 8388608
  12.1 7.0 %copy-start.2 = (bf16[384,256]{1,0:T(8,128)(2,1)S(1)}, bf16[384,256]{1,0:T(8,128)(2,1)}, u32[]{:S(2)}) copy-start(bf16[384,256]{1,0:T(8,128)(2,1)} %grads_hbm.1) | copy-start | bytes 589828
  22.2 5.3 %collective-permute-start = (bf16[8,4,96,256]{3,2,0,1:T(8,128)(2,1)S(1)}, bf16[8,4,96,256]{3,2,0,1:T(8,128)(2,1)S(1)}, u32[]{:S(2)}, u32[]{:S(2)}) collective-permute-start(bf16[8,4,96,256]{3,2,0,1:T(8,128)(2,1)S(1)} %bitcast.24), channel_id=1, source_target_pairs={{0,16},{16,0},{1,17},{17,1},{2,18},{18,2},{3,19},{19,3},{4,20},{20... | collective-permute-start | bytes 4718600 | tf_op jit(solution)/shard_map/ppermute | solution.py:15
  29.2 80.6 %copy-start = (bf16[24,6144]{1,0:T(8,128)(2,1)S(1)}, bf16[24,6144]{1,0:T(8,128)(2,1)}, u32[]{:S(2)}) copy-start(bf16[24,6144]{1,0:T(8,128)(2,1)} %skip_ref.1) | copy-start | bytes 884740
  29.2 47.4 %all-to-all-start = ((bf16[4,8,96,256]{3,2,1,0:T(8,128)(2,1)}), bf16[4,8,96,256]{3,2,1,0:T(8,128)(2,1)S(1)}, u32[]{:S(2)}, u32[]{:S(2)}) async-start(bf16[4,8,96,256]{3,2,1,0:T(8,128)(2,1)} %fusion.10), calls=%async_computation.1 | async-start | bytes 3145728 | tf_op jit(solution)/shard_map/all_to_all | solution.py:30
  77.7 21.0 %all-to-all-start.1 = ((bf16[8,96,256]{2,1,0:T(8,128)(2,1)}), bf16[8,96,256]{2,1,0:T(8,128)(2,1)S(1)}, u32[]{:S(2)}, u32[]{:S(2)}) async-start(bf16[8,96,256]{2,1,0:T(8,128)(2,1)} %reduce_sum.41), calls=%async_computation.2 | async-start | bytes 786432 | tf_op jit(solution)/shard_map/all_to_all | solution.py:30
  87.4 22.4 %collective-permute-start.1 = (bf16[24,6144]{1,0:T(8,128)(2,1)S(1)}, bf16[24,6144]{1,0:T(8,128)(2,1)S(1)}, u32[]{:S(2)}, u32[]{:S(2)}) collective-permute-start(bf16[24,6144]{1,0:T(8,128)(2,1)S(1)} %get-tuple-element.6), channel_id=1, source_target_pairs={{0,1},{1,0},{2,3},{3,2},{4,5},{5,4},{6,7},{7,6},{8,9},{9,8},{10,11... | collective-permute-start | bytes 884744 | tf_op jit(solution)/shard_map/ppermute | solution.py:15
Sparse Core Ops, SparseCore 0:
  12.2 74.0 reduce-scatter.1

commit v10 on v9

--- a/solution.py
+++ b/solution.py
@@ -88,6 +88,29 @@
     )(query_grad, w_query)
 
 
+def scaled_kernel(inputs_ref, gain_ref, out_ref):
+    values = inputs_ref[...].astype(jnp.float32)
+    center = values - jnp.mean(values, axis=1, keepdims=True)
+    inverse = lax.rsqrt(jnp.mean(center * center, axis=1, keepdims=True) + 1e-06)
+    out_ref[...] = (center * inverse * gain_ref[...]).astype(out_ref.dtype)
+
+
+def layer_norm(inputs, ln_gain):
+    rows, features = inputs.shape
+    block = rows // 6
+    return pl.pallas_call(
+        scaled_kernel,
+        grid=(rows // block,),
+        in_specs=[
+            pl.BlockSpec((block, features), lambda i: (i, 0)),
+            pl.BlockSpec((1, features), lambda i: (0, 0)),
+        ],
+        out_specs=pl.BlockSpec((block, features), lambda i: (i, 0)),
+        out_shape=jax.ShapeDtypeStruct(inputs.shape, jnp.bfloat16),
+        compiler_params=pltpu.CompilerParams(vmem_limit_bytes=60 << 20),
+    )(inputs, ln_gain[None, :])
+
+
 def finish_kernel(own_ref, arrived_ref, normed_ref, inverse_ref, skip_ref, gain_ref, out_ref):
     normed = normed_ref[...]
     summed = own_ref[...].astype(jnp.float32) + arrived_ref[...].astype(jnp.float32)
@@ -115,11 +138,7 @@
     term = product(query_grad, w_query, features)
     across = lax.psum_scatter(term, "x", scatter_dimension=0, tiled=True)
 
-    values = inputs.astype(jnp.float32)
-    mean = jnp.mean(values, axis=1, keepdims=True)
-    center = values - mean
-    inverse = lax.rsqrt(jnp.mean(center * center, axis=1, keepdims=True) + 1e-06)
-    scaled = (center * inverse * ln_gain[None, :]).astype(jnp.bfloat16)
+    scaled = layer_norm(inputs, ln_gain)
     pair = core_sum(
         lax.dot_general(
             scaled, query_grad, (((0,), (0,)), ((), ())), preferred_element_type=jnp.float32
@@ -136,11 +155,11 @@
     arrived = shifted(other, "z_hi", 1)
 
     first = lax.axis_index(TENSOR) * own_rows
-    own_values = lax.dynamic_slice_in_dim(inputs, first, own_rows, 0).astype(jnp.float32)
-    mean_own = lax.dynamic_slice_in_dim(mean, first, own_rows, 0)
-    inverse_own = lax.dynamic_slice_in_dim(inverse, first, own_rows, 0)
-    normed_own = (own_values - mean_own) * inverse_own
-    input_grad = finish(own, arrived, normed_own, inverse_own, skip_grad, ln_gain)
+    inputs, _ = lax.optimization_barrier((inputs, pair))
+    values = lax.dynamic_slice_in_dim(inputs, first, own_rows, 0).astype(jnp.float32)
+    center = values - jnp.mean(values, axis=1, keepdims=True)
+    inverse = lax.rsqrt(jnp.mean(center * center, axis=1, keepdims=True) + 1e-06)
+    input_grad = finish(own, arrived, center * inverse, inverse, skip_grad, ln_gain)
     return (input_grad, weight_grad)
 
 

time: 118 us -> 122 us (1.034)
  Pallas kernels: 5.99 us -> 13.8 us
  other arithmetic: 11.6 us -> 7.06 us
  matrix products: 2.8 us -> 4.17 us
    pallas_call x0 -> x1, Pallas kernels: none -> 7.87 us  [layer_norm(): pl.pallas_call(scaled_kernel, grid=(rows // block,), in_specs=[pl.BlockSp...]
    reduce_sum x1, other arithmetic: 3.71 us -> 1.22 us  [per_device(): jnp.mean(center * center, axis=1, keepdims=True) + 1e-06]
    reduce_sum x1, other arithmetic: 3.19 us -> 1.17 us  [per_device(): center = values - jnp.mean(values, axis=1, keepdims=True)]
    dot_general x1, matrix products: 2.8 us -> 4.17 us  [per_device(): lax.dot_general(scaled, query_grad, (((0,), (0,)), ((), ())), preferred_e...]
  transfers between devices with their start and end apart: 5 -> 5, of which waited for: 4 -> 3; matrix products, arithmetic and copies ran while one was open for 14% -> 10% of each run, Pallas kernels for 0% -> 6%
where the time goes in v10:
time: 122 us
  waiting for transfers between devices  49.4 us (40%)
  starting transfers between devices  31.7 us (26%)
  between operations  14.1 us (12%)
  Pallas kernels  13.8 us (11%)
  other arithmetic  7.06 us (6%)
  matrix products  4.17 us (3%)
  local copies, waits for them, and re-layouts  1.57 us (1%)
    all_to_all x2, waiting for transfers between devices, exchange(): lax.all_to_all(total, axis, 0, 0, tiled=True).astype(jnp.float32)  34.9 us
    all_to_all x2, starting transfers between devices, exchange(): lax.all_to_all(total, axis, 0, 0, tiled=True).astype(jnp.float32)  17.9 us
    ppermute x2, waiting for transfers between devices, shifted(): lax.ppermute(part, axis, [(i, (i + step) % size) for i in range(size)])  14.5 us
    ppermute x2, starting transfers between devices, shifted(): lax.ppermute(part, axis, [(i, (i + step) % size) for i in range(size)])  13.8 us
    pallas_call x1, Pallas kernels, layer_norm(): pl.pallas_call(scaled_kernel, grid=(rows // block,), in_specs=[pl.BlockSp...  7.87 us
    pallas_call x1, Pallas kernels, product(): pl.pallas_call(product_kernel, in_specs=[pl.BlockSpec(memory_space=pl.ANY...  4.81 us
    dot_general x1, matrix products, per_device(): lax.dot_general(scaled, query_grad, (((0,), (0,)), ((), ())), preferred_e...  4.17 us
  transfers between devices with their start and end apart: 5, of which 3 were waited for; matrix products, arithmetic and copies ran while one was open for 10% of the time, Pallas kernels for 6%

profile of v10, /device:TPU:24, one launch (start us, length us, event | category | flops | bytes accessed | tf_op | source)
XLA Modules:
  0.0 121.8 jit_solution(16787061668955696072)
XLA Ops:
  7.2 0.0 reduce-scatter.2.cloned.1.call-start
  7.2 4.8 %shard_map.68 = bf16[384,6144]{1,0:T(8,128)(2,1)} custom-call(bf16[384,256]{1,0:T(8,128)(2,1)} %grads_hbm.1, bf16[6144,256]{1,0:T(8,128)(2,1)} %weights_hbm.1), custom_call_target="tpu_custom_call" | custom-call | flops 1207959552 | bytes 8060928 | tf_op jit(solution)/shard_map/pallas_call | solution.py:69
  12.0 0.0 reduce-scatter.2.cloned.1.call-update
  12.1 0.0 copy-start.2
  12.1 7.9 %shard_map.69 = bf16[384,6144]{1,0:T(8,128)(2,1)} custom-call(bf16[384,6144]{1,0:T(8,128)(2,1)} %inputs_ref.1, f32[1,6144]{1,0:T(1,128)} %bitcast.21), custom_call_target="tpu_custom_call" | custom-call | tf_op jit(solution)/shard_map/pallas_call | solution.py:101
  19.9 0.0 copy-done.2
  19.9 4.2 %convolution_convert_fusion = bf16[6144,256]{1,0:T(8,128)(2,1)S(1)} fusion(bf16[384,6144]{1,0:T(8,128)(2,1)} %shard_map.69, bf16[384,256]{1,0:T(8,128)(2,1)S(1)} %copy-done.2), kind=kOutput, calls=%fused_computation | convolution fusion | flops 1209532416 | bytes 8060928 | tf_op jit(solution)/shard_map/dot_general | solution.py:143
  24.1 0.3 constant_dynamic-slice_fusion.1
  24.4 0.1 copy.19
  24.5 1.9 %collective-permute-start = (bf16[8,4,96,256]{3,2,0,1:T(8,128)(2,1)S(1)}, bf16[8,4,96,256]{3,2,0,1:T(8,128)(2,1)S(1)}, u32[]{:S(2)}, u32[]{:S(2)}) collective-permute-start(bf16[8,4,96,256]{3,2,0,1:T(8,128)(2,1)S(1)} %bitcast.24), channel_id=1, source_target_pairs={{0,16},{16,0},{1,17},{17,1},{2,18},{18,2},{3,19},{19,3},{4,20},{20... | collective-permute-start | bytes 4718600 | tf_op jit(solution)/shard_map/ppermute | solution.py:15
  26.4 3.4 %collective-permute-done = bf16[8,4,96,256]{3,2,0,1:T(8,128)(2,1)S(1)} collective-permute-done((bf16[8,4,96,256]{3,2,0,1:T(8,128)(2,1)S(1)}, bf16[8,4,96,256]{3,2,0,1:T(8,128)(2,1)S(1)}, u32[]{:S(2)}, u32[]{:S(2)}) %collective-permute-start) | collective-permute-done | bytes 1572896 | tf_op jit(solution)/shard_map/ppermute | solution.py:15
  29.8 1.8 %fusion.1 = bf16[4,8,96,256]{3,2,1,0:T(8,128)(2,1)} fusion(bf16[8,4,96,256]{3,2,0,1:T(8,128)(2,1)S(1)} %collective-permute-done, bf16[8,4,1,96,256]{4,3,2,1,0:T(8,128)(2,1)S(1)} %get-tuple-element.6), kind=kLoop, calls=%fused_computation.3 | loop fusion | flops 3145728 | bytes 4718592 | tf_op jit(solution)/shard_map/transpose | solution.py:26
  31.6 10.0 %all-to-all-start = ((bf16[4,8,96,256]{3,2,1,0:T(8,128)(2,1)}), bf16[4,8,96,256]{3,2,1,0:T(8,128)(2,1)S(1)}, u32[]{:S(2)}, u32[]{:S(2)}) async-start(bf16[4,8,96,256]{3,2,1,0:T(8,128)(2,1)} %fusion.1), calls=%async_computation.1 | async-start | bytes 3145728 | tf_op jit(solution)/shard_map/all_to_all | solution.py:30
  41.6 0.0 copy-start
  41.6 0.0 copy-start.1
  41.6 1.2 convert_reduce_fusion.1
  42.7 1.2 %fusion.4 = f32[24]{0:T(128)S(1)} fusion(f32[24]{0:T(128)S(1)} %broadcast_multiply_fusion.1, bf16[384,6144]{1,0:T(8,128)(2,1)} %inputs_ref.1, s32[]{:T(128)S(6)} %select_n.21), kind=kLoop, calls=%fused_computation.11 | loop fusion | flops 589800 | bytes 295108 | tf_op jit(solution)/shard_map/reduce_sum | solution.py:161
  44.0 34.9 %all-to-all-done = bf16[4,8,96,256]{3,2,1,0:T(8,128)(2,1)S(1)} async-done(((bf16[4,8,96,256]{3,2,1,0:T(8,128)(2,1)}), bf16[4,8,96,256]{3,2,1,0:T(8,128)(2,1)S(1)}, u32[]{:S(2)}, u32[]{:S(2)}) %all-to-all-start) | async-done | bytes 1572896 | tf_op jit(solution)/shard_map/all_to_all | solution.py:30
  78.8 1.1 reduce_sum.39
  79.9 7.9 %all-to-all-start.1 = ((bf16[8,96,256]{2,1,0:T(8,128)(2,1)}), bf16[8,96,256]{2,1,0:T(8,128)(2,1)S(1)}, u32[]{:S(2)}, u32[]{:S(2)}) async-start(bf16[8,96,256]{2,1,0:T(8,128)(2,1)} %reduce_sum.39), calls=%async_computation.2 | async-start | bytes 786432 | tf_op jit(solution)/shard_map/all_to_all | solution.py:30
  87.8 1.1 fusion.2.normed_ref
  88.9 0.1 copy.13.inverse_ref
  89.0 0.0 reduce-scatter.2.cloned.1.call-done
  89.0 1.1 dynamic-slice_bitcast_fusion
  90.1 11.9 %collective-permute-start.1 = (bf16[24,6144]{1,0:T(8,128)(2,1)S(1)}, bf16[24,6144]{1,0:T(8,128)(2,1)S(1)}, u32[]{:S(2)}, u32[]{:S(2)}) collective-permute-start(bf16[24,6144]{1,0:T(8,128)(2,1)S(1)} %get-tuple-element.8), channel_id=1, source_target_pairs={{0,1},{1,0},{2,3},{3,2},{4,5},{5,4},{6,7},{7,6},{8,9},{9,8},{10,11... | collective-permute-start | bytes 884744 | tf_op jit(solution)/shard_map/ppermute | solution.py:15
  102.0 0.0 all-to-all-done.1
  102.0 0.1 convert_reduce_fusion
  102.0 0.6 broadcast_multiply_fusion
  102.7 11.1 %collective-permute-done.1.arrived_ref = bf16[24,6144]{1,0:T(8,128)(2,1)S(1)} collective-permute-done((bf16[24,6144]{1,0:T(8,128)(2,1)S(1)}, bf16[24,6144]{1,0:T(8,128)(2,1)S(1)}, u32[]{:S(2)}, u32[]{:S(2)}) %collective-permute-start.1) | collective-permute-done | bytes 294944 | tf_op jit(solution)/shard_map/ppermute | solution.py:15
  113.8 0.0 copy-done
  113.8 0.0 copy-done.1
  113.8 1.2 shard_map.70
  (2 shorter events, 0.0 us)
Async XLA Ops:
  7.2 81.8 %reduce-scatter.2.cloned.1.call-start = ((), (), s32[]{:S(2)}) async-start(), calls=%async_computation.3 | async-start | bytes 5308416 | tf_op jit(solution)/shard_map/reduce_scatter | solution.py:139
  12.1 7.9 %copy-start.2 = (bf16[384,256]{1,0:T(8,128)(2,1)S(1)}, bf16[384,256]{1,0:T(8,128)(2,1)}, u32[]{:S(2)}) copy-start(bf16[384,256]{1,0:T(8,128)(2,1)} %grads_hbm.1) | copy-start | bytes 589828
  24.5 5.3 %collective-permute-start = (bf16[8,4,96,256]{3,2,0,1:T(8,128)(2,1)S(1)}, bf16[8,4,96,256]{3,2,0,1:T(8,128)(2,1)S(1)}, u32[]{:S(2)}, u32[]{:S(2)}) collective-permute-start(bf16[8,4,96,256]{3,2,0,1:T(8,128)(2,1)S(1)} %bitcast.24), channel_id=1, source_target_pairs={{0,16},{16,0},{1,17},{17,1},{2,18},{18,2},{3,19},{19,3},{4,20},{20... | collective-permute-start | bytes 4718600 | tf_op jit(solution)/shard_map/ppermute | solution.py:15
  31.6 47.2 %all-to-all-start = ((bf16[4,8,96,256]{3,2,1,0:T(8,128)(2,1)}), bf16[4,8,96,256]{3,2,1,0:T(8,128)(2,1)S(1)}, u32[]{:S(2)}, u32[]{:S(2)}) async-start(bf16[4,8,96,256]{3,2,1,0:T(8,128)(2,1)} %fusion.1), calls=%async_computation.1 | async-start | bytes 3145728 | tf_op jit(solution)/shard_map/all_to_all | solution.py:30
  41.6 72.2 %copy-start = (bf16[24,6144]{1,0:T(8,128)(2,1)S(1)}, bf16[24,6144]{1,0:T(8,128)(2,1)}, u32[]{:S(2)}) copy-start(bf16[24,6144]{1,0:T(8,128)(2,1)} %skip_ref.1) | copy-start | bytes 884740
  41.6 72.2 %copy-start.1 = (f32[6144]{0:T(1024)S(1)}, f32[6144]{0:T(1024)}, u32[]{:S(2)}) copy-start(f32[6144]{0:T(1024)} %param.6) | copy-start | bytes 73732
  79.9 22.0 %all-to-all-start.1 = ((bf16[8,96,256]{2,1,0:T(8,128)(2,1)}), bf16[8,96,256]{2,1,0:T(8,128)(2,1)S(1)}, u32[]{:S(2)}, u32[]{:S(2)}) async-start(bf16[8,96,256]{2,1,0:T(8,128)(2,1)} %reduce_sum.39), calls=%async_computation.2 | async-start | bytes 786432 | tf_op jit(solution)/shard_map/all_to_all | solution.py:30
  90.1 23.7 %collective-permute-start.1 = (bf16[24,6144]{1,0:T(8,128)(2,1)S(1)}, bf16[24,6144]{1,0:T(8,128)(2,1)S(1)}, u32[]{:S(2)}, u32[]{:S(2)}) collective-permute-start(bf16[24,6144]{1,0:T(8,128)(2,1)S(1)} %get-tuple-element.8), channel_id=1, source_target_pairs={{0,1},{1,0},{2,3},{3,2},{4,5},{5,4},{6,7},{7,6},{8,9},{9,8},{10,11... | collective-permute-start | bytes 884744 | tf_op jit(solution)/shard_map/ppermute | solution.py:15
Sparse Core Ops, SparseCore 0:
  12.2 74.0 reduce-scatter.1

commit v11 on v9

--- a/solution.py
+++ b/solution.py
@@ -17,13 +17,12 @@
 
 def core_sum(term):
     rows, columns = term.shape[0] // lax.axis_size(DP), term.shape[1]
-    sizes = [lax.axis_size(axis) for axis in DP]
-    blocks = term.astype(jnp.bfloat16).reshape(*sizes, rows, columns)
+    blocks = term.astype(jnp.bfloat16).reshape(-1, lax.axis_size("core"), rows, columns)
     me = lax.axis_index("core")
-    own = lax.dynamic_index_in_dim(blocks, me, 2, False)
-    other = lax.dynamic_index_in_dim(blocks, 1 - me, 2, False)
+    own = lax.dynamic_index_in_dim(blocks, me, 1, False)
+    other = lax.dynamic_index_in_dim(blocks, 1 - me, 1, False)
     pair = own.astype(jnp.float32) + shifted(other, "core", 1).astype(jnp.float32)
-    return pair.astype(jnp.bfloat16).swapaxes(0, 1)
+    return pair.astype(jnp.bfloat16)
 
 
 def exchange(total, axis):
@@ -125,9 +124,7 @@
             scaled, query_grad, (((0,), (0,)), ((), ())), preferred_element_type=jnp.float32
         )
     )
-    column = exchange(pair, "z_lo").astype(jnp.bfloat16)
-    across, _ = lax.optimization_barrier((across, column))
-    weight_grad = exchange(column, "y") / lax.axis_size(DP)
+    weight_grad = exchange(pair, ("y", "z_lo")) / lax.axis_size(DP)
 
     halves = across.reshape(2, own_rows, features)
     me = lax.axis_index("z_hi")

time: 118 us -> 118 us (level)
  the two profiles are of different devices: /device:TPU:24 before, /device:TPU:128 now
where the time goes in v11:
time: 118 us; the launch traced here: 117 us
  waiting for transfers between devices  53.8 us (46%)
  starting transfers between devices  25.1 us (21%)
  between operations  14.2 us (12%)
  other arithmetic  12.1 us (10%)
  Pallas kernels  5.99 us (5%)
  local copies, waits for them, and re-layouts  3.21 us (3%)
  matrix products  2.8 us (2%)
    reduce_scatter x1, waiting for transfers between devices, per_device(): across = lax.psum_scatter(term, 'x', scatter_dimension=0, tiled=True)  38.2 us
    ppermute x2, waiting for transfers between devices, shifted(): lax.ppermute(part, axis, [(i, (i + step) % size) for i in range(size)])  15.6 us
    all_to_all x1, starting transfers between devices, exchange(): lax.all_to_all(total, axis, 0, 0, tiled=True).astype(jnp.float32)  15.3 us
    ppermute x2, starting transfers between devices, shifted(): lax.ppermute(part, axis, [(i, (i + step) % size) for i in range(size)])  9.75 us
    pallas_call x1, Pallas kernels, product(): pl.pallas_call(product_kernel, in_specs=[pl.BlockSpec(memory_space=pl.ANY...  4.81 us
    reduce_sum x1, other arithmetic, per_device(): jnp.mean(center * center, axis=1, keepdims=True) + 1e-06  3.71 us
    convert_element_type x1, other arithmetic, core_sum(): return pair.astype(jnp.bfloat16)  3.22 us
    reduce_sum x1, other arithmetic, per_device(): mean = jnp.mean(values, axis=1, keepdims=True)  3.19 us
  transfers between devices with their start and end apart: 4, of which 3 were waited for; matrix products, arithmetic and copies ran while one was open for 14% of the time, Pallas kernels for 0%

profile of v11, /device:TPU:128, one launch (start us, length us, event | category | flops | bytes accessed | tf_op | source)
XLA Modules:
  0.0 117.2 jit_solution(2122587012717304330)
XLA Ops:
  7.2 0.0 reduce-scatter.2.cloned.1.call-start
  7.2 4.8 %shard_map.68 = bf16[384,6144]{1,0:T(8,128)(2,1)} custom-call(bf16[384,256]{1,0:T(8,128)(2,1)} %grads_hbm.1, bf16[6144,256]{1,0:T(8,128)(2,1)} %weights_hbm.1), custom_call_target="tpu_custom_call" | custom-call | flops 1207959552 | bytes 8060928 | tf_op jit(solution)/shard_map/pallas_call | solution.py:68
  12.0 0.0 slice-start
  12.0 0.0 reduce-scatter.2.cloned.1.call-update
  12.1 0.0 copy-start.1
  12.1 0.0 slice-start.1
  12.1 0.0 copy-start.3
  12.1 3.2 %convert_reduce_fusion = f32[384]{0:T(512)S(1)} fusion(bf16[384,6144]{1,0:T(8,128)(2,1)} %param.5), kind=kLoop, calls=%fused_computation.1 | loop fusion | flops 4718208 | bytes 4720128 | tf_op jit(solution)/shard_map/reduce_sum | solution.py:118
  15.3 3.7 %fusion.2 = f32[384]{0:T(512)S(1)} fusion(bf16[384,6144]{1,0:T(8,128)(2,1)} %param.5, f32[384]{0:T(512)S(1)} %broadcast_multiply_fusion.1), kind=kLoop, calls=%fused_computation.4 | loop fusion | flops 9436800 | bytes 4721664 | tf_op jit(solution)/shard_map/reduce_sum | solution.py:120
  19.0 0.0 slice-done
  19.0 0.0 copy-done.1
  19.0 0.0 slice-done.1
  19.1 2.8 %convolution_convert_fusion = bf16[6144,256]{1,0:T(8,128)(2,1)S(1)} fusion(bf16[384,256]{1,0:T(8,128)(2,1)S(1)} %copy-done.3, bf16[384,6144]{1,0:T(8,128)(2,1)S(1)} %bitcast.17, f32[6144]{0:T(1024)S(1)} %copy-done.1, f32[384]{0:T(512)S(1)} %add_rsqrt_fusion, f32[384]{0:T(512)S(1)} %broadcast_multiply_fusion.1), kind=kOutput, calls=%fused_computation.7 | convolution fusion | flops 1221328896 | bytes 8088576 | tf_op jit(solution)/shard_map/dot_general | solution.py:123
  21.9 1.6 %copy-done.2 = bf16[6144,256]{1,0:T(8,128)(2,1)} copy-done((bf16[6144,256]{1,0:T(8,128)(2,1)}, bf16[6144,256]{1,0:T(8,128)(2,1)S(1)}, u32[]{:S(2)}) %copy-start.2) | copy-done | bytes 3145752
  23.5 0.1 dynamic-slice_bitcast_fusion
  23.7 1.9 %collective-permute-start.1 = (bf16[32,96,256]{2,1,0:T(8,128)(2,1)S(1)}, bf16[32,96,256]{2,1,0:T(8,128)(2,1)S(1)}, u32[]{:S(2)}, u32[]{:S(2)}) collective-permute-start(bf16[32,96,256]{2,1,0:T(8,128)(2,1)S(1)} %dynamic-slice_bitcast_fusion), channel_id=1, source_target_pairs={{0,16},{16,0},{1,17},{17,1},{2,18},{18,2},{3,19},{19,3},{4,20},{20... | collective-permute-start | bytes 4718600 | tf_op jit(solution)/shard_map/ppermute | solution.py:15
  25.6 3.4 %collective-permute-done.1 = bf16[32,96,256]{2,1,0:T(8,128)(2,1)S(1)} collective-permute-done((bf16[32,96,256]{2,1,0:T(8,128)(2,1)S(1)}, bf16[32,96,256]{2,1,0:T(8,128)(2,1)S(1)}, u32[]{:S(2)}, u32[]{:S(2)}) %collective-permute-start.1) | collective-permute-done | bytes 1572896 | tf_op jit(solution)/shard_map/ppermute | solution.py:15
  29.0 3.2 %fusion.9 = bf16[32,96,256]{2,1,0:T(8,128)(2,1)} fusion(bf16[32,96,256]{2,1,0:T(8,128)(2,1)S(1)} %collective-permute-done.1, bf16[32,2,96,256]{3,2,1,0:T(8,128)(2,1)} %bitcast.19, s32[]{:T(128)S(6)} %select_n.22), kind=kLoop, calls=%fused_computation.12 | loop fusion | flops 3145728 | bytes 4718596 | tf_op jit(solution)/shard_map/convert_element_type | solution.py:25
  32.2 15.3 %all-to-all-start = ((bf16[32,96,256]{2,1,0:T(8,128)(2,1)}), bf16[32,96,256]{2,1,0:T(8,128)(2,1)S(1)}, u32[]{:S(2)}, u32[]{:S(2)}) async-start(bf16[32,96,256]{2,1,0:T(8,128)(2,1)} %fusion.9), calls=%async_computation.1 | async-start | bytes 3145728 | tf_op jit(solution)/shard_map/all_to_all | solution.py:29
  47.5 0.1 dynamic-slice.7
  47.6 0.1 dynamic-slice.6
  47.7 0.1 dynamic-slice_bitcast_fusion.3
  47.8 0.1 copy.7.inverse_ref
  47.9 1.1 subtract_multiply_fusion.normed_ref
  49.0 38.2 %reduce-scatter.2.cloned.1.call-done = bf16[48,6144]{1,0:T(8,128)(2,1)} async-done(((bf16[384,6144]{1,0:T(8,128)(2,1)}), bf16[48,6144]{1,0:T(8,128)(2,1)}) %reduce-scatter.2.cloned.1.call-update) | async-done | bytes 589840 | tf_op jit(solution)/shard_map/reduce_scatter | solution.py:115
  87.2 1.1 dynamic-slice_bitcast_fusion.1
  88.2 7.8 %collective-permute-start = (bf16[24,6144]{1,0:T(8,128)(2,1)S(1)}, bf16[24,6144]{1,0:T(8,128)(2,1)S(1)}, u32[]{:S(2)}, u32[]{:S(2)}) collective-permute-start(bf16[24,6144]{1,0:T(8,128)(2,1)S(1)} %get-tuple-element.2), channel_id=1, source_target_pairs={{0,1},{1,0},{2,3},{3,2},{4,5},{5,4},{6,7},{7,6},{8,9},{9,8},{10,11... | collective-permute-start | bytes 884744 | tf_op jit(solution)/shard_map/ppermute | solution.py:15
  96.1 0.0 all-to-all-done
  96.1 0.2 convert_reduce_fusion.1
  96.3 0.6 broadcast_multiply_fusion
  97.0 12.2 %collective-permute-done.arrived_ref = bf16[24,6144]{1,0:T(8,128)(2,1)S(1)} collective-permute-done((bf16[24,6144]{1,0:T(8,128)(2,1)S(1)}, bf16[24,6144]{1,0:T(8,128)(2,1)S(1)}, u32[]{:S(2)}, u32[]{:S(2)}) %collective-permute-start) | collective-permute-done | bytes 294944 | tf_op jit(solution)/shard_map/ppermute | solution.py:15
  109.2 1.2 %shard_map.69 = bf16[24,6144]{1,0:T(8,128)(2,1)} custom-call(bf16[24,6144]{1,0:T(8,128)(2,1)S(1)} %get-tuple-element.3.own_ref, bf16[24,6144]{1,0:T(8,128)(2,1)S(1)} %collective-permute-done.arrived_ref, f32[24,6144]{1,0:T(8,128)S(1)} %subtract_multiply_fusion.normed_ref, f32[24,1]{1,0:T(8,128)S(1)} %copy.7.inverse_ref, bf16[24,6144]{1,0:T(8,128)(2,1)S(1)} %copy-done, ...), custom_call_target="tpu_custom_call" | custom-call | tf_op jit(solution)/shard_map/pallas_call | solution.py:103
  (7 shorter events, 0.0 us)
Async XLA Ops:
  7.2 80.0 %reduce-scatter.2.cloned.1.call-start = ((), (), s32[]{:S(2)}) async-start(), calls=%async_computation.2 | async-start | bytes 5308416 | tf_op jit(solution)/shard_map/reduce_scatter | solution.py:115
  12.0 7.0 %slice-start = ((s8[4718592]{0:T(1024)(128)(4,1)}), s8[524288]{0:T(1024)(128)(4,1)S(1)}, s32[]{:S(2)}) async-start(s8[4718592]{0:T(1024)(128)(4,1)} %bitcast.16), calls=%async_computation.3 | async-start | bytes 1048576
  12.1 7.0 %copy-start.1 = (f32[6144]{0:T(1024)S(1)}, f32[6144]{0:T(1024)}, u32[]{:S(2)}) copy-start(f32[6144]{0:T(1024)} %param.6) | copy-start | bytes 73732
  12.1 7.0 %slice-start.1 = ((s8[4718592]{0:T(1024)(128)(4,1)}), s8[4194304]{0:T(1024)(128)(4,1)S(1)}, s32[]{:S(2)}) async-start(s8[4718592]{0:T(1024)(128)(4,1)} %bitcast.16), calls=%async_computation.4 | async-start | bytes 8388608
  12.1 7.0 %copy-start.3 = (bf16[384,256]{1,0:T(8,128)(2,1)S(1)}, bf16[384,256]{1,0:T(8,128)(2,1)}, u32[]{:S(2)}) copy-start(bf16[384,256]{1,0:T(8,128)(2,1)} %grads_hbm.1) | copy-start | bytes 589828
  21.9 1.7 %copy-start.2 = (bf16[6144,256]{1,0:T(8,128)(2,1)}, bf16[6144,256]{1,0:T(8,128)(2,1)S(1)}, u32[]{:S(2)}) copy-start(bf16[6144,256]{1,0:T(8,128)(2,1)S(1)} %convolution_convert_fusion) | copy-start | bytes 9437188
  23.7 5.3 %collective-permute-start.1 = (bf16[32,96,256]{2,1,0:T(8,128)(2,1)S(1)}, bf16[32,96,256]{2,1,0:T(8,128)(2,1)S(1)}, u32[]{:S(2)}, u32[]{:S(2)}) collective-permute-start(bf16[32,96,256]{2,1,0:T(8,128)(2,1)S(1)} %dynamic-slice_bitcast_fusion), channel_id=1, source_target_pairs={{0,16},{16,0},{1,17},{17,1},{2,18},{18,2},{3,19},{19,3},{4,20},{20... | collective-permute-start | bytes 4718600 | tf_op jit(solution)/shard_map/ppermute | solution.py:15
  32.2 77.0 %copy-start = (bf16[24,6144]{1,0:T(8,128)(2,1)S(1)}, bf16[24,6144]{1,0:T(8,128)(2,1)}, u32[]{:S(2)}) copy-start(bf16[24,6144]{1,0:T(8,128)(2,1)} %skip_ref.1) | copy-start | bytes 884740
  32.2 63.9 %all-to-all-start = ((bf16[32,96,256]{2,1,0:T(8,128)(2,1)}), bf16[32,96,256]{2,1,0:T(8,128)(2,1)S(1)}, u32[]{:S(2)}, u32[]{:S(2)}) async-start(bf16[32,96,256]{2,1,0:T(8,128)(2,1)} %fusion.9), calls=%async_computation.1 | async-start | bytes 3145728 | tf_op jit(solution)/shard_map/all_to_all | solution.py:29
  88.2 20.9 %collective-permute-start = (bf16[24,6144]{1,0:T(8,128)(2,1)S(1)}, bf16[24,6144]{1,0:T(8,128)(2,1)S(1)}, u32[]{:S(2)}, u32[]{:S(2)}) collective-permute-start(bf16[24,6144]{1,0:T(8,128)(2,1)S(1)} %get-tuple-element.2), channel_id=1, source_target_pairs={{0,1},{1,0},{2,3},{3,2},{4,5},{5,4},{6,7},{7,6},{8,9},{9,8},{10,11... | collective-permute-start | bytes 884744 | tf_op jit(solution)/shard_map/ppermute | solution.py:15
Sparse Core Ops, SparseCore 0:
  12.2 74.9 reduce-scatter.1

commit v12 on v11

--- a/solution.py
+++ b/solution.py
@@ -29,7 +29,7 @@
     return jnp.sum(lax.all_to_all(total, axis, 0, 0, tiled=True).astype(jnp.float32), axis=0)
 
 
-PIECES = 4
+PIECES = 3
 
 
 def product_kernel(grads_hbm, weights_hbm, out_hbm, grads, weights, out, took, loaded, stored):

time: 118 us -> 117 us (level)
  no operation moved by 1% of the time
where the time goes in v12:
time: 117 us
  waiting for transfers between devices  53.8 us (46%)
  starting transfers between devices  25.1 us (21%)
  between operations  14.2 us (12%)
  other arithmetic  12.1 us (10%)
  Pallas kernels  5.82 us (5%)
  local copies, waits for them, and re-layouts  3.21 us (3%)
  matrix products  2.8 us (2%)
    reduce_scatter x1, waiting for transfers between devices, per_device(): across = lax.psum_scatter(term, 'x', scatter_dimension=0, tiled=True)  38.2 us
    ppermute x2, waiting for transfers between devices, shifted(): lax.ppermute(part, axis, [(i, (i + step) % size) for i in range(size)])  15.6 us
    all_to_all x1, starting transfers between devices, exchange(): lax.all_to_all(total, axis, 0, 0, tiled=True).astype(jnp.float32)  15.3 us
    ppermute x2, starting transfers between devices, shifted(): lax.ppermute(part, axis, [(i, (i + step) % size) for i in range(size)])  9.75 us
    pallas_call x1, Pallas kernels, product(): pl.pallas_call(product_kernel, in_specs=[pl.BlockSpec(memory_space=pl.ANY...  4.64 us
    reduce_sum x1, other arithmetic, per_device(): jnp.mean(center * center, axis=1, keepdims=True) + 1e-06  3.71 us
    convert_element_type x1, other arithmetic, core_sum(): return pair.astype(jnp.bfloat16)  3.22 us
    reduce_sum x1, other arithmetic, per_device(): mean = jnp.mean(values, axis=1, keepdims=True)  3.19 us
  transfers between devices with their start and end apart: 4, of which 3 were waited for; matrix products, arithmetic and copies ran while one was open for 14% of the time, Pallas kernels for 0%

profile of v12, /device:TPU:128, one launch (start us, length us, event | category | flops | bytes accessed | tf_op | source)
XLA Modules:
  0.0 117.0 jit_solution(16698720624228696994)
XLA Ops:
  7.2 0.0 reduce-scatter.2.cloned.1.call-start
  7.2 4.6 %shard_map.68 = bf16[384,6144]{1,0:T(8,128)(2,1)} custom-call(bf16[384,256]{1,0:T(8,128)(2,1)} %grads_hbm.1, bf16[6144,256]{1,0:T(8,128)(2,1)} %weights_hbm.1), custom_call_target="tpu_custom_call" | custom-call | flops 1207959552 | bytes 8060928 | tf_op jit(solution)/shard_map/pallas_call | solution.py:68
  11.9 0.0 slice-start
  11.9 0.0 reduce-scatter.2.cloned.1.call-update
  11.9 0.0 copy-start.1
  11.9 0.0 slice-start.1
  11.9 0.0 copy-start.3
  11.9 3.2 %convert_reduce_fusion = f32[384]{0:T(512)S(1)} fusion(bf16[384,6144]{1,0:T(8,128)(2,1)} %param.5), kind=kLoop, calls=%fused_computation.1 | loop fusion | flops 4718208 | bytes 4720128 | tf_op jit(solution)/shard_map/reduce_sum | solution.py:118
  15.1 3.7 %fusion.2 = f32[384]{0:T(512)S(1)} fusion(bf16[384,6144]{1,0:T(8,128)(2,1)} %param.5, f32[384]{0:T(512)S(1)} %broadcast_multiply_fusion.1), kind=kLoop, calls=%fused_computation.4 | loop fusion | flops 9436800 | bytes 4721664 | tf_op jit(solution)/shard_map/reduce_sum | solution.py:120
  18.9 0.0 slice-done
  18.9 2.8 %convolution_convert_fusion = bf16[6144,256]{1,0:T(8,128)(2,1)S(1)} fusion(bf16[384,256]{1,0:T(8,128)(2,1)S(1)} %copy-done.3, bf16[384,6144]{1,0:T(8,128)(2,1)S(1)} %bitcast.17, f32[6144]{0:T(1024)S(1)} %copy-done.1, f32[384]{0:T(512)S(1)} %add_rsqrt_fusion, f32[384]{0:T(512)S(1)} %broadcast_multiply_fusion.1), kind=kOutput, calls=%fused_computation.7 | convolution fusion | flops 1221328896 | bytes 8088576 | tf_op jit(solution)/shard_map/dot_general | solution.py:123
  21.7 0.0 copy-start.2
  21.7 1.6 %copy-done.2 = bf16[6144,256]{1,0:T(8,128)(2,1)} copy-done((bf16[6144,256]{1,0:T(8,128)(2,1)}, bf16[6144,256]{1,0:T(8,128)(2,1)S(1)}, u32[]{:S(2)}) %copy-start.2) | copy-done | bytes 3145752
  23.4 0.1 dynamic-slice_bitcast_fusion
  23.5 1.9 %collective-permute-start.1 = (bf16[32,96,256]{2,1,0:T(8,128)(2,1)S(1)}, bf16[32,96,256]{2,1,0:T(8,128)(2,1)S(1)}, u32[]{:S(2)}, u32[]{:S(2)}) collective-permute-start(bf16[32,96,256]{2,1,0:T(8,128)(2,1)S(1)} %dynamic-slice_bitcast_fusion), channel_id=1, source_target_pairs={{0,16},{16,0},{1,17},{17,1},{2,18},{18,2},{3,19},{19,3},{4,20},{20... | collective-permute-start | bytes 4718600 | tf_op jit(solution)/shard_map/ppermute | solution.py:15
  25.4 3.4 %collective-permute-done.1 = bf16[32,96,256]{2,1,0:T(8,128)(2,1)S(1)} collective-permute-done((bf16[32,96,256]{2,1,0:T(8,128)(2,1)S(1)}, bf16[32,96,256]{2,1,0:T(8,128)(2,1)S(1)}, u32[]{:S(2)}, u32[]{:S(2)}) %collective-permute-start.1) | collective-permute-done | bytes 1572896 | tf_op jit(solution)/shard_map/ppermute | solution.py:15
  28.8 3.2 %fusion.9 = bf16[32,96,256]{2,1,0:T(8,128)(2,1)} fusion(bf16[32,96,256]{2,1,0:T(8,128)(2,1)S(1)} %collective-permute-done.1, bf16[32,2,96,256]{3,2,1,0:T(8,128)(2,1)} %bitcast.19, s32[]{:T(128)S(6)} %select_n.22), kind=kLoop, calls=%fused_computation.12 | loop fusion | flops 3145728 | bytes 4718596 | tf_op jit(solution)/shard_map/convert_element_type | solution.py:25
  32.0 15.3 %all-to-all-start = ((bf16[32,96,256]{2,1,0:T(8,128)(2,1)}), bf16[32,96,256]{2,1,0:T(8,128)(2,1)S(1)}, u32[]{:S(2)}, u32[]{:S(2)}) async-start(bf16[32,96,256]{2,1,0:T(8,128)(2,1)} %fusion.9), calls=%async_computation.1 | async-start | bytes 3145728 | tf_op jit(solution)/shard_map/all_to_all | solution.py:29
  47.4 0.1 dynamic-slice.7
  47.4 0.1 dynamic-slice.6
  47.5 0.1 dynamic-slice_bitcast_fusion.3
  47.6 0.1 copy.7.inverse_ref
  47.7 1.1 subtract_multiply_fusion.normed_ref
  48.8 38.2 %reduce-scatter.2.cloned.1.call-done = bf16[48,6144]{1,0:T(8,128)(2,1)} async-done(((bf16[384,6144]{1,0:T(8,128)(2,1)}), bf16[48,6144]{1,0:T(8,128)(2,1)}) %reduce-scatter.2.cloned.1.call-update) | async-done | bytes 589840 | tf_op jit(solution)/shard_map/reduce_scatter | solution.py:115
  87.0 1.1 dynamic-slice_bitcast_fusion.1
  88.1 7.8 %collective-permute-start = (bf16[24,6144]{1,0:T(8,128)(2,1)S(1)}, bf16[24,6144]{1,0:T(8,128)(2,1)S(1)}, u32[]{:S(2)}, u32[]{:S(2)}) collective-permute-start(bf16[24,6144]{1,0:T(8,128)(2,1)S(1)} %get-tuple-element.2), channel_id=1, source_target_pairs={{0,1},{1,0},{2,3},{3,2},{4,5},{5,4},{6,7},{7,6},{8,9},{9,8},{10,11... | collective-permute-start | bytes 884744 | tf_op jit(solution)/shard_map/ppermute | solution.py:15
  95.9 0.0 all-to-all-done
  95.9 0.2 convert_reduce_fusion.1
  96.1 0.6 broadcast_multiply_fusion
  96.8 12.2 %collective-permute-done.arrived_ref = bf16[24,6144]{1,0:T(8,128)(2,1)S(1)} collective-permute-done((bf16[24,6144]{1,0:T(8,128)(2,1)S(1)}, bf16[24,6144]{1,0:T(8,128)(2,1)S(1)}, u32[]{:S(2)}, u32[]{:S(2)}) %collective-permute-start) | collective-permute-done | bytes 294944 | tf_op jit(solution)/shard_map/ppermute | solution.py:15
  109.0 0.0 copy-done
  109.0 1.2 %shard_map.69 = bf16[24,6144]{1,0:T(8,128)(2,1)} custom-call(bf16[24,6144]{1,0:T(8,128)(2,1)S(1)} %get-tuple-element.3.own_ref, bf16[24,6144]{1,0:T(8,128)(2,1)S(1)} %collective-permute-done.arrived_ref, f32[24,6144]{1,0:T(8,128)S(1)} %subtract_multiply_fusion.normed_ref, f32[24,1]{1,0:T(8,128)S(1)} %copy.7.inverse_ref, bf16[24,6144]{1,0:T(8,128)(2,1)S(1)} %copy-done, ...), custom_call_target="tpu_custom_call" | custom-call | tf_op jit(solution)/shard_map/pallas_call | solution.py:103
  (7 shorter events, 0.0 us)
Async XLA Ops:
  7.2 79.8 %reduce-scatter.2.cloned.1.call-start = ((), (), s32[]{:S(2)}) async-start(), calls=%async_computation.2 | async-start | bytes 5308416 | tf_op jit(solution)/shard_map/reduce_scatter | solution.py:115
  11.9 7.0 %slice-start = ((s8[4718592]{0:T(1024)(128)(4,1)}), s8[524288]{0:T(1024)(128)(4,1)S(1)}, s32[]{:S(2)}) async-start(s8[4718592]{0:T(1024)(128)(4,1)} %bitcast.16), calls=%async_computation.3 | async-start | bytes 1048576
  11.9 7.0 %copy-start.1 = (f32[6144]{0:T(1024)S(1)}, f32[6144]{0:T(1024)}, u32[]{:S(2)}) copy-start(f32[6144]{0:T(1024)} %param.6) | copy-start | bytes 73732
  11.9 7.0 %slice-start.1 = ((s8[4718592]{0:T(1024)(128)(4,1)}), s8[4194304]{0:T(1024)(128)(4,1)S(1)}, s32[]{:S(2)}) async-start(s8[4718592]{0:T(1024)(128)(4,1)} %bitcast.16), calls=%async_computation.4 | async-start | bytes 8388608
  11.9 7.0 %copy-start.3 = (bf16[384,256]{1,0:T(8,128)(2,1)S(1)}, bf16[384,256]{1,0:T(8,128)(2,1)}, u32[]{:S(2)}) copy-start(bf16[384,256]{1,0:T(8,128)(2,1)} %grads_hbm.1) | copy-start | bytes 589828
  21.7 1.7 %copy-start.2 = (bf16[6144,256]{1,0:T(8,128)(2,1)}, bf16[6144,256]{1,0:T(8,128)(2,1)S(1)}, u32[]{:S(2)}) copy-start(bf16[6144,256]{1,0:T(8,128)(2,1)S(1)} %convolution_convert_fusion) | copy-start | bytes 9437188
  23.5 5.3 %collective-permute-start.1 = (bf16[32,96,256]{2,1,0:T(8,128)(2,1)S(1)}, bf16[32,96,256]{2,1,0:T(8,128)(2,1)S(1)}, u32[]{:S(2)}, u32[]{:S(2)}) collective-permute-start(bf16[32,96,256]{2,1,0:T(8,128)(2,1)S(1)} %dynamic-slice_bitcast_fusion), channel_id=1, source_target_pairs={{0,16},{16,0},{1,17},{17,1},{2,18},{18,2},{3,19},{19,3},{4,20},{20... | collective-permute-start | bytes 4718600 | tf_op jit(solution)/shard_map/ppermute | solution.py:15
  32.0 77.0 %copy-start = (bf16[24,6144]{1,0:T(8,128)(2,1)S(1)}, bf16[24,6144]{1,0:T(8,128)(2,1)}, u32[]{:S(2)}) copy-start(bf16[24,6144]{1,0:T(8,128)(2,1)} %skip_ref.1) | copy-start | bytes 884740
  32.0 63.9 %all-to-all-start = ((bf16[32,96,256]{2,1,0:T(8,128)(2,1)}), bf16[32,96,256]{2,1,0:T(8,128)(2,1)S(1)}, u32[]{:S(2)}, u32[]{:S(2)}) async-start(bf16[32,96,256]{2,1,0:T(8,128)(2,1)} %fusion.9), calls=%async_computation.1 | async-start | bytes 3145728 | tf_op jit(solution)/shard_map/all_to_all | solution.py:29
  88.1 20.9 %collective-permute-start = (bf16[24,6144]{1,0:T(8,128)(2,1)S(1)}, bf16[24,6144]{1,0:T(8,128)(2,1)S(1)}, u32[]{:S(2)}, u32[]{:S(2)}) collective-permute-start(bf16[24,6144]{1,0:T(8,128)(2,1)S(1)} %get-tuple-element.2), channel_id=1, source_target_pairs={{0,1},{1,0},{2,3},{3,2},{4,5},{5,4},{6,7},{7,6},{8,9},{9,8},{10,11... | collective-permute-start | bytes 884744 | tf_op jit(solution)/shard_map/ppermute | solution.py:15
Sparse Core Ops, SparseCore 0:
  12.0 74.9 reduce-scatter.1
